TPU v7x, 32 devices: a whole 2x2x4 slice. The times are simulated.
32 devices in a mesh: sec: 4 (over x, core), row: 8 (over z, y).
Axes of the slice: x: 2, y: 2, z: 4, core: 2. Of those that a mesh axis runs over, the one named last changes fastest.
Arguments:
- template_scan: float32 [32, 1024, 256], P('sec', 'row'), may hold values from -6 to 6
- reference_scan: float32 [32, 1024, 256], P('sec', 'row'), may hold values from -6 to 6
- velocity: float32 [3, 32, 256, 1024], P(None, 'sec', 'row'), may hold values from -0.75 to 0.75
- stiffness: float32 [32, 256, 1024], P('sec', 'row'), may hold values from 0.02 to 0.2
Outputs:
- gradient: float32 [3, 32, 256, 1024], P(None, 'sec', 'row')
- objective: float32 [], replicated
All inputs are finite; a program needn't handle non-finite values.
Results may differ from a plain program's by a relative error of at most 0.00002.
Values sent between devices are 32-bit elements; how exact they have to be, the bound alone decides.
No kernel may reach another device: no remote copies, remote signals or barrier semaphores. Data moves between devices by JAX's collectives and lax.ppermute only.
A program may use at most 128 MiB of HBM per device.

v0:
```python
import jax
import jax.numpy as jnp
from jax import lax
from jax.experimental import pallas as pl
from jax.experimental.pallas import tpu as pltpu
from jax.sharding import PartitionSpec as P

STEPS = 4

DT = 0.25
KAPPA = 0.5
BETA = 0.5

LANES = 128
TILE = 8
GAP = 8
SENT = 4
WIDE = STEPS - 1
WEIGHT = DT * KAPPA
SELF = 1.0 - 6.0 * WEIGHT
assert WEIGHT == DT * 0.5

VMEM = pl.BlockSpec(memory_space=pltpu.VMEM)
SMEM = pl.BlockSpec(memory_space=pltpu.SMEM)
ANY = pl.BlockSpec(memory_space=pl.ANY)


def exchange(low_part, high_part, axis):
    count = lax.axis_size(axis)
    below = lax.ppermute(high_part, axis, [(i, i + 1) for i in range(count - 1)])
    above = lax.ppermute(low_part, axis, [(i + 1, i) for i in range(count - 1)])
    return below, above


def columns(tiles):
    lane = lax.broadcasted_iota(jnp.int32, tiles[0].shape, 1)
    zero = jnp.zeros_like(tiles[0])
    up = [pltpu.roll(t, LANES - 1, 1) for t in tiles]
    down = [pltpu.roll(t, 1, 1) for t in tiles]
    plus = [jnp.where(lane == LANES - 1, n, u) for u, n in zip(up, up[1:] + [zero])]
    minus = [jnp.where(lane == 0, p, d) for d, p in zip(down, [zero] + down[:-1])]
    return plus, minus


def edges(tiles_up, tiles_down):
    lane = lax.broadcasted_iota(jnp.int32, tiles_up[0].shape, 1)
    zero = jnp.zeros_like(tiles_up[0])
    up = [pltpu.roll(t, LANES - 1, 1) for t in tiles_up]
    down = [pltpu.roll(t, 1, 1) for t in tiles_down]
    plus = [jnp.where(lane == LANES - 1, n, u) for u, n in zip(up, up[1:] + [zero])]
    minus = [jnp.where(lane == 0, p, d) for d, p in zip(down, [zero] + down[:-1])]
    return plus, minus


def fill(out, own, below, above, before, after, width):
    blocks, sections, rows, _ = own.shape

    def plane(src, z_src, z_out):
        for i in range(blocks):
            out[i, z_out, pl.ds(GAP, rows), :] = src[i, z_src, :, :]

    def whole(z, _):
        plane(own, z, z + width)
        return 0

    def halo(z, _):
        plane(below, z, z)
        plane(above, z, z + width + sections)
        return 0

    def sides(z, _):
        for i in range(blocks):
            out[i, z, pl.ds(GAP - SENT, SENT), :] = before[i, z, :, :]
            out[i, z, pl.ds(GAP + rows, SENT), :] = after[i, z, :, :]
        return 0

    lax.fori_loop(0, sections, whole, 0)
    lax.fori_loop(0, width, halo, 0)
    lax.fori_loop(0, sections + 2 * width, sides, 0)


def groups(rows, reach):
    if reach == 0:
        return [GAP + g for g in range(0, rows, TILE)]
    return [GAP - SENT + g for g in range(0, rows + TILE, TILE)]


def masked(value, start, rows, flags):
    row = start + lax.broadcasted_iota(jnp.int32, value.shape, 0)
    if start < GAP:
        return jnp.where((row >= GAP) | (flags[2] > 0.5), value, 0.0)
    if start + TILE > GAP + rows:
        return jnp.where((row < GAP + rows) | (flags[3] > 0.5), value, 0.0)
    return value


def weights(flags, z, low, high):
    factor = jnp.where(z < low, flags[0], jnp.where(z >= high, flags[1], 1.0))
    return SELF * factor, WEIGHT * factor


def forward_kernel(flags, own, below, above, before, after, vel, moved_ref, kept_ref, *scratch):
    levels, sem = scratch[:STEPS], scratch[STEPS]
    blocks, sections, rows, _ = own.shape
    fill(levels[0], own, below, above, before, after, STEPS)
    copies = []
    for step in range(STEPS):
        src = levels[step]
        copies.append(
            pltpu.make_async_copy(
                src.at[:, pl.ds(STEPS - 1, sections + 2), :, :], kept_ref.at[step], sem.at[step]
            )
        )
        copies[-1].start()
        reach = STEPS - 1 - step

        def plane(z, _, src=src, step=step, reach=reach):
            keep, weight = weights(flags, z, STEPS, STEPS + sections)
            for r in groups(rows, reach):
                here = pl.ds(r, TILE)
                mids = [src[i, z, here, :] for i in range(blocks)]
                plus, minus = columns(mids)
                for i in range(blocks):
                    zp, zm = src[i, z + 1, here, :], src[i, z - 1, here, :]
                    xp, xm = src[i, z, pl.ds(r + 1, TILE), :], src[i, z, pl.ds(r - 1, TILE), :]
                    yp, ym = plus[i], minus[i]
                    total = (zp + zm) - vel[0, i, z - 1, here, :] * (zp - zm)
                    total = total + ((xp + xm) - vel[1, i, z - 1, here, :] * (xp - xm))
                    total = total + ((yp + ym) - vel[2, i, z - 1, here, :] * (yp - ym))
                    value = keep * mids[i] + weight * total
                    if step == STEPS - 1:
                        moved_ref[i, z - STEPS, pl.ds(r - GAP, TILE), :] = value
                    else:
                        levels[step + 1][i, z, here, :] = masked(value, r, rows, flags)
            return 0

        lax.fori_loop(STEPS - reach, STEPS + sections + reach, plane, 0)
    for copy in copies:
        copy.wait()


def adjoint_kernel(flags, own, below, above, before, after, vel, kept, reg, grad_ref, *levels):
    blocks, sections, rows, _ = own.shape
    fill(levels[0], own, below, above, before, after, WIDE)
    for step in range(WIDE):
        src, out = levels[step], levels[step + 1]
        reach = WIDE - 1 - step

        def plane(z, _, src=src, out=out, reach=reach):
            keep, weight = weights(flags, z, WIDE, WIDE + sections)
            for r in groups(rows, reach):
                here, up, down = pl.ds(r, TILE), pl.ds(r + 1, TILE), pl.ds(r - 1, TILE)
                mids = [src[i, z, here, :] for i in range(blocks)]
                prods = [mids[i] * vel[2, i, z, here, :] for i in range(blocks)]
                plus, minus = edges(
                    [m + p for m, p in zip(mids, prods)], [m - p for m, p in zip(mids, prods)]
                )
                for i in range(blocks):
                    zp, zm = src[i, z + 1, here, :], src[i, z - 1, here, :]
                    xp, xm = src[i, z, up, :], src[i, z, down, :]
                    total = plus[i] + minus[i]
                    total = total + (zp + zp * vel[0, i, z + 1, here, :])
                    total = total + (zm - zm * vel[0, i, z - 1, here, :])
                    total = total + (xp + xp * vel[1, i, z, up, :])
                    total = total + (xm - xm * vel[1, i, z, down, :])
                    value = keep * mids[i] + weight * total
                    if reach > 0:
                        value = masked(value, r, rows, flags)
                    out[i, z, here, :] = value
            return 0

        lax.fori_loop(WIDE - reach, WIDE + sections + reach, plane, 0)

    def slope(z, _):
        for r in groups(rows, 0):
            here, up, down = pl.ds(r, TILE), pl.ds(r + 1, TILE), pl.ds(r - 1, TILE)
            at = pl.ds(r - GAP, TILE)
            sums = [[None] * 3 for _ in range(blocks)]
            for k in range(STEPS):
                adj = [levels[STEPS - 1 - k][i, z + WIDE, here, :] for i in range(blocks)]
                plus, minus = columns([kept[k, i, z + 1, here, :] for i in range(blocks)])
                for i in range(blocks):
                    parts = (
                        adj[i] * (kept[k, i, z + 2, here, :] - kept[k, i, z, here, :]),
                        adj[i] * (kept[k, i, z + 1, up, :] - kept[k, i, z + 1, down, :]),
                        adj[i] * (plus[i] - minus[i]),
                    )
                    for a in range(3):
                        sums[i][a] = parts[a] if k == 0 else sums[i][a] + parts[a]
            for i in range(blocks):
                lanes = pl.ds(i * LANES, LANES)
                for a in range(3):
                    grad_ref[a, z, at, lanes] = reg[a, z, at, lanes] - (0.5 * DT) * sums[i][a]
        return 0

    lax.fori_loop(0, sections, slope, 0)


def regular_kernel(vel, vel_below, vel_above, vel_before, vel_after,
                   sti, sti_below, sti_above, sti_before, sti_after,
                   ext_ref, reg_ref, sum_ref, sti_ext):
    _, sections, rows, width = vel.shape
    blocks = width // LANES

    def lay(out, src, z_out, z_src):
        for i in range(blocks):
            out[i, z_out, pl.ds(GAP, rows), :] = src[z_src, :, pl.ds(i * LANES, LANES)]

    def lay_sides(out, z, low, high, count):
        for i in range(blocks):
            lanes = pl.ds(i * LANES, LANES)
            out[i, z, pl.ds(GAP - count, count), :] = low[:, lanes]
            out[i, z, pl.ds(GAP + rows, count), :] = high[:, lanes]

    for c in range(3):
        def mid(z, _, c=c):
            lay(ext_ref.at[c], vel.at[c], z + WIDE, z)
            return 0

        def far(z, _, c=c):
            lay(ext_ref.at[c], vel_below.at[c], z, z)
            lay(ext_ref.at[c], vel_above.at[c], z + WIDE + sections, z)
            return 0

        def side(z, _, c=c):
            lay_sides(ext_ref.at[c], z, vel_before.at[c, z], vel_after.at[c, z], SENT)
            return 0

        lax.fori_loop(0, sections, mid, 0)
        lax.fori_loop(0, WIDE, far, 0)
        lax.fori_loop(0, sections + 2 * WIDE, side, 0)

    lay(sti_ext, sti_below, 0, 0)
    lay(sti_ext, sti_above, sections + 1, 0)

    def mid_s(z, _):
        lay(sti_ext, sti, z + 1, z)
        lay_sides(sti_ext, z + 1, sti_before.at[z], sti_after.at[z], 1)
        return 0

    lax.fori_loop(0, sections, mid_s, 0)

    def plane(z, acc):
        for r in groups(rows, 0):
            here, up, down = pl.ds(r, TILE), pl.ds(r + 1, TILE), pl.ds(r - 1, TILE)
            at = pl.ds(r - GAP, TILE)
            s_mid = [sti_ext[i, z + 1, here, :] for i in range(blocks)]
            s_plus, s_minus = columns(s_mid)
            faces = []
            for i in range(blocks):
                s = s_mid[i]
                faces.append([
                    (s + sti_ext[i, z, here, :], s + sti_ext[i, z + 2, here, :]),
                    (s + sti_ext[i, z + 1, down, :], s + sti_ext[i, z + 1, up, :]),
                    (s + s_minus[i], s + s_plus[i]),
                ])
            for c in range(3):
                v_mid = [ext_ref[c, i, z + WIDE, here, :] for i in range(blocks)]
                v_plus, v_minus = columns(v_mid)
                for i in range(blocks):
                    v = v_mid[i]
                    pairs = (
                        (ext_ref[c, i, z + WIDE - 1, here, :], ext_ref[c, i, z + WIDE + 1, here, :]),
                        (ext_ref[c, i, z + WIDE, down, :], ext_ref[c, i, z + WIDE, up, :]),
                        (v_minus[i], v_plus[i]),
                    )
                    total = None
                    for (low, high), (f_low, f_high) in zip(pairs, faces[i]):
                        part = f_low * (v - low) + f_high * (v - high)
                        total = part if total is None else total + part
                    term = (0.5 * BETA) * total
                    reg_ref[c, z, at, pl.ds(i * LANES, LANES)] = term
                    acc = acc + v * term
        return acc

    acc = lax.fori_loop(0, sections, plane, jnp.zeros((TILE, LANES), jnp.float32))
    sum_ref[...] = acc


def to_rows(scan):
    count = lax.axis_size("row")
    sections, width, rows = scan.shape
    own = rows // count
    parts = jnp.swapaxes(scan, 1, 2).reshape(sections, count, own, width).transpose(1, 0, 2, 3)
    parts = lax.all_to_all(parts, "row", split_axis=0, concat_axis=0, tiled=True)
    if width == LANES:
        return parts
    whole = parts.transpose(1, 2, 0, 3).reshape(sections, own, count * width // LANES, LANES)
    return whole.transpose(2, 0, 1, 3)


def with_halos(field, width):
    rows = field.shape[2]
    below, above = exchange(field[:, :width], field[:, -width:], "sec")
    low, high = (
        jnp.concatenate([part[:, :, cut] for part in (below, field, above)], axis=1)
        for cut in (slice(0, SENT), slice(rows - SENT, rows))
    )
    before, after = exchange(low, high, "row")
    return below, above, before, after


def call(kernel, shapes, ins, scratch, megabytes, flops=0):
    return pl.pallas_call(
        kernel,
        out_shape=[jax.ShapeDtypeStruct(shape, jnp.float32) for shape, _ in shapes],
        in_specs=ins,
        out_specs=[spec for _, spec in shapes],
        scratch_shapes=scratch,
        compiler_params=pltpu.CompilerParams(vmem_limit_bytes=megabytes << 20),
        cost_estimate=pl.CostEstimate(flops=flops, bytes_accessed=16 << 20, transcendentals=0),
    )


def local(template_scan, reference_scan, velocity, stiffness):
    _, sections, rows, width = velocity.shape
    blocks = width // LANES
    tall = rows + 2 * GAP
    sec, row = lax.axis_index("sec"), lax.axis_index("row")
    flags = jnp.stack([
        sec > 0, sec < lax.axis_size("sec") - 1, row > 0, row < lax.axis_size("row") - 1
    ]).astype(jnp.float32)

    template = to_rows(template_scan)

    low = jnp.concatenate([velocity[:, :WIDE].reshape(3 * WIDE, rows, width), stiffness[:1]])
    high = jnp.concatenate([velocity[:, -WIDE:].reshape(3 * WIDE, rows, width), stiffness[-1:]])
    below, above = exchange(low, high, "sec")
    vel_below, vel_above = (
        part[:-1].reshape(3, WIDE, rows, width) for part in (below, above)
    )
    sides = []
    for cut in (slice(0, SENT), slice(rows - SENT, rows)):
        vel_cut = jnp.concatenate(
            [vel_below[:, :, cut], velocity[:, :, cut], vel_above[:, :, cut]], axis=1
        )
        sides.append(
            jnp.concatenate([vel_cut.reshape(-1, SENT, width), stiffness[:, cut]], axis=0)
        )
    before, after = exchange(sides[0], sides[1], "row")
    deep = sections + 2 * WIDE
    vel_before, vel_after = (
        part[: 3 * deep].reshape(3, deep, SENT, width) for part in (before, after)
    )
    sti_before = before[3 * deep :, SENT - 1 :]
    sti_after = after[3 * deep :, :1]

    def regular(*args):
        return call(
            regular_kernel,
            [
                ((3, blocks, deep, tall, LANES), VMEM),
                ((3, sections, rows, width), VMEM),
                ((TILE, LANES), VMEM),
            ],
            [VMEM] * 10,
            [pltpu.VMEM((blocks, sections + 2, tall, LANES), jnp.float32)],
            56,
            20 << 20,
        )(*args)

    extended, reg, reg_sums = regular(
        velocity, vel_below, vel_above, vel_before, vel_after,
        stiffness, below[-1:], above[-1:], sti_before, sti_after,
    )

    halos = with_halos(template, STEPS)
    field = (blocks, sections + 2 * STEPS, tall, LANES)
    moved, kept = call(
        forward_kernel,
        [
            ((blocks, sections, rows, LANES), VMEM),
            ((STEPS, blocks, sections + 2, tall, LANES), ANY),
        ],
        [SMEM] + [VMEM] * 6,
        [pltpu.VMEM(field, jnp.float32)] * STEPS + [pltpu.SemaphoreType.DMA((STEPS,))],
        56,
        20 << 20,
    )(flags, template, *halos, extended)

    fixed = to_rows(reference_scan)
    misfit = moved - fixed
    partial = 0.5 * jnp.sum(misfit * misfit) + 0.5 * jnp.sum(reg_sums)
    everyone = lax.axis_size("sec") * lax.axis_size("row")
    spread = lax.all_to_all(
        jnp.full((everyone, LANES), partial), ("sec", "row"), split_axis=0, concat_axis=0, tiled=True
    )
    voxels = sections * rows * width * everyone
    objective = jnp.sum(spread[:, 0]) / voxels

    halos = with_halos(misfit, WIDE)
    (gradient,) = call(
        adjoint_kernel,
        [((3, sections, rows, width), VMEM)],
        [SMEM] + [VMEM] * 8,
        [pltpu.VMEM((blocks, deep, tall, LANES), jnp.float32)] * STEPS,
        56,
        20 << 20,
    )(flags, misfit, *halos, extended, kept, reg)
    return (gradient, objective)


def solution(mesh):
    return jax.shard_map(
        local,
        mesh=mesh,
        in_specs=(
            P("sec", "row", None),
            P("sec", "row", None),
            P(None, "sec", "row", None),
            P("sec", "row", None),
        ),
        out_specs=(P(None, "sec", "row", None), P()),
        check_vma=False,
    )
```

profile of v0, /device:TPU:0, one launch (start us, length us, event | category | flops | bytes accessed | tf_op | source)
XLA Modules:
  0.0 190.8 jit_solution(16996438078425278098)
XLA Ops:
  0.6 2.5 %copy.14 = f32[8,128,256]{1,2,0:T(8,128)} copy(f32[8,128,256]{2,1,0:T(8,128)} %param.4) | data formatting | bytes 2097152 | tf_op args[0]
  3.2 2.5 %copy.23 = f32[8,8,32,128]{3,2,0,1:T(8,128)} copy(f32[8,8,32,128]{3,2,1,0:T(8,128)} %bitcast.32) | data formatting | bytes 2097152 | tf_op jit(solution)/shard_map/reshape | solution.py:284
  5.6 7.3 %all-to-all-start = ((f32[8,8,32,128]{3,2,1,0:T(8,128)}), f32[8,8,32,128]{3,2,1,0:T(8,128)}, u32[]{:S(2)}, u32[]{:S(2)}) async-start(f32[8,8,32,128]{3,2,1,0:T(8,128)} %bitcast.31), calls=%async_computation | async-start | bytes 2097152 | tf_op jit(solution)/shard_map/all_to_all | solution.py:285
  12.9 1.0 fusion.7
  14.2 1.1 pad_maximum_fusion
  15.3 2.5 %collective-permute-start.4 = (f32[10,32,1024]{2,1,0:T(8,128)}, f32[10,32,1024]{2,1,0:T(8,128)}, u32[]{:S(2)}, u32[]{:S(2)}) collective-permute-start(f32[10,32,1024]{2,1,0:T(8,128)} %pad_maximum_fusion), channel_id=1, source_target_pairs={{0,8},{8,16},{16,24},{1,9},{9,17},{17,25},{2,10},{10,18},{18,26},{... | collective-permute-start | bytes 3932168 | tf_op jit(solution)/shard_map/ppermute | solution.py:30
  17.9 1.2 pad_maximum_fusion.1
  19.0 1.3 collective-permute-start.5
  20.3 2.5 %copy.16 = f32[8,128,256]{1,2,0:T(8,128)} copy(f32[8,128,256]{2,1,0:T(8,128)} %param.5) | data formatting | bytes 2097152 | tf_op args[1]
  22.9 2.3 %copy.22 = f32[8,8,32,128]{3,2,0,1:T(8,128)} copy(f32[8,8,32,128]{3,2,1,0:T(8,128)} %bitcast.33) | data formatting | bytes 2097152 | tf_op jit(solution)/shard_map/reshape | solution.py:284
  25.2 1.8 fusion.6
  26.9 0.9 fusion
  27.9 1.4 slice.156
  29.3 1.8 slice.157
  31.2 7.6 %all-to-all-done.own = f32[8,8,32,128]{3,2,1,0:T(8,128)} async-done(((f32[8,8,32,128]{3,2,1,0:T(8,128)}), f32[8,8,32,128]{3,2,1,0:T(8,128)}, u32[]{:S(2)}, u32[]{:S(2)}) %all-to-all-start) | async-done | bytes 1048608 | tf_op jit(solution)/shard_map/all_to_all | solution.py:285
  38.8 3.6 %all-to-all-start.1 = ((f32[8,8,32,128]{3,2,1,0:T(8,128)}), f32[8,8,32,128]{3,2,1,0:T(8,128)S(1)}, u32[]{:S(2)}, u32[]{:S(2)}) async-start(f32[8,8,32,128]{3,2,1,0:T(8,128)} %bitcast.23), calls=%async_computation.1 | async-start | bytes 2097152 | tf_op jit(solution)/shard_map/all_to_all | solution.py:285
  42.4 1.3 fusion.9
  43.7 1.3 collective-permute-start.1
  46.2 1.3 collective-permute-start.7
  47.5 7.6 %collective-permute-start = (f32[8,4,32,128]{3,2,1,0:T(8,128)S(1)}, f32[8,4,32,128]{3,2,1,0:T(8,128)S(1)}, u32[]{:S(2)}, u32[]{:S(2)}) collective-permute-start(f32[8,4,32,128]{3,2,1,0:T(8,128)S(1)} %get-tuple-element.33), channel_id=1, source_target_pairs={{0,8},{8,16},{16,24},{1,9},{9,17},{17,25},{2,10},{10,18},{18,26},{... | collective-permute-start | bytes 1572872 | tf_op jit(solution)/shard_map/ppermute | solution.py:30
  55.0 1.1 pad_maximum_fusion.2
  56.2 5.2 %collective-permute-start.6 = (f32[50,4,1024]{2,1,0:T(4,128)}, f32[50,4,1024]{2,1,0:T(4,128)}, u32[]{:S(2)}, u32[]{:S(2)}) collective-permute-start(f32[50,4,1024]{2,1,0:T(4,128)} %pad_maximum_fusion.2), channel_id=1, source_target_pairs={{0,1},{1,2},{2,3},{3,4},{4,5},{5,6},{6,7},{8,9},{9,10},{10,11},{11... | collective-permute-start | bytes 2457608 | tf_op jit(solution)/shard_map/ppermute | solution.py:30
  61.3 1.1 fusion.8
  62.5 0.9 pad_maximum_fusion.6
  63.4 3.6 %collective-permute-start.2 = (f32[8,16,4,128]{3,2,1,0:T(4,128)}, f32[8,16,4,128]{3,2,1,0:T(4,128)S(1)}, u32[]{:S(2)}, u32[]{:S(2)}) collective-permute-start(f32[8,16,4,128]{3,2,1,0:T(4,128)} %pad_maximum_fusion.6), channel_id=1, source_target_pairs={{0,1},{1,2},{2,3},{3,4},{4,5},{5,6},{6,7},{8,9},{9,10},{10,11},{11... | collective-permute-start | bytes 786440 | tf_op jit(solution)/shard_map/ppermute | solution.py:30
  67.1 0.8 pad_maximum_fusion.7
  67.9 1.3 collective-permute-start.3
  69.2 0.6 add_convert_fusion.flags
  69.8 1.6 slice.164.sti_below
  71.3 1.6 slice.165.sti_above
  72.9 1.5 collective-permute-done.7
  74.4 1.5 slice.167.sti_after
  75.9 2.0 %slice.163 = f32[42,4,1024]{2,1,0:T(4,128)} slice(f32[50,4,1024]{2,1,0:T(4,128)} %collective-permute-done.7), slice={[0:42], [0:4], [0:1024]} | slice | bytes 1376256 | tf_op jit(solution)/shard_map/slice | solution.py:343
  77.9 22.7 %collective-permute-done.6 = f32[50,4,1024]{2,1,0:T(4,128)} collective-permute-done((f32[50,4,1024]{2,1,0:T(4,128)}, f32[50,4,1024]{2,1,0:T(4,128)}, u32[]{:S(2)}, u32[]{:S(2)}) %collective-permute-start.6) | collective-permute-done | bytes 819232 | tf_op jit(solution)/shard_map/ppermute | solution.py:30
  100.7 1.6 slice.166.sti_before
  102.2 2.0 %slice.160 = f32[42,4,1024]{2,1,0:T(4,128)} slice(f32[50,4,1024]{2,1,0:T(4,128)} %collective-permute-done.6), slice={[0:42], [0:4], [0:1024]} | slice | bytes 1376256 | tf_op jit(solution)/shard_map/slice | solution.py:343
  104.2 11.3 %shard_map.59 = (f32[3,8,14,48,128]{4,3,2,1,0:T(8,128)}, f32[3,8,32,1024]{3,2,1,0:T(8,128)}, f32[8,128]{1,0:T(8,128)}) custom-call(f32[3,8,32,1024]{3,2,1,0:T(8,128)} %vel.1, f32[3,3,32,1024]{3,2,1,0:T(8,128)} %bitcast.26, f32[3,3,32,1024]{3,2,1,0:T(8,128)} %bitcast.28, f32[3,14,4,1024]{3,2,1,0:T(4,128)} %bitcast.37, f32[3,14,4,1024]{3,2,1,0:T(4,128)} %bitcast.36, ...), custom_call_target="tpu_custom_call" | custom-call | flops 20971520 | bytes 16777216 | tf_op jit(solution)/shard_map/pallas_call | solution.py:349
  115.5 0.7 copy-done.11
  116.2 14.0 %shard_map.60 = (f32[8,8,32,128]{3,2,1,0:T(8,128)}, f32[4,8,10,48,128]{4,3,2,1,0:T(8,128)}) custom-call(f32[4]{0:T(128)} %add_convert_fusion.flags, f32[8,8,32,128]{3,2,1,0:T(8,128)} %all-to-all-done.own, f32[8,4,32,128]{3,2,1,0:T(8,128)} %copy-done.6, f32[8,4,32,128]{3,2,1,0:T(8,128)} %copy-done.5, f32[8,16,4,128]{3,2,1,0:T(4,128)} %copy-done.11, ...), custom_call_target="tpu_custom_call" | custom-call | flops 20971520 | bytes 16777216 | tf_op jit(solution)/shard_map/pallas_call | solution.py:369
  130.2 2.1 %multiply_reduce_fusion = (f32[]{:T(128)}, f32[8,8,32,128]{3,2,1,0:T(8,128)S(1)}) fusion(f32[8,8,32,128]{3,2,1,0:T(8,128)} %get-tuple-element.8, f32[8,8,32,128]{3,2,1,0:T(8,128)S(1)} %all-to-all-done.1), kind=kLoop, calls=%fused_computation.4 | loop fusion | flops 786431 | bytes 3145732 | tf_op jit(solution)/shard_map/reduce_sum | solution.py:383
  132.4 1.3 collective-permute-start.9
  133.7 3.8 %collective-permute-start.8 = (f32[8,3,32,128]{3,2,1,0:T(8,128)S(1)}, f32[8,3,32,128]{3,2,1,0:T(8,128)S(1)}, u32[]{:S(2)}, u32[]{:S(2)}) collective-permute-start(f32[8,3,32,128]{3,2,1,0:T(8,128)S(1)} %get-tuple-element.25), channel_id=1, source_target_pairs={{0,8},{8,16},{16,24},{1,9},{9,17},{17,25},{2,10},{10,18},{18,26},{... | collective-permute-start | bytes 1179656 | tf_op jit(solution)/shard_map/ppermute | solution.py:30
  137.6 1.2 collective-permute-done.8.below
  138.9 4.3 %collective-permute-start.10 = (f32[8,14,4,128]{3,2,1,0:T(4,128)S(1)}, f32[8,14,4,128]{3,2,1,0:T(4,128)S(1)}, u32[]{:S(2)}, u32[]{:S(2)}) collective-permute-start(f32[8,14,4,128]{3,2,1,0:T(4,128)S(1)} %pad_maximum_fusion.8), channel_id=1, source_target_pairs={{0,1},{1,2},{2,3},{3,4},{4,5},{5,6},{6,7},{8,9},{9,10},{10,11},{11... | collective-permute-start | bytes 688136 | tf_op jit(solution)/shard_map/ppermute | solution.py:30
  143.3 1.3 collective-permute-start.11
  146.5 21.9 %all_to_all.19 = f32[32,1,128]{2,1,0:T(1,128)S(1)} all-to-all(f32[32,1,128]{2,1,0:T(1,128)S(1)} %broadcast_in_dim.3), channel_id=1, replica_groups=mesh['sec'=4,'row'=8] {'sec','row'}, dimensions={0} | all-to-all | bytes 32768 | tf_op jit(solution)/shard_map/all_to_all | solution.py:385
  169.7 0.7 copy-done.12
  170.4 19.2 %shard_map.61 = f32[3,8,32,1024]{3,2,1,0:T(8,128)} custom-call(f32[4]{0:T(128)} %add_convert_fusion.flags, f32[8,8,32,128]{3,2,1,0:T(8,128)} %copy-done.1, f32[8,3,32,128]{3,2,1,0:T(8,128)} %copy-done.8, f32[8,3,32,128]{3,2,1,0:T(8,128)} %copy-done.7, f32[8,14,4,128]{3,2,1,0:T(4,128)} %copy-done.12, f32[8,14,4,128]{3,2,1,0:T(4,128)} %copy-done.13, ...), custom_call_target="tpu_custom_call" | custom-call | flops 20971520 | bytes 16777216 | tf_op jit(solution)/shard_map/pallas_call | solution.py:392
  (54 shorter events, 3.1 us)
Async XLA Ops:
  3.2 10.8 %copy-start = (f32[3,8,32,1024]{3,2,1,0:T(8,128)S(1)}, f32[3,8,32,1024]{3,2,1,0:T(8,128)}, u32[]{:S(2)}) copy-start(f32[3,8,32,1024]{3,2,1,0:T(8,128)} %vel.1) | copy-start | bytes 9437188
  5.6 33.2 %all-to-all-start = ((f32[8,8,32,128]{3,2,1,0:T(8,128)}), f32[8,8,32,128]{3,2,1,0:T(8,128)}, u32[]{:S(2)}, u32[]{:S(2)}) async-start(f32[8,8,32,128]{3,2,1,0:T(8,128)} %bitcast.31), calls=%async_computation | async-start | bytes 2097152 | tf_op jit(solution)/shard_map/all_to_all | solution.py:285
  15.3 12.5 %collective-permute-start.4 = (f32[10,32,1024]{2,1,0:T(8,128)}, f32[10,32,1024]{2,1,0:T(8,128)}, u32[]{:S(2)}, u32[]{:S(2)}) collective-permute-start(f32[10,32,1024]{2,1,0:T(8,128)} %pad_maximum_fusion), channel_id=1, source_target_pairs={{0,8},{8,16},{16,24},{1,9},{9,17},{17,25},{2,10},{10,18},{18,26},{... | collective-permute-start | bytes 3932168 | tf_op jit(solution)/shard_map/ppermute | solution.py:30
  19.0 10.2 %collective-permute-start.5 = (f32[10,32,1024]{2,1,0:T(8,128)}, f32[10,32,1024]{2,1,0:T(8,128)}, u32[]{:S(2)}, u32[]{:S(2)}) collective-permute-start(f32[10,32,1024]{2,1,0:T(8,128)} %pad_maximum_fusion.1), channel_id=1, source_target_pairs={{8,0},{16,8},{24,16},{9,1},{17,9},{25,17},{10,2},{18,10},{26,18},{... | collective-permute-start | bytes 3932168 | tf_op jit(solution)/shard_map/ppermute | solution.py:31
  29.3 1.9 copy-start.2
  31.1 7.7 %copy-start.3 = (f32[9,32,1024]{2,1,0:T(8,128)}, f32[9,32,1024]{2,1,0:T(8,128)S(1)}, u32[]{:S(2)}) copy-start(f32[9,32,1024]{2,1,0:T(8,128)S(1)} %slice.157) | copy-start | bytes 3538948
  38.8 91.4 %all-to-all-start.1 = ((f32[8,8,32,128]{3,2,1,0:T(8,128)}), f32[8,8,32,128]{3,2,1,0:T(8,128)S(1)}, u32[]{:S(2)}, u32[]{:S(2)}) async-start(f32[8,8,32,128]{3,2,1,0:T(8,128)} %bitcast.23), calls=%async_computation.1 | async-start | bytes 2097152 | tf_op jit(solution)/shard_map/all_to_all | solution.py:285
  42.4 2.6 %copy-start.4 = (f32[3,8,4,1024]{3,2,1,0:T(4,128)S(1)}, f32[3,8,4,1024]{3,2,1,0:T(4,128)}, u32[]{:S(2)}) copy-start(f32[3,8,4,1024]{3,2,1,0:T(4,128)} %get-tuple-element.15) | copy-start | bytes 1179652
  43.7 18.7 %collective-permute-start.1 = (f32[8,4,32,128]{3,2,1,0:T(8,128)S(1)}, f32[8,4,32,128]{3,2,1,0:T(8,128)S(1)}, u32[]{:S(2)}, u32[]{:S(2)}) collective-permute-start(f32[8,4,32,128]{3,2,1,0:T(8,128)S(1)} %get-tuple-element.32), channel_id=1, source_target_pairs={{8,0},{16,8},{24,16},{9,1},{17,9},{25,17},{10,2},{18,10},{26,18},{... | collective-permute-start | bytes 1572872 | tf_op jit(solution)/shard_map/ppermute | solution.py:31
  45.0 0.9 copy-start.10
  45.4 9.6 %copy-start.9 = (f32[8,4,1024]{2,1,0:T(4,128)S(1)}, f32[8,4,1024]{2,1,0:T(4,128)}, u32[]{:S(2)}) copy-start(f32[8,4,1024]{2,1,0:T(4,128)} %get-tuple-element.27) | copy-start | bytes 393220
  46.2 28.2 %collective-permute-start.7 = (f32[50,4,1024]{2,1,0:T(4,128)S(1)}, f32[50,4,1024]{2,1,0:T(4,128)}, u32[]{:S(2)}, u32[]{:S(2)}) collective-permute-start(f32[50,4,1024]{2,1,0:T(4,128)S(1)} %pad_maximum_fusion.3), channel_id=1, source_target_pairs={{1,0},{2,1},{3,2},{4,3},{5,4},{6,5},{7,6},{9,8},{10,9},{11,10},{12... | collective-permute-start | bytes 2457608 | tf_op jit(solution)/shard_map/ppermute | solution.py:31
  47.5 15.0 %collective-permute-start = (f32[8,4,32,128]{3,2,1,0:T(8,128)S(1)}, f32[8,4,32,128]{3,2,1,0:T(8,128)S(1)}, u32[]{:S(2)}, u32[]{:S(2)}) collective-permute-start(f32[8,4,32,128]{3,2,1,0:T(8,128)S(1)} %get-tuple-element.33), channel_id=1, source_target_pairs={{0,8},{8,16},{16,24},{1,9},{9,17},{17,25},{2,10},{10,18},{18,26},{... | collective-permute-start | bytes 1572872 | tf_op jit(solution)/shard_map/ppermute | solution.py:30
  56.2 44.5 %collective-permute-start.6 = (f32[50,4,1024]{2,1,0:T(4,128)}, f32[50,4,1024]{2,1,0:T(4,128)}, u32[]{:S(2)}, u32[]{:S(2)}) collective-permute-start(f32[50,4,1024]{2,1,0:T(4,128)} %pad_maximum_fusion.2), channel_id=1, source_target_pairs={{0,1},{1,2},{2,3},{3,4},{4,5},{5,6},{6,7},{8,9},{9,10},{10,11},{11... | collective-permute-start | bytes 2457608 | tf_op jit(solution)/shard_map/ppermute | solution.py:30
  62.4 15.5 %copy-start.5 = (f32[8,4,32,128]{3,2,1,0:T(8,128)}, f32[8,4,32,128]{3,2,1,0:T(8,128)S(1)}, u32[]{:S(2)}) copy-start(f32[8,4,32,128]{3,2,1,0:T(8,128)S(1)} %collective-permute-done.1.above) | copy-start | bytes 1572868
  62.5 15.4 %copy-start.6 = (f32[8,4,32,128]{3,2,1,0:T(8,128)}, f32[8,4,32,128]{3,2,1,0:T(8,128)S(1)}, u32[]{:S(2)}) copy-start(f32[8,4,32,128]{3,2,1,0:T(8,128)S(1)} %collective-permute-done.below) | copy-start | bytes 1572868
  63.4 52.0 %collective-permute-start.2 = (f32[8,16,4,128]{3,2,1,0:T(4,128)}, f32[8,16,4,128]{3,2,1,0:T(4,128)S(1)}, u32[]{:S(2)}, u32[]{:S(2)}) collective-permute-start(f32[8,16,4,128]{3,2,1,0:T(4,128)} %pad_maximum_fusion.6), channel_id=1, source_target_pairs={{0,1},{1,2},{2,3},{3,4},{4,5},{5,6},{6,7},{8,9},{9,10},{10,11},{11... | collective-permute-start | bytes 786440 | tf_op jit(solution)/shard_map/ppermute | solution.py:30
  67.9 47.6 %collective-permute-start.3 = (f32[8,16,4,128]{3,2,1,0:T(4,128)}, f32[8,16,4,128]{3,2,1,0:T(4,128)}, u32[]{:S(2)}, u32[]{:S(2)}) collective-permute-start(f32[8,16,4,128]{3,2,1,0:T(4,128)} %pad_maximum_fusion.7), channel_id=1, source_target_pairs={{1,0},{2,1},{3,2},{4,3},{5,4},{6,5},{7,6},{9,8},{10,9},{11,10},{12... | collective-permute-start | bytes 786440 | tf_op jit(solution)/shard_map/ppermute | solution.py:31
  115.5 0.7 copy-start.11
  132.3 6.6 %copy-start.1 = (f32[8,8,32,128]{3,2,1,0:T(8,128)}, f32[8,8,32,128]{3,2,1,0:T(8,128)S(1)}, u32[]{:S(2)}) copy-start(f32[8,8,32,128]{3,2,1,0:T(8,128)S(1)} %get-tuple-element.13.own) | copy-start | bytes 3145732
  132.4 12.2 %copy-start.14 = (f32[8,128]{1,0:T(8,128)S(1)}, f32[8,128]{1,0:T(8,128)}, u32[]{:S(2)}) copy-start(f32[8,128]{1,0:T(8,128)} %get-tuple-element.11) | copy-start | bytes 12292
  132.4 5.1 %collective-permute-start.9 = (f32[8,3,32,128]{3,2,1,0:T(8,128)S(1)}, f32[8,3,32,128]{3,2,1,0:T(8,128)S(1)}, u32[]{:S(2)}, u32[]{:S(2)}) collective-permute-start(f32[8,3,32,128]{3,2,1,0:T(8,128)S(1)} %get-tuple-element.24), channel_id=1, source_target_pairs={{8,0},{16,8},{24,16},{9,1},{17,9},{25,17},{10,2},{18,10},{26,18},{... | collective-permute-start | bytes 1179656 | tf_op jit(solution)/shard_map/ppermute | solution.py:31
  133.7 5.1 %collective-permute-start.8 = (f32[8,3,32,128]{3,2,1,0:T(8,128)S(1)}, f32[8,3,32,128]{3,2,1,0:T(8,128)S(1)}, u32[]{:S(2)}, u32[]{:S(2)}) collective-permute-start(f32[8,3,32,128]{3,2,1,0:T(8,128)S(1)} %get-tuple-element.25), channel_id=1, source_target_pairs={{0,8},{8,16},{16,24},{1,9},{9,17},{17,25},{2,10},{10,18},{18,26},{... | collective-permute-start | bytes 1179656 | tf_op jit(solution)/shard_map/ppermute | solution.py:30
  137.6 32.1 %copy-start.7 = (f32[8,3,32,128]{3,2,1,0:T(8,128)}, f32[8,3,32,128]{3,2,1,0:T(8,128)S(1)}, u32[]{:S(2)}) copy-start(f32[8,3,32,128]{3,2,1,0:T(8,128)S(1)} %collective-permute-done.9.above) | copy-start | bytes 1179652
  138.8 30.9 %copy-start.8 = (f32[8,3,32,128]{3,2,1,0:T(8,128)}, f32[8,3,32,128]{3,2,1,0:T(8,128)S(1)}, u32[]{:S(2)}) copy-start(f32[8,3,32,128]{3,2,1,0:T(8,128)S(1)} %collective-permute-done.8.below) | copy-start | bytes 1179652
  138.9 30.8 %collective-permute-start.10 = (f32[8,14,4,128]{3,2,1,0:T(4,128)S(1)}, f32[8,14,4,128]{3,2,1,0:T(4,128)S(1)}, u32[]{:S(2)}, u32[]{:S(2)}) collective-permute-start(f32[8,14,4,128]{3,2,1,0:T(4,128)S(1)} %pad_maximum_fusion.8), channel_id=1, source_target_pairs={{0,1},{1,2},{2,3},{3,4},{4,5},{5,6},{6,7},{8,9},{9,10},{10,11},{11... | collective-permute-start | bytes 688136 | tf_op jit(solution)/shard_map/ppermute | solution.py:30
  143.3 26.4 %collective-permute-start.11 = (f32[8,14,4,128]{3,2,1,0:T(4,128)S(1)}, f32[8,14,4,128]{3,2,1,0:T(4,128)S(1)}, u32[]{:S(2)}, u32[]{:S(2)}) collective-permute-start(f32[8,14,4,128]{3,2,1,0:T(4,128)S(1)} %pad_maximum_fusion.9), channel_id=1, source_target_pairs={{1,0},{2,1},{3,2},{4,3},{5,4},{6,5},{7,6},{9,8},{10,9},{11,10},{12... | collective-permute-start | bytes 688136 | tf_op jit(solution)/shard_map/ppermute | solution.py:31
  169.7 0.7 copy-start.12
  169.7 0.7 copy-start.13
where the time goes:
time: 192 us; the launch traced here: 191 us
  starting transfers between devices  45.6 us (24%)
  Pallas kernels  44.5 us (23%)
  waiting for transfers between devices  33 us (17%)
  local copies, waits for them, and re-layouts  31.9 us (17%)
  blocking collectives  21.9 us (11%)
  other arithmetic  9.75 us (5%)
  between operations  4.17 us (2%)
    ppermute x6, starting transfers between devices, exchange(): lax.ppermute(high_part, axis, [(i, i + 1) for i in range(count - 1)])  27 us
    ppermute x6, waiting for transfers between devices, exchange(): lax.ppermute(high_part, axis, [(i, i + 1) for i in range(count - 1)])  23.9 us
    all_to_all x1, blocking collectives, local(): lax.all_to_all(jnp.full((everyone, LANES), partial), ('sec', 'row'), spli...  21.9 us
    pallas_call x1, Pallas kernels, local(): call(adjoint_kernel, [((3, sections, rows, width), VMEM)], [SMEM] + [VMEM...  19.2 us
    pallas_call x1, Pallas kernels, local(): call(forward_kernel, [((blocks, sections, rows, LANES), VMEM), ((STEPS, b...  14 us
    pallas_call x1, Pallas kernels, regular(): call(regular_kernel, [((3, blocks, deep, tall, LANES), VMEM), ((3, sectio...  11.3 us
    all_to_all x2, starting transfers between devices, to_rows(): lax.all_to_all(parts, 'row', split_axis=0, concat_axis=0, tiled=True)  10.9 us
    ppermute x6, starting transfers between devices, exchange(): above = lax.ppermute(low_part, axis, [(i + 1, i) for i in range(count - 1)])  7.73 us
  transfers between devices with their start and end apart: 14, of which 4 were waited for; matrix products, arithmetic and copies ran while one was open for 17% of the time, Pallas kernels for 13%

commit v1 on v0

v1 whole, which is shorter than its diff:
```python
import jax
import jax.numpy as jnp
from jax import lax
from jax.experimental import pallas as pl
from jax.experimental.pallas import tpu as pltpu
from jax.sharding import PartitionSpec as P

STEPS = 4

DT = 0.25
KAPPA = 0.5
BETA = 0.5

LANES = 128
TILE = 8
GAP = 8
SENT = 4
WIDE = STEPS - 1
WEIGHT = DT * KAPPA
SELF = 1.0 - 6.0 * WEIGHT
assert WEIGHT == DT * 0.5

VMEM = pl.BlockSpec(memory_space=pltpu.VMEM)
SMEM = pl.BlockSpec(memory_space=pltpu.SMEM)
ANY = pl.BlockSpec(memory_space=pl.ANY)


def exchange(low_part, high_part, axis):
    count = lax.axis_size(axis)
    below = lax.ppermute(high_part, axis, [(i, i + 1) for i in range(count - 1)])
    above = lax.ppermute(low_part, axis, [(i + 1, i) for i in range(count - 1)])
    return below, above


def edges(tiles_up, tiles_down):
    lane = lax.broadcasted_iota(jnp.int32, tiles_up[0].shape, 1)
    zero = jnp.zeros_like(tiles_up[0])
    up = [pltpu.roll(t, LANES - 1, 1) for t in tiles_up]
    down = [pltpu.roll(t, 1, 1) for t in tiles_down]
    plus = [jnp.where(lane == LANES - 1, n, u) for u, n in zip(up, up[1:] + [zero])]
    minus = [jnp.where(lane == 0, p, d) for d, p in zip(down, [zero] + down[:-1])]
    return plus, minus


def edges_of(tiles):
    return edges(tiles, tiles)


def fill(out, own, below, above, before, after, corners_below, corners_above, width):
    blocks, sections, rows, _ = own.shape
    top, bottom = pl.ds(GAP - SENT, SENT), pl.ds(GAP + rows, SENT)

    def whole(z, _):
        for i in range(blocks):
            out[i, z + width, pl.ds(GAP, rows), :] = own[i, z, :, :]
            out[i, z + width, top, :] = before[i, z, :, :]
            out[i, z + width, bottom, :] = after[i, z, :, :]
        return 0

    def halo(z, _):
        for planes, corners, at in ((below, corners_below, z), (above, corners_above, z + width + sections)):
            for i in range(blocks):
                out[i, at, pl.ds(GAP, rows), :] = planes[i, z, :, :]
                out[i, at, top, :] = corners[i, z, pl.ds(0, SENT), :]
                out[i, at, bottom, :] = corners[i, z, pl.ds(SENT, SENT), :]
        return 0

    lax.fori_loop(0, sections, whole, 0)
    lax.fori_loop(0, width, halo, 0)


def block_kernel(scan, out):
    sections, width, rows = scan.shape
    own = out.shape[2]

    def section(z, _):
        for cut in range(0, rows, width):
            turned = scan[z, :, pl.ds(cut, width)].T
            for r in range(0, width, own):
                out[(cut + r) // own, z, :, :] = turned[r : r + own]
        return 0

    lax.fori_loop(0, sections, section, 0)


def part_kernel(field, low_rows, high_rows, low, high):
    blocks, sections, rows, _ = field.shape
    width = low.shape[1]

    def row_ends(z, _):
        for i in range(blocks):
            low_rows[i, z, :, :] = field[i, z, pl.ds(0, SENT), :]
            high_rows[i, z, :, :] = field[i, z, pl.ds(rows - SENT, SENT), :]
        return 0

    def planes(z, _):
        for i in range(blocks):
            low[i, z, :, :] = field[i, z, :, :]
            high[i, z, :, :] = field[i, z + sections - width, :, :]
        return 0

    lax.fori_loop(0, sections, row_ends, 0)
    lax.fori_loop(0, width, planes, 0)


def misfit_kernel(moved, fixed, sums, misfit, low_rows, high_rows, low, high, total_ref):
    blocks, sections, rows, _ = moved.shape

    def section(z, acc):
        for i in range(blocks):
            for r in range(0, rows, TILE):
                value = moved[i, z, pl.ds(r, TILE), :] - fixed[i, z, pl.ds(r, TILE), :]
                misfit[i, z, pl.ds(r, TILE), :] = value
                acc = acc + value * value
        return acc

    zero = jnp.zeros((TILE, LANES), jnp.float32)
    total_ref[...] = 0.5 * (lax.fori_loop(0, sections, section, zero) + sums[...])
    part_kernel(misfit, low_rows, high_rows, low, high)


def groups(rows, reach):
    if reach == 0:
        return [GAP + g for g in range(0, rows, TILE)]
    return [GAP - SENT + g for g in range(0, rows + TILE, TILE)]


def masked(value, start, rows, flags):
    row = start + lax.broadcasted_iota(jnp.int32, value.shape, 0)
    if start < GAP:
        return jnp.where((row >= GAP) | (flags[2] > 0.5), value, 0.0)
    if start + TILE > GAP + rows:
        return jnp.where((row < GAP + rows) | (flags[3] > 0.5), value, 0.0)
    return value


def weights(flags, z, low, high):
    factor = jnp.where(z < low, flags[0], jnp.where(z >= high, flags[1], 1.0))
    return SELF * factor, WEIGHT * factor


def forward_kernel(flags, own, below, above, before, after, low_corners, high_corners, vel, moved_ref, *levels):
    blocks, sections, rows, _ = own.shape
    fill(levels[0], own, below, above, before, after, low_corners, high_corners, STEPS)
    for step in range(STEPS):
        src = levels[step]
        reach = STEPS - 1 - step

        def plane(z, _, src=src, step=step, reach=reach):
            keep, weight = weights(flags, z, STEPS, STEPS + sections)
            for r in groups(rows, reach):
                here = pl.ds(r, TILE)
                mids = [src[i, z, here, :] for i in range(blocks)]
                plus, minus = edges_of(mids)
                for i in range(blocks):
                    zp, zm = src[i, z + 1, here, :], src[i, z - 1, here, :]
                    xp, xm = src[i, z, pl.ds(r + 1, TILE), :], src[i, z, pl.ds(r - 1, TILE), :]
                    yp, ym = plus[i], minus[i]
                    total = (zp + zm) - vel[0, i, z - 1, here, :] * (zp - zm)
                    total = total + ((xp + xm) - vel[1, i, z - 1, here, :] * (xp - xm))
                    total = total + ((yp + ym) - vel[2, i, z - 1, here, :] * (yp - ym))
                    value = keep * mids[i] + weight * total
                    if step == STEPS - 1:
                        moved_ref[i, z - STEPS, pl.ds(r - GAP, TILE), :] = value
                    else:
                        levels[step + 1][i, z, here, :] = masked(value, r, rows, flags)
            return 0

        lax.fori_loop(STEPS - reach, STEPS + sections + reach, plane, 0)


def adjoint_kernel(flags, own, below, above, before, after, low_corners, high_corners, vel, *refs):
    kept, reg, grad_ref, levels = refs[:STEPS], refs[STEPS], refs[STEPS + 1], refs[STEPS + 2 :]
    blocks, sections, rows, _ = own.shape
    fill(levels[0], own, below, above, before, after, low_corners, high_corners, WIDE)
    for step in range(WIDE):
        src, out = levels[step], levels[step + 1]
        reach = WIDE - 1 - step

        def plane(z, _, src=src, out=out, reach=reach):
            keep, weight = weights(flags, z, WIDE, WIDE + sections)
            for r in groups(rows, reach):
                here, up, down = pl.ds(r, TILE), pl.ds(r + 1, TILE), pl.ds(r - 1, TILE)
                mids = [src[i, z, here, :] for i in range(blocks)]
                prods = [mids[i] * vel[2, i, z, here, :] for i in range(blocks)]
                plus, minus = edges(
                    [m + p for m, p in zip(mids, prods)], [m - p for m, p in zip(mids, prods)]
                )
                for i in range(blocks):
                    zp, zm = src[i, z + 1, here, :], src[i, z - 1, here, :]
                    xp, xm = src[i, z, up, :], src[i, z, down, :]
                    total = plus[i] + minus[i]
                    total = total + (zp + zp * vel[0, i, z + 1, here, :])
                    total = total + (zm - zm * vel[0, i, z - 1, here, :])
                    total = total + (xp + xp * vel[1, i, z, up, :])
                    total = total + (xm - xm * vel[1, i, z, down, :])
                    value = keep * mids[i] + weight * total
                    if reach > 0:
                        value = masked(value, r, rows, flags)
                    out[i, z, here, :] = value
            return 0

        lax.fori_loop(WIDE - reach, WIDE + sections + reach, plane, 0)

    def slope(z, _):
        for r in groups(rows, 0):
            here, up, down = pl.ds(r, TILE), pl.ds(r + 1, TILE), pl.ds(r - 1, TILE)
            at = pl.ds(r - GAP, TILE)
            sums = [[None] * 3 for _ in range(blocks)]
            for k in range(STEPS):
                adj = [levels[STEPS - 1 - k][i, z + WIDE, here, :] for i in range(blocks)]
                plus, minus = edges_of([kept[k][i, z + STEPS, here, :] for i in range(blocks)])
                for i in range(blocks):
                    parts = (
                        adj[i] * (kept[k][i, z + STEPS + 1, here, :] - kept[k][i, z + STEPS - 1, here, :]),
                        adj[i] * (kept[k][i, z + STEPS, up, :] - kept[k][i, z + STEPS, down, :]),
                        adj[i] * (plus[i] - minus[i]),
                    )
                    for a in range(3):
                        sums[i][a] = parts[a] if k == 0 else sums[i][a] + parts[a]
            for i in range(blocks):
                lanes = pl.ds(i * LANES, LANES)
                for a in range(3):
                    grad_ref[a, z, at, lanes] = reg[a, z, at, lanes] - (0.5 * DT) * sums[i][a]
        return 0

    lax.fori_loop(0, sections, slope, 0)


def regular_kernel(vel, sti, planes_below, planes_above, before, after, corners_below, corners_above,
                   ext_ref, reg_ref, sum_ref, sti_ext):
    _, sections, rows, width = vel.shape
    blocks = width // LANES

    def lay(out, src, z):
        for i in range(blocks):
            out[i, z, pl.ds(GAP, rows), :] = src[:, pl.ds(i * LANES, LANES)]

    def lay_rows(out, z, row, src, at, count):
        for i in range(blocks):
            out[i, z, pl.ds(row, count), :] = src[pl.ds(at, count), pl.ds(i * LANES, LANES)]

    def mid(z, _):
        for c in range(3):
            lay(ext_ref.at[c], vel.at[c, z], z + WIDE)
        lay(sti_ext, sti.at[z], z + 1)
        return 0

    def far(z, _):
        for c in range(3):
            lay(ext_ref.at[c], planes_below.at[c * WIDE + z], z)
            lay(ext_ref.at[c], planes_above.at[c * WIDE + z], z + WIDE + sections)
        return 0

    lax.fori_loop(0, sections, mid, 0)
    lax.fori_loop(0, WIDE, far, 0)
    lay(sti_ext, planes_below.at[3 * WIDE], 0)
    lay(sti_ext, planes_above.at[3 * WIDE], sections + 1)
    low, high = GAP - WIDE, GAP + rows
    for c in range(3):
        for z in range(sections):
            at = (c * sections + z) * WIDE
            lay_rows(ext_ref.at[c], z + WIDE, low, before, at, WIDE)
            lay_rows(ext_ref.at[c], z + WIDE, high, after, at, WIDE)
        for z in range(WIDE):
            at, half = (c * WIDE + z) * WIDE, 3 * WIDE * WIDE
            for src, z_out in ((corners_below, z), (corners_above, z + WIDE + sections)):
                lay_rows(ext_ref.at[c], z_out, low, src, at, WIDE)
                lay_rows(ext_ref.at[c], z_out, high, src, at + half, WIDE)
    for z in range(sections):
        at = 3 * sections * WIDE + z
        lay_rows(sti_ext, z + 1, GAP - 1, before, at, 1)
        lay_rows(sti_ext, z + 1, GAP + rows, after, at, 1)

    def plane(z, acc):
        for r in groups(rows, 0):
            here, up, down = pl.ds(r, TILE), pl.ds(r + 1, TILE), pl.ds(r - 1, TILE)
            at = pl.ds(r - GAP, TILE)
            s_mid = [sti_ext[i, z + 1, here, :] for i in range(blocks)]
            s_plus, s_minus = edges_of(s_mid)
            faces = []
            for i in range(blocks):
                s = s_mid[i]
                faces.append([
                    (s + sti_ext[i, z, here, :], s + sti_ext[i, z + 2, here, :]),
                    (s + sti_ext[i, z + 1, down, :], s + sti_ext[i, z + 1, up, :]),
                    (s + s_minus[i], s + s_plus[i]),
                ])
            for c in range(3):
                v_mid = [ext_ref[c, i, z + WIDE, here, :] for i in range(blocks)]
                v_plus, v_minus = edges_of(v_mid)
                for i in range(blocks):
                    v = v_mid[i]
                    pairs = (
                        (ext_ref[c, i, z + WIDE - 1, here, :], ext_ref[c, i, z + WIDE + 1, here, :]),
                        (ext_ref[c, i, z + WIDE, down, :], ext_ref[c, i, z + WIDE, up, :]),
                        (v_minus[i], v_plus[i]),
                    )
                    total = None
                    for (low, high), (f_low, f_high) in zip(pairs, faces[i]):
                        part = f_low * (v - low) + f_high * (v - high)
                        total = part if total is None else total + part
                    term = (0.5 * BETA) * total
                    reg_ref[c, z, at, pl.ds(i * LANES, LANES)] = term
                    acc = acc + v * term
        return acc

    acc = lax.fori_loop(0, sections, plane, jnp.zeros((TILE, LANES), jnp.float32))
    sum_ref[...] = acc


def to_rows(scan):
    count = lax.axis_size("row")
    sections, width, rows = scan.shape
    own = rows // count
    shape = (count, sections, own, width)
    if width == LANES and rows % width == 0 and width % own == 0:
        (parts,) = call(block_kernel, [shape], [VMEM], [])(scan)
    else:
        parts = jnp.swapaxes(scan, 1, 2).reshape(sections, count, own, width).transpose(1, 0, 2, 3)
    parts = lax.all_to_all(parts, "row", split_axis=0, concat_axis=0, tiled=True)
    if width == LANES:
        return parts
    whole = parts.transpose(1, 2, 0, 3).reshape(sections, own, count * width // LANES, LANES)
    return whole.transpose(2, 0, 1, 3)


def part_shapes(shape, width):
    blocks, sections, rows, _ = shape
    return [(blocks, sections, SENT, LANES)] * 2 + [(blocks, width, rows, LANES)] * 2


def halos(low_rows, high_rows, low, high):
    width = low.shape[1]
    before, after = exchange(low_rows, high_rows, "row")
    below, above = exchange(low, high, "sec")
    corners = [
        jnp.concatenate([before[:, cut], after[:, cut]], axis=2)
        for cut in (slice(0, width), slice(before.shape[1] - width, None))
    ]
    return (below, above, before, after) + exchange(*corners, "sec")


def everywhere(part):
    for axis in ("row", "sec"):
        count, near = lax.axis_size(axis), 1
        if count & (count - 1):
            part = lax.psum(part, axis)
            continue
        while near < count:
            part = part + lax.ppermute(part, axis, [(i, i ^ near) for i in range(count)])
            near *= 2
    return part


def call(kernel, shapes, ins, scratch, flops=0, megabytes=20):
    return pl.pallas_call(
        kernel,
        out_shape=[jax.ShapeDtypeStruct(shape, jnp.float32) for shape in shapes],
        in_specs=ins,
        out_specs=[VMEM] * len(shapes),
        scratch_shapes=[pltpu.VMEM(shape, jnp.float32) for shape in scratch],
        compiler_params=pltpu.CompilerParams(vmem_limit_bytes=megabytes << 20),
        cost_estimate=pl.CostEstimate(flops=flops, bytes_accessed=4 << 20, transcendentals=0),
    )


def local(template_scan, reference_scan, velocity, stiffness):
    _, sections, rows, width = velocity.shape
    blocks = width // LANES
    tall, deep = rows + 2 * GAP, sections + 2 * WIDE
    own = (blocks, sections, rows, LANES)
    sec, row = lax.axis_index("sec"), lax.axis_index("row")
    flags = jnp.stack([
        sec > 0, sec < lax.axis_size("sec") - 1, row > 0, row < lax.axis_size("row") - 1
    ]).astype(jnp.float32)

    template = to_rows(template_scan)

    sides = [
        jnp.concatenate([velocity[:, :, cut].reshape(-1, width), stiffness[:, one]], axis=0)
        for cut, one in ((slice(0, WIDE), 0), (slice(rows - WIDE, rows), rows - 1))
    ]
    before, after = exchange(sides[0], sides[1], "row")
    planes = [
        jnp.concatenate([velocity[:, cut].reshape(-1, rows, width), stiffness[one]], axis=0)
        for cut, one in (
            (slice(0, WIDE), slice(0, 1)), (slice(sections - WIDE, sections), slice(sections - 1, sections))
        )
    ]
    below, above = exchange(planes[0], planes[1], "sec")
    corners = [
        jnp.concatenate([
            side[: 3 * sections * WIDE].reshape(3, sections, WIDE, width)[:, cut].reshape(-1, width)
            for side in (before, after)
        ], axis=0)
        for cut in (slice(0, WIDE), slice(sections - WIDE, sections))
    ]
    corners_below, corners_above = exchange(corners[0], corners[1], "sec")
    extended, reg, reg_sums = call(
        regular_kernel,
        [(3, blocks, deep, tall, LANES), velocity.shape, (TILE, LANES)],
        [VMEM] * 8,
        [(blocks, sections + 2, tall, LANES)],
        20 << 20,
    )(velocity, stiffness, below, above, before, after, corners_below, corners_above)

    parts = call(part_kernel, part_shapes(own, STEPS), [VMEM], [])(template)
    moved, *levels = call(
        forward_kernel,
        [own] + [(blocks, sections + 2 * STEPS, tall, LANES)] * STEPS,
        [SMEM] + [VMEM] * 8,
        [],
        20 << 20,
    )(flags, template, *halos(*parts), extended)

    fixed = to_rows(reference_scan)
    misfit, *parts, partial = call(
        misfit_kernel, [own] + part_shapes(own, WIDE) + [(TILE, LANES)], [VMEM] * 3, []
    )(moved, fixed, reg_sums)
    (gradient,) = call(
        adjoint_kernel,
        [velocity.shape],
        [SMEM] + [VMEM] * (9 + STEPS),
        [(blocks, deep, tall, LANES)] * STEPS,
        20 << 20,
    )(flags, misfit, *halos(*parts), extended, *levels, reg)

    voxels = sections * rows * width * lax.axis_size("sec") * lax.axis_size("row")
    objective = jnp.sum(everywhere(partial)) / voxels
    return (gradient, objective)


def solution(mesh):
    return jax.shard_map(
        local,
        mesh=mesh,
        in_specs=(
            P("sec", "row", None),
            P("sec", "row", None),
            P(None, "sec", "row", None),
            P("sec", "row", None),
        ),
        out_specs=(P(None, "sec", "row", None), P()),
        check_vma=False,
    )
```

time: 192 us -> 212 us (1.10); the launches traced: 191 us -> 208 us
  local copies, waits for them, and re-layouts: 31.9 us -> 70.5 us
  starting transfers between devices: 45.6 us -> 68.4 us
  blocking collectives: 21.9 us -> 0 us
  waiting for transfers between devices: 33 us -> 20.9 us
  Pallas kernels: 44.5 us -> 34.5 us
    unnamed x32 -> x78, local copies, waits for them, and re-layouts: 7.04 us -> 45.6 us
    ppermute x6 -> x9, waiting for transfers between devices: 23.9 us -> 0.02 us  [exchange(): lax.ppermute(high_part, axis, [(i, i + 1) for i in range(count - 1)])]
    all_to_all x1 -> x0, blocking collectives: 21.9 us -> none  [local(): lax.all_to_all(jnp.full((everyone, LANES), partial), ('sec', 'row'), spli...]
    pallas_call x3 -> x7, Pallas kernels: 44.5 us -> 34.5 us  [the longest x1 12.3 us: local(): call(adjoint_kernel, [velocity.shape], [SMEM] + [VMEM] * (9 + STEPS), [(b...]
    ppermute x6 -> x9, starting transfers between devices: 27 us -> 36.3 us  [exchange(): lax.ppermute(high_part, axis, [(i, i + 1) for i in range(count - 1)])]
    ppermute x0 -> x5, starting transfers between devices: none -> 8.99 us  [everywhere(): lax.ppermute(part, axis, [(i, i ^ near) for i in range(count)])]
    ppermute x0 -> x5, waiting for transfers between devices: none -> 8.93 us  [everywhere(): lax.ppermute(part, axis, [(i, i ^ near) for i in range(count)])]
    reshape x2 -> x8, local copies, waits for them, and re-layouts: 4.76 us -> 13.2 us  [the longest x6 10.2 us: local(): side[:3 * sections * WIDE].reshape(3, sections, WIDE, width)[:, cut]]
  transfers between devices with their start and end apart: 14 -> 25, of which waited for: 4 -> 8; matrix products, arithmetic and copies ran while one was open for 17% -> 17% of each run, Pallas kernels for 13% -> 9%
where the time goes in v1:
time: 212 us; the launch traced here: 208 us
  local copies, waits for them, and re-layouts  70.5 us (33%)
  starting transfers between devices  68.4 us (32%)
  Pallas kernels  34.5 us (16%)
  waiting for transfers between devices  20.9 us (10%)
  other arithmetic  11 us (5%)
  between operations  2.84 us (1%)
    unnamed x78, local copies, waits for them, and re-layouts  45.6 us
    ppermute x9, starting transfers between devices, exchange(): lax.ppermute(high_part, axis, [(i, i + 1) for i in range(count - 1)])  36.3 us
    pallas_call x1, Pallas kernels, local(): call(adjoint_kernel, [velocity.shape], [SMEM] + [VMEM] * (9 + STEPS), [(b...  12.3 us
    ppermute x9, starting transfers between devices, exchange(): above = lax.ppermute(low_part, axis, [(i + 1, i) for i in range(count - 1)])  11.6 us
    all_to_all x2, starting transfers between devices, to_rows(): lax.all_to_all(parts, 'row', split_axis=0, concat_axis=0, tiled=True)  11.5 us
    pallas_call x1, Pallas kernels, local(): call(forward_kernel, [own] + [(blocks, sections + 2 * STEPS, tall, LANES)...  10.2 us
    reshape x6, local copies, waits for them, and re-layouts, local(): side[:3 * sections * WIDE].reshape(3, sections, WIDE, width)[:, cut]  10.2 us
    all_to_all x2, waiting for transfers between devices, to_rows(): lax.all_to_all(parts, 'row', split_axis=0, concat_axis=0, tiled=True)  9.68 us
  transfers between devices with their start and end apart: 25, of which 8 were waited for; matrix products, arithmetic and copies ran while one was open for 17% of the time, Pallas kernels for 9%

profile of v1, /device:TPU:0, one launch (start us, length us, event | category | flops | bytes accessed | tf_op | source)
XLA Modules:
  0.0 208.2 jit_solution(17635812001310469958)
XLA Ops:
  3.6 7.3 %all-to-all-start = ((f32[8,8,32,128]{3,2,1,0:T(8,128)}), f32[8,8,32,128]{3,2,1,0:T(8,128)}, u32[]{:S(2)}, u32[]{:S(2)}) async-start(f32[8,8,32,128]{3,2,1,0:T(8,128)} %copy-done.4), calls=%async_computation | async-start | bytes 2097152 | tf_op jit(solution)/shard_map/all_to_all | solution.py:321
  15.0 3.9 %collective-permute-start.8 = (f32[80,1024]{1,0:T(8,128)}, f32[80,1024]{1,0:T(8,128)S(1)}, u32[]{:S(2)}, u32[]{:S(2)}) collective-permute-start(f32[80,1024]{1,0:T(8,128)} %pad_maximum_fusion.2), channel_id=1, source_target_pairs={{0,1},{1,2},{2,3},{3,4},{4,5},{5,6},{6,7},{8,9},{9,10},{10,11},{11... | collective-permute-start | bytes 983048 | tf_op jit(solution)/shard_map/ppermute | solution.py:30
  19.0 1.8 reshape.39
  20.8 1.7 pad_maximum_fusion.3
  26.9 1.7 fusion.1
  28.6 9.7 %all-to-all-done.field.own = f32[8,8,32,128]{3,2,1,0:T(8,128)} async-done(((f32[8,8,32,128]{3,2,1,0:T(8,128)}), f32[8,8,32,128]{3,2,1,0:T(8,128)}, u32[]{:S(2)}, u32[]{:S(2)}) %all-to-all-start) | async-done | bytes 1048608 | tf_op jit(solution)/shard_map/all_to_all | solution.py:321
  38.3 4.2 %all-to-all-start.1 = ((f32[8,8,32,128]{3,2,1,0:T(8,128)}), f32[8,8,32,128]{3,2,1,0:T(8,128)}, u32[]{:S(2)}, u32[]{:S(2)}) async-start(f32[8,8,32,128]{3,2,1,0:T(8,128)} %copy-done.3), calls=%async_computation.1 | async-start | bytes 2097152 | tf_op jit(solution)/shard_map/all_to_all | solution.py:321
  43.5 2.6 %pad_maximum_fusion = f32[10,32,1024]{2,1,0:T(8,128)} fusion(f32[1,32,1024]{2,1,0:T(8,128)S(1)} %get-tuple-element.45, f32[9,32,1024]{2,1,0:T(8,128)} %bitcast.13), kind=kLoop, calls=%fused_computation | loop fusion | flops 327680 | bytes 2621440 | tf_op jit(solution)/shard_map/concatenate | solution.py:386
  46.1 2.4 %collective-permute-start.6 = (f32[10,32,1024]{2,1,0:T(8,128)}, f32[10,32,1024]{2,1,0:T(8,128)}, u32[]{:S(2)}, u32[]{:S(2)}) collective-permute-start(f32[10,32,1024]{2,1,0:T(8,128)} %pad_maximum_fusion), channel_id=1, source_target_pairs={{0,8},{8,16},{16,24},{1,9},{9,17},{17,25},{2,10},{10,18},{18,26},{... | collective-permute-start | bytes 3932168 | tf_op jit(solution)/shard_map/ppermute | solution.py:30
  51.6 1.8 reshape.40
  53.5 1.8 fusion.4
  55.2 1.6 reshape.41
  56.9 1.7 slice.96
  58.6 1.8 reshape.42
  60.4 1.8 fusion.5
  62.2 1.6 reshape.43
  63.8 2.0 shard_map.60
  68.1 4.4 %collective-permute-start.2 = (f32[8,8,4,128]{3,2,1,0:T(4,128)}, f32[8,8,4,128]{3,2,1,0:T(4,128)}, u32[]{:S(2)}, u32[]{:S(2)}) collective-permute-start(f32[8,8,4,128]{3,2,1,0:T(4,128)} %get-tuple-element.22), channel_id=1, source_target_pairs={{0,1},{1,2},{2,3},{3,4},{4,5},{5,6},{6,7},{8,9},{9,10},{10,11},{11... | collective-permute-start | bytes 393224 | tf_op jit(solution)/shard_map/ppermute | solution.py:30
  72.6 1.7 pad_maximum_fusion.4
  74.3 1.6 reshape.44
  75.9 1.6 reshape.45
  77.5 3.4 %collective-permute-start.10 = (f32[54,1024]{1,0:T(8,128)}, f32[54,1024]{1,0:T(8,128)S(1)}, u32[]{:S(2)}, u32[]{:S(2)}) collective-permute-start(f32[54,1024]{1,0:T(8,128)} %pad_maximum_fusion.4), channel_id=1, source_target_pairs={{0,8},{8,16},{16,24},{1,9},{9,17},{17,25},{2,10},{10,18},{18,26},{... | collective-permute-start | bytes 663560 | tf_op jit(solution)/shard_map/ppermute | solution.py:30
  83.2 4.7 %collective-permute-start = (f32[8,4,32,128]{3,2,1,0:T(8,128)}, f32[8,4,32,128]{3,2,1,0:T(8,128)}, u32[]{:S(2)}, u32[]{:S(2)}) collective-permute-start(f32[8,4,32,128]{3,2,1,0:T(8,128)} %copy-done.35), channel_id=1, source_target_pairs={{0,8},{8,16},{16,24},{1,9},{9,17},{17,25},{2,10},{10,18},{18,26},{... | collective-permute-start | bytes 1572872 | tf_op jit(solution)/shard_map/ppermute | solution.py:30
  94.7 1.7 collective-permute-done.11.corners_above
  97.1 9.6 %collective-permute-start.4 = (f32[8,4,8,128]{3,2,1,0:T(8,128)}, f32[8,4,8,128]{3,2,1,0:T(8,128)}, u32[]{:S(2)}, u32[]{:S(2)}) collective-permute-start(f32[8,4,8,128]{3,2,1,0:T(8,128)} %pad_maximum_fusion.6), channel_id=1, source_target_pairs={{0,8},{8,16},{16,24},{1,9},{9,17},{17,25},{2,10},{10,18},{18,26},{... | collective-permute-start | bytes 393224 | tf_op jit(solution)/shard_map/ppermute | solution.py:30
  111.1 5.8 %shard_map.61 = (f32[3,8,14,48,128]{4,3,2,1,0:T(8,128)S(1)}, f32[3,8,32,1024]{3,2,1,0:T(8,128)S(1)}, f32[8,128]{1,0:T(8,128)S(1)}) custom-call(f32[3,8,32,1024]{3,2,1,0:T(8,128)S(1)} %copy-done.2, f32[8,32,1024]{2,1,0:T(8,128)S(1)} %copy-done.15, f32[10,32,1024]{2,1,0:T(8,128)} %collective-permute-done.6.planes_below, ...), custom_call_target="tpu_custom_call" | custom-call | flops 20971520 | bytes 4194304 | tf_op jit(solution)/shard_map/pallas_call | solution.py:400
  118.6 10.2 %shard_map.62 = (f32[8,8,32,128]{3,2,1,0:T(8,128)S(1)}, f32[8,16,48,128]{3,2,1,0:T(8,128)S(1)}, f32[8,16,48,128]{3,2,1,0:T(8,128)S(1)}, f32[8,16,48,128]{3,2,1,0:T(8,128)S(1)}, f32[8,16,48,128]{3,2,1,0:T(8,128)S(1)}) custom-call(f32[4]{0:T(128)S(1)} %add_convert_fusion.flags, f32[8,8,32,128]{3,2,1,0:T(8,128)} %all-to-all-done.field.own, ...), custom_call_target="tpu_custom_call" | custom-call | flops 20971520 | bytes 4194304 | tf_op jit(solution)/shard_map/pallas_call | solution.py:409
  128.9 3.3 %copy-done = f32[3,8,14,48,128]{4,3,2,1,0:T(8,128)} copy-done((f32[3,8,14,48,128]{4,3,2,1,0:T(8,128)}, f32[3,8,14,48,128]{4,3,2,1,0:T(8,128)S(1)}, u32[]{:S(2)}) %copy-start) | copy-done | bytes 8257560
  132.1 1.7 copy-done.7
  133.8 1.6 copy-done.9
  135.4 1.6 copy-done.11
  137.1 1.7 copy-done.13
  141.0 2.6 %shard_map.64 = (f32[8,8,32,128]{3,2,1,0:T(8,128)S(1)}, f32[8,8,4,128]{3,2,1,0:T(4,128)S(1)}, f32[8,8,4,128]{3,2,1,0:T(4,128)S(1)}, f32[8,3,32,128]{3,2,1,0:T(8,...) custom-call(f32[8,8,32,128]{3,2,1,0:T(8,128)S(1)} %copy-done.21, f32[8,8,32,128]{3,2,1,0:T(8,128)} %all-to-all-done.1.fixed, ...), custom_call_target="tpu_custom_call" | custom-call | bytes 4194304 | tf_op jit(solution)/shard_map/pallas_call | solution.py:418
  144.5 3.6 %collective-permute-start.14 = (f32[8,8,4,128]{3,2,1,0:T(4,128)S(1)}, f32[8,8,4,128]{3,2,1,0:T(4,128)S(1)}, u32[]{:S(2)}, u32[]{:S(2)}) collective-permute-start(f32[8,8,4,128]{3,2,1,0:T(4,128)S(1)} %get-tuple-element.30), channel_id=1, source_target_pairs={{0,1},{1,2},{2,3},{3,4},{4,5},{5,6},{6,7},{8,9},{9,10},{10,11},{11... | collective-permute-start | bytes 393224 | tf_op jit(solution)/shard_map/ppermute | solution.py:30
  148.8 3.2 %collective-permute-done.18 = f32[8,128]{1,0:T(8,128)S(1)} collective-permute-done((f32[8,128]{1,0:T(8,128)S(1)}, f32[8,128]{1,0:T(8,128)S(1)}, u32[]{:S(2)}, u32[]{:S(2)}) %collective-permute-start.18) | collective-permute-done | bytes 4128 | tf_op jit(solution)/shard_map/ppermute | solution.py:351
  152.0 2.1 collective-permute-start.19
  155.6 2.9 %collective-permute-start.20 = (f32[8,128]{1,0:T(8,128)S(1)}, f32[8,128]{1,0:T(8,128)S(1)}, u32[]{:S(2)}, u32[]{:S(2)}) collective-permute-start(f32[8,128]{1,0:T(8,128)S(1)} %add.16), channel_id=1, source_target_pairs={{0,4},{1,5},{2,6},{3,7},{4,0},{5,1},{6,2},{7,3},{8,12},{9,13},{10,... | collective-permute-start | bytes 12296 | tf_op jit(solution)/shard_map/ppermute | solution.py:351
  161.4 2.4 %collective-permute-start.12 = (f32[8,3,32,128]{3,2,1,0:T(8,128)}, f32[8,3,32,128]{3,2,1,0:T(8,128)S(1)}, u32[]{:S(2)}, u32[]{:S(2)}) collective-permute-start(f32[8,3,32,128]{3,2,1,0:T(8,128)} %get-tuple-element.28), channel_id=1, source_target_pairs={{0,8},{8,16},{16,24},{1,9},{9,17},{17,25},{2,10},{10,18},{18,26},{... | collective-permute-start | bytes 1179656 | tf_op jit(solution)/shard_map/ppermute | solution.py:30
  165.2 3.4 %collective-permute-start.22 = (f32[8,128]{1,0:T(8,128)S(1)}, f32[8,128]{1,0:T(8,128)S(1)}, u32[]{:S(2)}, u32[]{:S(2)}) collective-permute-start(f32[8,128]{1,0:T(8,128)S(1)} %add.18), channel_id=1, source_target_pairs={{0,16},{8,24},{16,0},{24,8},{1,17},{9,25},{17,1},{25,9},{2,18},{10... | collective-permute-start | bytes 12296 | tf_op jit(solution)/shard_map/ppermute | solution.py:351
  168.7 1.8 collective-permute-start.16
  171.8 2.6 %collective-permute-done.22 = f32[8,128]{1,0:T(8,128)S(1)} collective-permute-done((f32[8,128]{1,0:T(8,128)S(1)}, f32[8,128]{1,0:T(8,128)S(1)}, u32[]{:S(2)}, u32[]{:S(2)}) %collective-permute-start.22) | collective-permute-done | bytes 4128 | tf_op jit(solution)/shard_map/ppermute | solution.py:351
  177.9 3.3 %copy-done.1 = f32[3,8,14,48,128]{4,3,2,1,0:T(8,128)S(1)} copy-done((f32[3,8,14,48,128]{4,3,2,1,0:T(8,128)S(1)}, f32[3,8,14,48,128]{4,3,2,1,0:T(8,128)}, u32[]{:S(2)}) %copy-start.1) | copy-done | bytes 8257560
  181.2 1.9 copy-done.6
  183.1 1.9 copy-done.8
  185.0 1.9 copy-done.10
  186.9 1.9 copy-done.12
  188.8 1.9 copy-done.14
  194.8 12.3 %shard_map.65 = f32[3,8,32,1024]{3,2,1,0:T(8,128)} custom-call(f32[4]{0:T(128)S(1)} %add_convert_fusion.flags, f32[8,8,32,128]{3,2,1,0:T(8,128)S(1)} %copy-done.17, f32[8,3,32,128]{3,2,1,0:T(8,128)S(1)} %copy-done.25, f32[8,3,32,128]{3,2,1,0:T(8,128)S(1)} %copy-done.27, f32[8,8,4,128]{3,2,1,0:T(4,128)S(1)} %collective-permute-done.14.before, ...), custom_call_target="tpu_custom_call" | custom-call | flops 20971520 | bytes 4194304 | tf_op jit(solution)/shard_map/pallas_call | solution.py:421
  (123 shorter events, 51.5 us)
Async XLA Ops:
  0.6 1.2 copy-start.18
  1.9 10.2 %copy-start.2 = (f32[3,8,32,1024]{3,2,1,0:T(8,128)S(1)}, f32[3,8,32,1024]{3,2,1,0:T(8,128)}, u32[]{:S(2)}) copy-start(f32[3,8,32,1024]{3,2,1,0:T(8,128)} %vel.1) | copy-start | bytes 9437188
  3.6 34.6 %all-to-all-start = ((f32[8,8,32,128]{3,2,1,0:T(8,128)}), f32[8,8,32,128]{3,2,1,0:T(8,128)}, u32[]{:S(2)}, u32[]{:S(2)}) async-start(f32[8,8,32,128]{3,2,1,0:T(8,128)} %copy-done.4), calls=%async_computation | async-start | bytes 2097152 | tf_op jit(solution)/shard_map/all_to_all | solution.py:321
  15.0 35.9 %collective-permute-start.8 = (f32[80,1024]{1,0:T(8,128)}, f32[80,1024]{1,0:T(8,128)S(1)}, u32[]{:S(2)}, u32[]{:S(2)}) collective-permute-start(f32[80,1024]{1,0:T(8,128)} %pad_maximum_fusion.2), channel_id=1, source_target_pairs={{0,1},{1,2},{2,3},{3,4},{4,5},{5,6},{6,7},{8,9},{9,10},{10,11},{11... | collective-permute-start | bytes 983048 | tf_op jit(solution)/shard_map/ppermute | solution.py:30
  22.5 34.3 %collective-permute-start.9 = (f32[80,1024]{1,0:T(8,128)}, f32[80,1024]{1,0:T(8,128)}, u32[]{:S(2)}, u32[]{:S(2)}) collective-permute-start(f32[80,1024]{1,0:T(8,128)} %pad_maximum_fusion.3), channel_id=1, source_target_pairs={{1,0},{2,1},{3,2},{4,3},{5,4},{6,5},{7,6},{9,8},{10,9},{11,10},{12... | collective-permute-start | bytes 983048 | tf_op jit(solution)/shard_map/ppermute | solution.py:31
  23.8 1.2 copy-start.19
  25.9 1.0 copy-start.3
  38.3 101.5 %all-to-all-start.1 = ((f32[8,8,32,128]{3,2,1,0:T(8,128)}), f32[8,8,32,128]{3,2,1,0:T(8,128)}, u32[]{:S(2)}, u32[]{:S(2)}) async-start(f32[8,8,32,128]{3,2,1,0:T(8,128)} %copy-done.3), calls=%async_computation.1 | async-start | bytes 2097152 | tf_op jit(solution)/shard_map/all_to_all | solution.py:321
  43.5 4.9 %copy-start.37 = (f32[3,3,32,1024]{3,2,1,0:T(8,128)S(1)}, f32[3,3,32,1024]{3,2,1,0:T(8,128)}, u32[]{:S(2)}) copy-start(f32[3,3,32,1024]{3,2,1,0:T(8,128)} %get-tuple-element.40) | copy-start | bytes 3538948
  46.1 60.6 %collective-permute-start.6 = (f32[10,32,1024]{2,1,0:T(8,128)}, f32[10,32,1024]{2,1,0:T(8,128)}, u32[]{:S(2)}, u32[]{:S(2)}) collective-permute-start(f32[10,32,1024]{2,1,0:T(8,128)} %pad_maximum_fusion), channel_id=1, source_target_pairs={{0,8},{8,16},{16,24},{1,9},{9,17},{17,25},{2,10},{10,18},{18,26},{... | collective-permute-start | bytes 3932168 | tf_op jit(solution)/shard_map/ppermute | solution.py:30
  49.6 58.4 %collective-permute-start.7 = (f32[10,32,1024]{2,1,0:T(8,128)}, f32[10,32,1024]{2,1,0:T(8,128)}, u32[]{:S(2)}, u32[]{:S(2)}) collective-permute-start(f32[10,32,1024]{2,1,0:T(8,128)} %pad_maximum_fusion.1), channel_id=1, source_target_pairs={{8,0},{16,8},{24,16},{9,1},{17,9},{25,17},{10,2},{18,10},{26,18},{... | collective-permute-start | bytes 3932168 | tf_op jit(solution)/shard_map/ppermute | solution.py:31
  68.1 15.1 %collective-permute-start.2 = (f32[8,8,4,128]{3,2,1,0:T(4,128)}, f32[8,8,4,128]{3,2,1,0:T(4,128)}, u32[]{:S(2)}, u32[]{:S(2)}) collective-permute-start(f32[8,8,4,128]{3,2,1,0:T(4,128)} %get-tuple-element.22), channel_id=1, source_target_pairs={{0,1},{1,2},{2,3},{3,4},{4,5},{5,6},{6,7},{8,9},{9,10},{10,11},{11... | collective-permute-start | bytes 393224 | tf_op jit(solution)/shard_map/ppermute | solution.py:30
  77.5 13.8 %collective-permute-start.10 = (f32[54,1024]{1,0:T(8,128)}, f32[54,1024]{1,0:T(8,128)S(1)}, u32[]{:S(2)}, u32[]{:S(2)}) collective-permute-start(f32[54,1024]{1,0:T(8,128)} %pad_maximum_fusion.4), channel_id=1, source_target_pairs={{0,8},{8,16},{16,24},{1,9},{9,17},{17,25},{2,10},{10,18},{18,26},{... | collective-permute-start | bytes 663560 | tf_op jit(solution)/shard_map/ppermute | solution.py:30
  81.9 7.4 %collective-permute-start.3 = (f32[8,8,4,128]{3,2,1,0:T(4,128)}, f32[8,8,4,128]{3,2,1,0:T(4,128)S(1)}, u32[]{:S(2)}, u32[]{:S(2)}) collective-permute-start(f32[8,8,4,128]{3,2,1,0:T(4,128)} %copy-done.36), channel_id=1, source_target_pairs={{1,0},{2,1},{3,2},{4,3},{5,4},{6,5},{7,6},{9,8},{10,9},{11,10},{12... | collective-permute-start | bytes 393224 | tf_op jit(solution)/shard_map/ppermute | solution.py:31
  83.2 35.4 %collective-permute-start = (f32[8,4,32,128]{3,2,1,0:T(8,128)}, f32[8,4,32,128]{3,2,1,0:T(8,128)}, u32[]{:S(2)}, u32[]{:S(2)}) collective-permute-start(f32[8,4,32,128]{3,2,1,0:T(8,128)} %copy-done.35), channel_id=1, source_target_pairs={{0,8},{8,16},{16,24},{1,9},{9,17},{17,25},{2,10},{10,18},{18,26},{... | collective-permute-start | bytes 1572872 | tf_op jit(solution)/shard_map/ppermute | solution.py:30
  89.4 29.3 %collective-permute-start.1 = (f32[8,4,32,128]{3,2,1,0:T(8,128)}, f32[8,4,32,128]{3,2,1,0:T(8,128)}, u32[]{:S(2)}, u32[]{:S(2)}) collective-permute-start(f32[8,4,32,128]{3,2,1,0:T(8,128)} %copy-done.34), channel_id=1, source_target_pairs={{8,0},{16,8},{24,16},{9,1},{17,9},{25,17},{10,2},{18,10},{26,18},{... | collective-permute-start | bytes 1572872 | tf_op jit(solution)/shard_map/ppermute | solution.py:31
  92.0 4.4 %collective-permute-start.11 = (f32[54,1024]{1,0:T(8,128)S(1)}, f32[54,1024]{1,0:T(8,128)S(1)}, u32[]{:S(2)}, u32[]{:S(2)}) collective-permute-start(f32[54,1024]{1,0:T(8,128)S(1)} %pad_maximum_fusion.5), channel_id=1, source_target_pairs={{8,0},{16,8},{24,16},{9,1},{17,9},{25,17},{10,2},{18,10},{26,18},{... | collective-permute-start | bytes 663560 | tf_op jit(solution)/shard_map/ppermute | solution.py:31
  97.1 21.5 %collective-permute-start.4 = (f32[8,4,8,128]{3,2,1,0:T(8,128)}, f32[8,4,8,128]{3,2,1,0:T(8,128)}, u32[]{:S(2)}, u32[]{:S(2)}) collective-permute-start(f32[8,4,8,128]{3,2,1,0:T(8,128)} %pad_maximum_fusion.6), channel_id=1, source_target_pairs={{0,8},{8,16},{16,24},{1,9},{9,17},{17,25},{2,10},{10,18},{18,26},{... | collective-permute-start | bytes 393224 | tf_op jit(solution)/shard_map/ppermute | solution.py:30
  106.6 12.0 %collective-permute-start.5 = (f32[8,4,8,128]{3,2,1,0:T(8,128)}, f32[8,4,8,128]{3,2,1,0:T(8,128)}, u32[]{:S(2)}, u32[]{:S(2)}) collective-permute-start(f32[8,4,8,128]{3,2,1,0:T(8,128)} %pad_maximum_fusion.7), channel_id=1, source_target_pairs={{8,0},{16,8},{24,16},{9,1},{17,9},{25,17},{10,2},{18,10},{26,18},{... | collective-permute-start | bytes 393224 | tf_op jit(solution)/shard_map/ppermute | solution.py:31
  108.0 1.2 copy-start.15
  111.1 7.5 %copy-start.23 = (f32[8,8,4,128]{3,2,1,0:T(4,128)S(1)}, f32[8,8,4,128]{3,2,1,0:T(4,128)}, u32[]{:S(2)}) copy-start(f32[8,8,4,128]{3,2,1,0:T(4,128)} %copy-done.22) | copy-start | bytes 393220
  117.0 1.6 copy-start.5
  128.9 3.3 %copy-start = (f32[3,8,14,48,128]{4,3,2,1,0:T(8,128)}, f32[3,8,14,48,128]{4,3,2,1,0:T(8,128)S(1)}, u32[]{:S(2)}) copy-start(f32[3,8,14,48,128]{4,3,2,1,0:T(8,128)S(1)} %get-tuple-element.24.vel) | copy-start | bytes 24772612
  132.1 1.7 copy-start.7
  133.8 1.6 copy-start.9
  135.4 1.6 copy-start.11
  137.1 1.7 copy-start.13
  139.7 1.2 copy-start.21
  143.5 1.0 copy-start.16
  144.5 24.0 %collective-permute-start.14 = (f32[8,8,4,128]{3,2,1,0:T(4,128)S(1)}, f32[8,8,4,128]{3,2,1,0:T(4,128)S(1)}, u32[]{:S(2)}, u32[]{:S(2)}) collective-permute-start(f32[8,8,4,128]{3,2,1,0:T(4,128)S(1)} %get-tuple-element.30), channel_id=1, source_target_pairs={{0,1},{1,2},{2,3},{3,4},{4,5},{5,6},{6,7},{8,9},{9,10},{10,11},{11... | collective-permute-start | bytes 393224 | tf_op jit(solution)/shard_map/ppermute | solution.py:30
  148.2 3.8 %collective-permute-start.18 = (f32[8,128]{1,0:T(8,128)S(1)}, f32[8,128]{1,0:T(8,128)S(1)}, u32[]{:S(2)}, u32[]{:S(2)}) collective-permute-start(f32[8,128]{1,0:T(8,128)S(1)} %get-tuple-element.37), channel_id=1, source_target_pairs={{0,1},{1,0},{2,3},{3,2},{4,5},{5,4},{6,7},{7,6},{8,9},{9,8},{10,11... | collective-permute-start | bytes 12296 | tf_op jit(solution)/shard_map/ppermute | solution.py:351
  152.0 3.7 %collective-permute-start.19 = (f32[8,128]{1,0:T(8,128)S(1)}, f32[8,128]{1,0:T(8,128)S(1)}, u32[]{:S(2)}, u32[]{:S(2)}) collective-permute-start(f32[8,128]{1,0:T(8,128)S(1)} %add.15), channel_id=1, source_target_pairs={{0,2},{1,3},{2,0},{3,1},{4,6},{5,7},{6,4},{7,5},{8,10},{9,11},{10,... | collective-permute-start | bytes 12296 | tf_op jit(solution)/shard_map/ppermute | solution.py:351
  155.6 4.5 %collective-permute-start.20 = (f32[8,128]{1,0:T(8,128)S(1)}, f32[8,128]{1,0:T(8,128)S(1)}, u32[]{:S(2)}, u32[]{:S(2)}) collective-permute-start(f32[8,128]{1,0:T(8,128)S(1)} %add.16), channel_id=1, source_target_pairs={{0,4},{1,5},{2,6},{3,7},{4,0},{5,1},{6,2},{7,3},{8,12},{9,13},{10,... | collective-permute-start | bytes 12296 | tf_op jit(solution)/shard_map/ppermute | solution.py:351
  160.1 5.0 %collective-permute-start.21 = (f32[8,128]{1,0:T(8,128)S(1)}, f32[8,128]{1,0:T(8,128)S(1)}, u32[]{:S(2)}, u32[]{:S(2)}) collective-permute-start(f32[8,128]{1,0:T(8,128)S(1)} %add.17), channel_id=1, source_target_pairs={{0,8},{8,0},{16,24},{24,16},{1,9},{9,1},{17,25},{25,17},{2,10},{10... | collective-permute-start | bytes 12296 | tf_op jit(solution)/shard_map/ppermute | solution.py:351
  160.1 8.5 %collective-permute-start.15 = (f32[8,8,4,128]{3,2,1,0:T(4,128)S(1)}, f32[8,8,4,128]{3,2,1,0:T(4,128)S(1)}, u32[]{:S(2)}, u32[]{:S(2)}) collective-permute-start(f32[8,8,4,128]{3,2,1,0:T(4,128)S(1)} %get-tuple-element.31), channel_id=1, source_target_pairs={{1,0},{2,1},{3,2},{4,3},{5,4},{6,5},{7,6},{9,8},{10,9},{11,10},{12... | collective-permute-start | bytes 393224 | tf_op jit(solution)/shard_map/ppermute | solution.py:31
  161.4 14.9 %collective-permute-start.12 = (f32[8,3,32,128]{3,2,1,0:T(8,128)}, f32[8,3,32,128]{3,2,1,0:T(8,128)S(1)}, u32[]{:S(2)}, u32[]{:S(2)}) collective-permute-start(f32[8,3,32,128]{3,2,1,0:T(8,128)} %get-tuple-element.28), channel_id=1, source_target_pairs={{0,8},{8,16},{16,24},{1,9},{9,17},{17,25},{2,10},{10,18},{18,26},{... | collective-permute-start | bytes 1179656 | tf_op jit(solution)/shard_map/ppermute | solution.py:30
  163.9 13.2 %collective-permute-start.13 = (f32[8,3,32,128]{3,2,1,0:T(8,128)}, f32[8,3,32,128]{3,2,1,0:T(8,128)S(1)}, u32[]{:S(2)}, u32[]{:S(2)}) collective-permute-start(f32[8,3,32,128]{3,2,1,0:T(8,128)} %get-tuple-element.29), channel_id=1, source_target_pairs={{8,0},{16,8},{24,16},{9,1},{17,9},{25,17},{10,2},{18,10},{26,18},{... | collective-permute-start | bytes 1179656 | tf_op jit(solution)/shard_map/ppermute | solution.py:31
  165.2 9.2 %collective-permute-start.22 = (f32[8,128]{1,0:T(8,128)S(1)}, f32[8,128]{1,0:T(8,128)S(1)}, u32[]{:S(2)}, u32[]{:S(2)}) collective-permute-start(f32[8,128]{1,0:T(8,128)S(1)} %add.18), channel_id=1, source_target_pairs={{0,16},{8,24},{16,0},{24,8},{1,17},{9,25},{17,1},{25,9},{2,18},{10... | collective-permute-start | bytes 12296 | tf_op jit(solution)/shard_map/ppermute | solution.py:351
  168.7 7.0 %collective-permute-start.16 = (f32[8,3,8,128]{3,2,1,0:T(8,128)S(1)}, f32[8,3,8,128]{3,2,1,0:T(8,128)S(1)}, u32[]{:S(2)}, u32[]{:S(2)}) collective-permute-start(f32[8,3,8,128]{3,2,1,0:T(8,128)S(1)} %pad_maximum_fusion.8), channel_id=1, source_target_pairs={{0,8},{8,16},{16,24},{1,9},{9,17},{17,25},{2,10},{10,18},{18,26},{... | collective-permute-start | bytes 294920 | tf_op jit(solution)/shard_map/ppermute | solution.py:30
  170.5 5.2 %collective-permute-start.17 = (f32[8,3,8,128]{3,2,1,0:T(8,128)S(1)}, f32[8,3,8,128]{3,2,1,0:T(8,128)S(1)}, u32[]{:S(2)}, u32[]{:S(2)}) collective-permute-start(f32[8,3,8,128]{3,2,1,0:T(8,128)S(1)} %pad_maximum_fusion.9), channel_id=1, source_target_pairs={{8,0},{16,8},{24,16},{9,1},{17,9},{25,17},{10,2},{18,10},{26,18},{... | collective-permute-start | bytes 294920 | tf_op jit(solution)/shard_map/ppermute | solution.py:31
  177.9 3.3 %copy-start.1 = (f32[3,8,14,48,128]{4,3,2,1,0:T(8,128)S(1)}, f32[3,8,14,48,128]{4,3,2,1,0:T(8,128)}, u32[]{:S(2)}) copy-start(f32[3,8,14,48,128]{4,3,2,1,0:T(8,128)} %copy-done) | copy-start | bytes 24772612
  181.2 1.9 copy-start.6
  183.1 1.9 copy-start.8
  185.0 1.9 copy-start.10
  186.9 1.9 copy-start.12
  188.8 1.9 copy-start.14
  190.7 1.2 copy-start.17
  191.9 1.0 copy-start.25
  (15 other events, 12.2 us)

commit v2 on v1

--- a/solution.py
+++ b/solution.py
@@ -46,7 +46,7 @@
     return edges(tiles, tiles)
 
 
-def fill(out, own, below, above, before, after, corners_below, corners_above, width):
+def fill(out, own, below, above, before, after, width):
     blocks, sections, rows, _ = own.shape
     top, bottom = pl.ds(GAP - SENT, SENT), pl.ds(GAP + rows, SENT)
 
@@ -58,11 +58,11 @@
         return 0
 
     def halo(z, _):
-        for planes, corners, at in ((below, corners_below, z), (above, corners_above, z + width + sections)):
+        for planes, at in ((below, z), (above, z + width + sections)):
             for i in range(blocks):
-                out[i, at, pl.ds(GAP, rows), :] = planes[i, z, :, :]
-                out[i, at, top, :] = corners[i, z, pl.ds(0, SENT), :]
-                out[i, at, bottom, :] = corners[i, z, pl.ds(SENT, SENT), :]
+                out[i, at, pl.ds(GAP, rows), :] = planes[i, z, pl.ds(0, rows), :]
+                out[i, at, top, :] = planes[i, z, pl.ds(rows, SENT), :]
+                out[i, at, bottom, :] = planes[i, z, pl.ds(rows + SENT, SENT), :]
         return 0
 
     lax.fori_loop(0, sections, whole, 0)
@@ -83,27 +83,35 @@
     lax.fori_loop(0, sections, section, 0)
 
 
-def part_kernel(field, low_rows, high_rows, low, high):
+def end_kernel(field, gate, low_rows, high_rows):
+    del gate
     blocks, sections, rows, _ = field.shape
-    width = low.shape[1]
-
-    def row_ends(z, _):
+
+    def section(z, _):
         for i in range(blocks):
             low_rows[i, z, :, :] = field[i, z, pl.ds(0, SENT), :]
             high_rows[i, z, :, :] = field[i, z, pl.ds(rows - SENT, SENT), :]
         return 0
 
-    def planes(z, _):
-        for i in range(blocks):
-            low[i, z, :, :] = field[i, z, :, :]
-            high[i, z, :, :] = field[i, z + sections - width, :, :]
-        return 0
-
-    lax.fori_loop(0, sections, row_ends, 0)
-    lax.fori_loop(0, width, planes, 0)
-
-
-def misfit_kernel(moved, fixed, sums, misfit, low_rows, high_rows, low, high, total_ref):
+    lax.fori_loop(0, sections, section, 0)
+
+
+def plane_kernel(field, before, after, low, high):
+    blocks, sections, rows, _ = field.shape
+    width = low.shape[1]
+
+    def plane(z, _):
+        for out, at in ((low, z), (high, z + sections - width)):
+            for i in range(blocks):
+                out[i, z, pl.ds(0, rows), :] = field[i, at, :, :]
+                out[i, z, pl.ds(rows, SENT), :] = before[i, at, :, :]
+                out[i, z, pl.ds(rows + SENT, SENT), :] = after[i, at, :, :]
+        return 0
+
+    lax.fori_loop(0, width, plane, 0)
+
+
+def misfit_kernel(moved, fixed, sums, misfit, low_rows, high_rows, total_ref):
     blocks, sections, rows, _ = moved.shape
 
     def section(z, acc):
@@ -112,11 +120,47 @@
                 value = moved[i, z, pl.ds(r, TILE), :] - fixed[i, z, pl.ds(r, TILE), :]
                 misfit[i, z, pl.ds(r, TILE), :] = value
                 acc = acc + value * value
+                if r == 0:
+                    low_rows[i, z, :, :] = value[:SENT]
+                if r == rows - TILE:
+                    high_rows[i, z, :, :] = value[TILE - SENT :]
         return acc
 
     zero = jnp.zeros((TILE, LANES), jnp.float32)
     total_ref[...] = 0.5 * (lax.fori_loop(0, sections, section, zero) + sums[...])
-    part_kernel(misfit, low_rows, high_rows, low, high)
+
+
+def pack_kernel(vel, sti, low_rows, high_rows, low, high):
+    _, sections, rows, _ = vel.shape
+    for c in range(3):
+        for z in range(sections):
+            at = pl.ds((c * sections + z) * WIDE, WIDE)
+            low_rows[at, :] = vel[c, z, pl.ds(0, WIDE), :]
+            high_rows[at, :] = vel[c, z, pl.ds(rows - WIDE, WIDE), :]
+    for z in range(sections):
+        at = pl.ds(3 * sections * WIDE + z, 1)
+        low_rows[at, :] = sti[z, pl.ds(0, 1), :]
+        high_rows[at, :] = sti[z, pl.ds(rows - 1, 1), :]
+
+    def plane(z, _):
+        for c in range(3):
+            low[c * WIDE + z, :, :] = vel[c, z, :, :]
+            high[c * WIDE + z, :, :] = vel[c, sections - WIDE + z, :, :]
+        return 0
+
+    lax.fori_loop(0, WIDE, plane, 0)
+    low[3 * WIDE, :, :] = sti[0, :, :]
+    high[3 * WIDE, :, :] = sti[sections - 1, :, :]
+
+
+def corner_kernel(before, after, low, high):
+    size = WIDE * WIDE
+    sections = before.shape[0] // (3 * WIDE + 1)
+    for c in range(3):
+        for half, src in enumerate((before, after)):
+            to = pl.ds((half * 3 + c) * size, size)
+            low[to, :] = src[pl.ds(c * sections * WIDE, size), :]
+            high[to, :] = src[pl.ds((c + 1) * sections * WIDE - size, size), :]
 
 
 def groups(rows, reach):
@@ -139,14 +183,30 @@
     return SELF * factor, WEIGHT * factor
 
 
-def forward_kernel(flags, own, below, above, before, after, low_corners, high_corners, vel, moved_ref, *levels):
+def forward_kernel(flags, own, below, above, before, after, ext, moved_ref, kept, *scratch):
+    levels, vel, vel_sem, kept_sem = scratch[:STEPS], scratch[STEPS], scratch[STEPS + 1], scratch[STEPS + 2]
     blocks, sections, rows, _ = own.shape
-    fill(levels[0], own, below, above, before, after, low_corners, high_corners, STEPS)
+
+    def load(z):
+        return pltpu.make_async_copy(ext.at[:, :, z], vel.at[:, :, z], vel_sem.at[z])
+
+    for z in range(sections + 2 * WIDE):
+        load(z).start()
+    fill(levels[0], own, below, above, before, after, STEPS)
+    copies = []
     for step in range(STEPS):
         src = levels[step]
+        copies.append(
+            pltpu.make_async_copy(
+                src.at[:, pl.ds(STEPS - 1, sections + 2)], kept.at[step], kept_sem.at[step]
+            )
+        )
+        copies[-1].start()
         reach = STEPS - 1 - step
 
         def plane(z, _, src=src, step=step, reach=reach):
+            if step == 0:
+                load(z - 1).wait()
             keep, weight = weights(flags, z, STEPS, STEPS + sections)
             for r in groups(rows, reach):
                 here = pl.ds(r, TILE)
@@ -167,17 +227,37 @@
             return 0
 
         lax.fori_loop(STEPS - reach, STEPS + sections + reach, plane, 0)
-
-
-def adjoint_kernel(flags, own, below, above, before, after, low_corners, high_corners, vel, *refs):
-    kept, reg, grad_ref, levels = refs[:STEPS], refs[STEPS], refs[STEPS + 1], refs[STEPS + 2 :]
+    for copy in copies:
+        copy.wait()
+
+
+def adjoint_kernel(flags, own, below, above, before, after, ext, kept_all, reg_all, grad_all, *scratch):
+    levels, (vel, kept, reg, grad_ref, vel_sem, kept_sem, reg_sem, grad_sem) = scratch[:STEPS], scratch[STEPS:]
     blocks, sections, rows, _ = own.shape
-    fill(levels[0], own, below, above, before, after, low_corners, high_corners, WIDE)
+
+    def load(z):
+        return pltpu.make_async_copy(ext.at[:, :, z], vel.at[:, :, z], vel_sem.at[z])
+
+    def save(z):
+        return pltpu.make_async_copy(grad_ref.at[:, z], grad_all.at[:, z], grad_sem.at[z])
+
+    later = [
+        pltpu.make_async_copy(kept_all.at[k], kept.at[k], kept_sem.at[k]) for k in range(STEPS)
+    ] + [pltpu.make_async_copy(reg_all, reg, reg_sem.at[0])]
+    for z in range(sections + 2 * WIDE):
+        load(z).start()
+    for copy in later:
+        copy.start()
+    fill(levels[0], own, below, above, before, after, WIDE)
+    load(0).wait()
+    load(1).wait()
     for step in range(WIDE):
         src, out = levels[step], levels[step + 1]
         reach = WIDE - 1 - step
 
         def plane(z, _, src=src, out=out, reach=reach):
+            if reach == WIDE - 1:
+                load(z + 1).wait()
             keep, weight = weights(flags, z, WIDE, WIDE + sections)
             for r in groups(rows, reach):
                 here, up, down = pl.ds(r, TILE), pl.ds(r + 1, TILE), pl.ds(r - 1, TILE)
@@ -202,6 +282,9 @@
 
         lax.fori_loop(WIDE - reach, WIDE + sections + reach, plane, 0)
 
+    for copy in later:
+        copy.wait()
+
     def slope(z, _):
         for r in groups(rows, 0):
             here, up, down = pl.ds(r, TILE), pl.ds(r + 1, TILE), pl.ds(r - 1, TILE)
@@ -209,11 +292,11 @@
             sums = [[None] * 3 for _ in range(blocks)]
             for k in range(STEPS):
                 adj = [levels[STEPS - 1 - k][i, z + WIDE, here, :] for i in range(blocks)]
-                plus, minus = edges_of([kept[k][i, z + STEPS, here, :] for i in range(blocks)])
+                plus, minus = edges_of([kept[k, i, z + 1, here, :] for i in range(blocks)])
                 for i in range(blocks):
                     parts = (
-                        adj[i] * (kept[k][i, z + STEPS + 1, here, :] - kept[k][i, z + STEPS - 1, here, :]),
-                        adj[i] * (kept[k][i, z + STEPS, up, :] - kept[k][i, z + STEPS, down, :]),
+                        adj[i] * (kept[k, i, z + 2, here, :] - kept[k, i, z, here, :]),
+                        adj[i] * (kept[k, i, z + 1, up, :] - kept[k, i, z + 1, down, :]),
                         adj[i] * (plus[i] - minus[i]),
                     )
                     for a in range(3):
@@ -222,28 +305,31 @@
                 lanes = pl.ds(i * LANES, LANES)
                 for a in range(3):
                     grad_ref[a, z, at, lanes] = reg[a, z, at, lanes] - (0.5 * DT) * sums[i][a]
+        save(z).start()
         return 0
 
     lax.fori_loop(0, sections, slope, 0)
-
-
-def regular_kernel(vel, sti, planes_below, planes_above, before, after, corners_below, corners_above,
-                   ext_ref, reg_ref, sum_ref, sti_ext):
-    _, sections, rows, width = vel.shape
-    blocks = width // LANES
-
-    def lay(out, src, z):
-        for i in range(blocks):
-            out[i, z, pl.ds(GAP, rows), :] = src[:, pl.ds(i * LANES, LANES)]
-
-    def lay_rows(out, z, row, src, at, count):
-        for i in range(blocks):
-            out[i, z, pl.ds(row, count), :] = src[pl.ds(at, count), pl.ds(i * LANES, LANES)]
+    for z in range(sections):
+        save(z).wait()
+
+
+def lay(out, src, z):
+    rows, width = src.shape
+    for i in range(width // LANES):
+        out[i, z, pl.ds(GAP, rows), :] = src[:, pl.ds(i * LANES, LANES)]
+
+
+def lay_rows(out, z, row, src, at, count):
+    for i in range(src.shape[1] // LANES):
+        out[i, z, pl.ds(row, count), :] = src[pl.ds(at, count), pl.ds(i * LANES, LANES)]
+
+
+def extend_kernel(vel, planes_below, planes_above, before, after, corners_below, corners_above, ext_ref):
+    _, sections, rows, _ = vel.shape
 
     def mid(z, _):
         for c in range(3):
             lay(ext_ref.at[c], vel.at[c, z], z + WIDE)
-        lay(sti_ext, sti.at[z], z + 1)
         return 0
 
     def far(z, _):
@@ -254,8 +340,6 @@
 
     lax.fori_loop(0, sections, mid, 0)
     lax.fori_loop(0, WIDE, far, 0)
-    lay(sti_ext, planes_below.at[3 * WIDE], 0)
-    lay(sti_ext, planes_above.at[3 * WIDE], sections + 1)
     low, high = GAP - WIDE, GAP + rows
     for c in range(3):
         for z in range(sections):
@@ -267,6 +351,20 @@
             for src, z_out in ((corners_below, z), (corners_above, z + WIDE + sections)):
                 lay_rows(ext_ref.at[c], z_out, low, src, at, WIDE)
                 lay_rows(ext_ref.at[c], z_out, high, src, at + half, WIDE)
+
+
+def regular_kernel(gate, ext_ref, sti, planes_below, planes_above, before, after, reg_ref, sum_ref, sti_ext):
+    del gate
+    sections, rows, width = sti.shape
+    blocks = width // LANES
+
+    def mid(z, _):
+        lay(sti_ext, sti.at[z], z + 1)
+        return 0
+
+    lax.fori_loop(0, sections, mid, 0)
+    lay(sti_ext, planes_below.at[3 * WIDE], 0)
+    lay(sti_ext, planes_above.at[3 * WIDE], sections + 1)
     for z in range(sections):
         at = 3 * sections * WIDE + z
         lay_rows(sti_ext, z + 1, GAP - 1, before, at, 1)
@@ -309,36 +407,44 @@
     sum_ref[...] = acc
 
 
-def to_rows(scan):
+def after(value, *gates):
+    def kernel(*refs):
+        del refs
+
+    return pl.pallas_call(
+        kernel,
+        out_shape=jax.ShapeDtypeStruct(value.shape, value.dtype),
+        in_specs=[ANY] * (1 + len(gates)),
+        out_specs=ANY,
+        input_output_aliases={0: 0},
+    )(value, *gates)
+
+
+def to_blocks(scan):
     count = lax.axis_size("row")
     sections, width, rows = scan.shape
     own = rows // count
-    shape = (count, sections, own, width)
     if width == LANES and rows % width == 0 and width % own == 0:
-        (parts,) = call(block_kernel, [shape], [VMEM], [])(scan)
-    else:
-        parts = jnp.swapaxes(scan, 1, 2).reshape(sections, count, own, width).transpose(1, 0, 2, 3)
+        return call(block_kernel, [(count, sections, own, width)], [VMEM])(scan)[0]
+    return jnp.swapaxes(scan, 1, 2).reshape(sections, count, own, width).transpose(1, 0, 2, 3)
+
+
+def to_rows(parts):
     parts = lax.all_to_all(parts, "row", split_axis=0, concat_axis=0, tiled=True)
+    count, sections, own, width = parts.shape
     if width == LANES:
         return parts
     whole = parts.transpose(1, 2, 0, 3).reshape(sections, own, count * width // LANES, LANES)
     return whole.transpose(2, 0, 1, 3)
 
 
-def part_shapes(shape, width):
-    blocks, sections, rows, _ = shape
-    return [(blocks, sections, SENT, LANES)] * 2 + [(blocks, width, rows, LANES)] * 2
-
-
-def halos(low_rows, high_rows, low, high):
-    width = low.shape[1]
-    before, after = exchange(low_rows, high_rows, "row")
-    below, above = exchange(low, high, "sec")
-    corners = [
-        jnp.concatenate([before[:, cut], after[:, cut]], axis=2)
-        for cut in (slice(0, width), slice(before.shape[1] - width, None))
-    ]
-    return (below, above, before, after) + exchange(*corners, "sec")
+def halos(field, width, low_rows, high_rows):
+    blocks, _, rows, _ = field.shape
+    before, after_ = exchange(low_rows, high_rows, "row")
+    low, high = call(plane_kernel, [(blocks, width, rows + 2 * SENT, LANES)] * 2, [VMEM] * 3)(
+        field, before, after_
+    )
+    return exchange(low, high, "sec") + (before, after_)
 
 
 def everywhere(part):
@@ -353,14 +459,17 @@
     return part
 
 
-def call(kernel, shapes, ins, scratch, flops=0, megabytes=20):
+def call(kernel, shapes, ins, scratch=(), outs=None, flops=0):
     return pl.pallas_call(
         kernel,
         out_shape=[jax.ShapeDtypeStruct(shape, jnp.float32) for shape in shapes],
         in_specs=ins,
-        out_specs=[VMEM] * len(shapes),
-        scratch_shapes=[pltpu.VMEM(shape, jnp.float32) for shape in scratch],
-        compiler_params=pltpu.CompilerParams(vmem_limit_bytes=megabytes << 20),
+        out_specs=outs or [VMEM] * len(shapes),
+        scratch_shapes=[
+            pltpu.VMEM(shape, jnp.float32) if isinstance(shape, tuple) else pltpu.SemaphoreType.DMA((shape,))
+            for shape in scratch
+        ],
+        compiler_params=pltpu.CompilerParams(vmem_limit_bytes=63 << 20),
         cost_estimate=pl.CostEstimate(flops=flops, bytes_accessed=4 << 20, transcendentals=0),
     )
 
@@ -370,64 +479,62 @@
     blocks = width // LANES
     tall, deep = rows + 2 * GAP, sections + 2 * WIDE
     own = (blocks, sections, rows, LANES)
+    ends = (blocks, sections, SENT, LANES)
     sec, row = lax.axis_index("sec"), lax.axis_index("row")
     flags = jnp.stack([
         sec > 0, sec < lax.axis_size("sec") - 1, row > 0, row < lax.axis_size("row") - 1
     ]).astype(jnp.float32)
 
-    template = to_rows(template_scan)
-
-    sides = [
-        jnp.concatenate([velocity[:, :, cut].reshape(-1, width), stiffness[:, one]], axis=0)
-        for cut, one in ((slice(0, WIDE), 0), (slice(rows - WIDE, rows), rows - 1))
-    ]
-    before, after = exchange(sides[0], sides[1], "row")
-    planes = [
-        jnp.concatenate([velocity[:, cut].reshape(-1, rows, width), stiffness[one]], axis=0)
-        for cut, one in (
-            (slice(0, WIDE), slice(0, 1)), (slice(sections - WIDE, sections), slice(sections - 1, sections))
-        )
-    ]
-    below, above = exchange(planes[0], planes[1], "sec")
-    corners = [
-        jnp.concatenate([
-            side[: 3 * sections * WIDE].reshape(3, sections, WIDE, width)[:, cut].reshape(-1, width)
-            for side in (before, after)
-        ], axis=0)
-        for cut in (slice(0, WIDE), slice(sections - WIDE, sections))
-    ]
-    corners_below, corners_above = exchange(corners[0], corners[1], "sec")
-    extended, reg, reg_sums = call(
+    template = to_rows(to_blocks(template_scan))
+
+    lines = (3 * WIDE + 1) * sections
+    low_rows, high_rows, low, high = call(
+        pack_kernel, [(lines, width)] * 2 + [(3 * WIDE + 1, rows, width)] * 2, [VMEM] * 2
+    )(velocity, stiffness)
+    before, after_ = exchange(low_rows, high_rows, "row")
+    below, above = exchange(low, high, "sec")
+    corners = call(corner_kernel, [(6 * WIDE * WIDE, width)] * 2, [VMEM] * 2)(before, after_)
+    (extended,) = call(extend_kernel, [(3, blocks, deep, tall, LANES)], [VMEM] * 7)(
+        velocity, below, above, before, after_, *exchange(*corners, "sec")
+    )
+
+    parts = call(end_kernel, [ends] * 2, [VMEM, ANY])(template, extended)
+    fixed = to_rows(after(to_blocks(reference_scan), parts[0]))
+    level = (blocks, sections + 2 * STEPS, tall, LANES)
+    moved, kept = call(
+        forward_kernel,
+        [own, (STEPS, blocks, sections + 2, tall, LANES)],
+        [SMEM] + [VMEM] * 5 + [ANY],
+        [level] * STEPS + [(3, blocks, deep, tall, LANES), deep, STEPS],
+        [VMEM, ANY],
+        20 << 20,
+    )(flags, template, *halos(template, STEPS, *parts), extended)
+
+    reg, reg_sums = call(
         regular_kernel,
-        [(3, blocks, deep, tall, LANES), velocity.shape, (TILE, LANES)],
-        [VMEM] * 8,
+        [velocity.shape, (TILE, LANES)],
+        [ANY] + [VMEM] * 6,
         [(blocks, sections + 2, tall, LANES)],
-        20 << 20,
-    )(velocity, stiffness, below, above, before, after, corners_below, corners_above)
-
-    parts = call(part_kernel, part_shapes(own, STEPS), [VMEM], [])(template)
-    moved, *levels = call(
-        forward_kernel,
-        [own] + [(blocks, sections + 2 * STEPS, tall, LANES)] * STEPS,
-        [SMEM] + [VMEM] * 8,
-        [],
-        20 << 20,
-    )(flags, template, *halos(*parts), extended)
-
-    fixed = to_rows(reference_scan)
-    misfit, *parts, partial = call(
-        misfit_kernel, [own] + part_shapes(own, WIDE) + [(TILE, LANES)], [VMEM] * 3, []
-    )(moved, fixed, reg_sums)
+        flops=20 << 20,
+    )(moved, extended, stiffness, below, above, before, after_)
+
+    misfit, *parts, partial = call(misfit_kernel, [own, ends, ends, (TILE, LANES)], [VMEM] * 3)(
+        moved, fixed, reg_sums
+    )
+    around = halos(misfit, WIDE, *parts)
     (gradient,) = call(
         adjoint_kernel,
         [velocity.shape],
-        [SMEM] + [VMEM] * (9 + STEPS),
-        [(blocks, deep, tall, LANES)] * STEPS,
+        [SMEM] + [VMEM] * 5 + [ANY] * 3,
+        [(blocks, deep, tall, LANES)] * STEPS
+        + [(3, blocks, deep, tall, LANES), (STEPS, blocks, sections + 2, tall, LANES)]
+        + [velocity.shape] * 2 + [deep, STEPS, 1, sections],
+        [ANY],
         20 << 20,
-    )(flags, misfit, *halos(*parts), extended, *levels, reg)
+    )(flags, misfit, *around, extended, kept, reg)
 
     voxels = sections * rows * width * lax.axis_size("sec") * lax.axis_size("row")
-    objective = jnp.sum(everywhere(partial)) / voxels
+    objective = jnp.sum(everywhere(after(partial, around[2], around[3]))) / voxels
     return (gradient, objective)
 
 

time: 212 us -> 195 us (0.920); the launches traced: 208 us -> 194 us
  local copies, waits for them, and re-layouts: 70.5 us -> 4.34 us
  Pallas kernels: 34.5 us -> 66.3 us
  waiting for transfers between devices: 20.9 us -> 39.8 us
  starting transfers between devices: 68.4 us -> 79.2 us
  other arithmetic: 11 us -> 1.95 us
    unnamed x78 -> x26, local copies, waits for them, and re-layouts: 45.6 us -> 4.34 us
    pallas_call x7 -> x14, Pallas kernels: 34.5 us -> 66.3 us  [the longest x1 15 us: local(): call(adjoint_kernel, [velocity.shape], [SMEM] + [VMEM] * 5 + [ANY] * 3, [...]
    ppermute x9 -> x7, waiting for transfers between devices: 0.02 us -> 19.9 us  [exchange(): lax.ppermute(high_part, axis, [(i, i + 1) for i in range(count - 1)])]
    reshape x8 -> x0, local copies, waits for them, and re-layouts: 13.2 us -> none  [the longest x6 10.2 us: local(): side[:3 * sections * WIDE].reshape(3, sections, WIDE, width)[:, cut]]
    slice x12 -> x0, local copies, waits for them, and re-layouts: 11.8 us -> none  [the longest x4 5.98 us: local(): side[:3 * sections * WIDE].reshape(3, sections, WIDE, width)[:, cut]]
    concatenate x10 -> x0, other arithmetic: 10.3 us -> none  [the longest x2 3.73 us: local(): jnp.concatenate([velocity[:, cut].reshape(-1, rows, width), stiffness[one...]
    all_to_all x2, waiting for transfers between devices: 9.68 us -> 0.01 us  [to_rows(): lax.all_to_all(parts, 'row', split_axis=0, concat_axis=0, tiled=True)]
    ppermute x9 -> x7, waiting for transfers between devices: 2.3 us -> 11.2 us  [exchange(): above = lax.ppermute(low_part, axis, [(i + 1, i) for i in range(count - 1)])]
  transfers between devices with their start and end apart: 25 -> 21, of which waited for: 8 -> 12; matrix products, arithmetic and copies ran while one was open for 17% -> 1% of each run, Pallas kernels for 9% -> 21%
where the time goes in v2:
time: 195 us; the launch traced here: 194 us
  starting transfers between devices  79.2 us (41%)
  Pallas kernels  66.3 us (34%)
  waiting for transfers between devices  39.8 us (20%)
  local copies, waits for them, and re-layouts  4.34 us (2%)
  between operations  2.63 us (1%)
  other arithmetic  1.95 us (1%)
    ppermute x7, starting transfers between devices, exchange(): lax.ppermute(high_part, axis, [(i, i + 1) for i in range(count - 1)])  37.1 us
    ppermute x7, waiting for transfers between devices, exchange(): lax.ppermute(high_part, axis, [(i, i + 1) for i in range(count - 1)])  19.9 us
    all_to_all x2, starting transfers between devices, to_rows(): lax.all_to_all(parts, 'row', split_axis=0, concat_axis=0, tiled=True)  18.5 us
    pallas_call x1, Pallas kernels, local(): call(adjoint_kernel, [velocity.shape], [SMEM] + [VMEM] * 5 + [ANY] * 3, [...  15 us
    ppermute x5, starting transfers between devices, everywhere(): lax.ppermute(part, axis, [(i, i ^ near) for i in range(count)])  14.6 us
    pallas_call x1, Pallas kernels, local(): call(forward_kernel, [own, (STEPS, blocks, sections + 2, tall, LANES)], [...  12.9 us
    ppermute x7, waiting for transfers between devices, exchange(): above = lax.ppermute(low_part, axis, [(i + 1, i) for i in range(count - 1)])  11.2 us
    pallas_call x1, Pallas kernels, local(): call(regular_kernel, [velocity.shape, (TILE, LANES)], [ANY] + [VMEM] * 6,...  9.56 us
  transfers between devices with their start and end apart: 21, of which 12 were waited for; matrix products, arithmetic and copies ran while one was open for 1% of the time, Pallas kernels for 21%

profile of v2, /device:TPU:0, one launch (start us, length us, event | category | flops | bytes accessed | tf_op | source)
XLA Modules:
  0.0 194.2 jit_solution(6724983990605903527)
XLA Ops:
  0.6 3.0 %shard_map.59 = f32[8,8,32,128]{3,2,1,0:T(8,128)} custom-call(f32[8,128,256]{2,1,0:T(8,128)} %scan.2), custom_call_target="tpu_custom_call" | custom-call | bytes 4194304 | tf_op jit(solution)/shard_map/pallas_call | solution.py:428
  3.7 7.3 %all-to-all-start = ((f32[8,8,32,128]{3,2,1,0:T(8,128)}), f32[8,8,32,128]{3,2,1,0:T(8,128)}, u32[]{:S(2)}, u32[]{:S(2)}) async-start(f32[8,8,32,128]{3,2,1,0:T(8,128)} %shard_map.59), calls=%async_computation | async-start | bytes 2097152 | tf_op jit(solution)/shard_map/all_to_all | solution.py:433
  11.0 4.3 %shard_map.60 = (f32[80,1024]{1,0:T(8,128)}, f32[80,1024]{1,0:T(8,128)}, f32[10,32,1024]{2,1,0:T(8,128)}, f32[10,32,1024]{2,1,0:T(8,128)}) custom-call(f32[3,8,32,1024]{3,2,1,0:T(8,128)} %vel.3, f32[8,32,1024]{2,1,0:T(8,128)} %sti.3), custom_call_target="tpu_custom_call" | custom-call | bytes 4194304 | tf_op jit(solution)/shard_map/pallas_call | solution.py:491
  15.2 2.5 %collective-permute-start = (f32[10,32,1024]{2,1,0:T(8,128)}, f32[10,32,1024]{2,1,0:T(8,128)}, u32[]{:S(2)}, u32[]{:S(2)}) collective-permute-start(f32[10,32,1024]{2,1,0:T(8,128)} %get-tuple-element.22), channel_id=1, source_target_pairs={{0,8},{8,16},{16,24},{1,9},{9,17},{17,25},{2,10},{10,18},{18,26},{... | collective-permute-start | bytes 3932168 | tf_op jit(solution)/shard_map/ppermute | solution.py:30
  17.8 1.3 collective-permute-start.1
  19.0 3.8 %collective-permute-start.2 = (f32[80,1024]{1,0:T(8,128)}, f32[80,1024]{1,0:T(8,128)S(1)}, u32[]{:S(2)}, u32[]{:S(2)}) collective-permute-start(f32[80,1024]{1,0:T(8,128)} %get-tuple-element.24), channel_id=1, source_target_pairs={{0,1},{1,2},{2,3},{3,4},{4,5},{5,6},{6,7},{8,9},{9,10},{10,11},{11... | collective-permute-start | bytes 983048 | tf_op jit(solution)/shard_map/ppermute | solution.py:30
  22.8 1.3 collective-permute-start.3
  24.1 10.9 %collective-permute-done.2.before = f32[80,1024]{1,0:T(8,128)S(1)} collective-permute-done((f32[80,1024]{1,0:T(8,128)}, f32[80,1024]{1,0:T(8,128)S(1)}, u32[]{:S(2)}, u32[]{:S(2)}) %collective-permute-start.2) | collective-permute-done | bytes 327712 | tf_op jit(solution)/shard_map/ppermute | solution.py:30
  35.0 1.7 collective-permute-done.3.after
  36.7 0.8 copy-done.1
  37.5 1.9 shard_map.61
  39.4 2.9 %collective-permute-start.4 = (f32[54,1024]{1,0:T(8,128)}, f32[54,1024]{1,0:T(8,128)S(1)}, u32[]{:S(2)}, u32[]{:S(2)}) collective-permute-start(f32[54,1024]{1,0:T(8,128)} %get-tuple-element.26), channel_id=1, source_target_pairs={{0,8},{8,16},{16,24},{1,9},{9,17},{17,25},{2,10},{10,18},{18,26},{... | collective-permute-start | bytes 663560 | tf_op jit(solution)/shard_map/ppermute | solution.py:30
  42.4 1.3 collective-permute-start.5
  43.7 3.0 %shard_map.66.refs_0_ = f32[8,8,32,128]{3,2,1,0:T(8,128)} custom-call(f32[8,128,256]{2,1,0:T(8,128)} %scan.3), custom_call_target="tpu_custom_call" | custom-call | bytes 4194304 | tf_op jit(solution)/shard_map/pallas_call | solution.py:428
  46.7 0.8 collective-permute-done.5.corners_above
  48.2 6.8 %shard_map.62.gate.ext.ext_ref = f32[3,8,14,48,128]{4,3,2,1,0:T(8,128)} custom-call(f32[3,8,32,1024]{3,2,1,0:T(8,128)} %vel.3, f32[10,32,1024]{2,1,0:T(8,128)} %collective-permute-done.planes_below, f32[10,32,1024]{2,1,0:T(8,128)} %collective-permute-done.1.planes_above, f32[80,1024]{1,0:T(8,128)} %copy-done, f32[80,1024]{1,0:T(8,128)} %copy-done.1, ...), custom_call_target="tpu_custom_call" | custom-call | bytes 4194304 | tf_op jit(solution)/shard_map/pallas_call | solution.py:497
  55.0 2.0 %shard_map.63 = (f32[8,8,4,128]{3,2,1,0:T(4,128)}, f32[8,8,4,128]{3,2,1,0:T(4,128)}) custom-call(f32[8,8,32,128]{3,2,1,0:T(8,128)} %all-to-all-done.field.own, f32[3,8,14,48,128]{4,3,2,1,0:T(8,128)} %shard_map.62.gate.ext.ext_ref), custom_call_target="tpu_custom_call" | custom-call | bytes 4194304 | tf_op jit(solution)/shard_map/pallas_call | solution.py:501
  57.0 11.2 %all-to-all-start.1 = ((f32[8,8,32,128]{3,2,1,0:T(8,128)}), f32[8,8,32,128]{3,2,1,0:T(8,128)}, u32[]{:S(2)}, u32[]{:S(2)}) async-start(f32[8,8,32,128]{3,2,1,0:T(8,128)} %shard_map.67), calls=%async_computation.1 | async-start | bytes 2097152 | tf_op jit(solution)/shard_map/all_to_all | solution.py:433
  68.3 3.9 %collective-permute-start.6 = (f32[8,8,4,128]{3,2,1,0:T(4,128)S(1)}, f32[8,8,4,128]{3,2,1,0:T(4,128)S(1)}, u32[]{:S(2)}, u32[]{:S(2)}) collective-permute-start(f32[8,8,4,128]{3,2,1,0:T(4,128)S(1)} %copy-done.12), channel_id=1, source_target_pairs={{0,1},{1,2},{2,3},{3,4},{4,5},{5,6},{6,7},{8,9},{9,10},{10,11},{11... | collective-permute-start | bytes 393224 | tf_op jit(solution)/shard_map/ppermute | solution.py:30
  72.2 1.3 collective-permute-start.7
  73.5 7.5 %collective-permute-done.6.before = f32[8,8,4,128]{3,2,1,0:T(4,128)S(1)} collective-permute-done((f32[8,8,4,128]{3,2,1,0:T(4,128)S(1)}, f32[8,8,4,128]{3,2,1,0:T(4,128)S(1)}, u32[]{:S(2)}, u32[]{:S(2)}) %collective-permute-start.6) | collective-permute-done | bytes 131104 | tf_op jit(solution)/shard_map/ppermute | solution.py:30
  82.3 2.5 %shard_map.64 = (f32[8,4,40,128]{3,2,1,0:T(8,128)}, f32[8,4,40,128]{3,2,1,0:T(8,128)}) custom-call(f32[8,8,32,128]{3,2,1,0:T(8,128)} %all-to-all-done.field.own, f32[8,8,4,128]{3,2,1,0:T(4,128)} %copy-done.5, f32[8,8,4,128]{3,2,1,0:T(4,128)} %copy-done.6), custom_call_target="tpu_custom_call" | custom-call | bytes 4194304 | tf_op jit(solution)/shard_map/pallas_call | solution.py:444
  84.8 5.9 %collective-permute-start.8 = (f32[8,4,40,128]{3,2,1,0:T(8,128)}, f32[8,4,40,128]{3,2,1,0:T(8,128)S(1)}, u32[]{:S(2)}, u32[]{:S(2)}) collective-permute-start(f32[8,4,40,128]{3,2,1,0:T(8,128)} %get-tuple-element.30), channel_id=1, source_target_pairs={{0,8},{8,16},{16,24},{1,9},{9,17},{17,25},{2,10},{10,18},{18,26},{... | collective-permute-start | bytes 1966088 | tf_op jit(solution)/shard_map/ppermute | solution.py:30
  90.7 1.3 collective-permute-start.9
  92.0 0.7 add_convert_fusion.flags
  92.7 2.8 %collective-permute-done.9.above = f32[8,4,40,128]{3,2,1,0:T(8,128)} collective-permute-done((f32[8,4,40,128]{3,2,1,0:T(8,128)}, f32[8,4,40,128]{3,2,1,0:T(8,128)}, u32[]{:S(2)}, u32[]{:S(2)}) %collective-permute-start.9) | collective-permute-done | bytes 655392 | tf_op jit(solution)/shard_map/ppermute | solution.py:31
  95.5 12.9 %shard_map.65 = (f32[8,8,32,128]{3,2,1,0:T(8,128)}, f32[4,8,10,48,128]{4,3,2,1,0:T(8,128)}) custom-call(f32[4]{0:T(128)} %add_convert_fusion.flags, f32[8,8,32,128]{3,2,1,0:T(8,128)} %all-to-all-done.field.own, f32[8,4,40,128]{3,2,1,0:T(8,128)} %copy-done.4, f32[8,4,40,128]{3,2,1,0:T(8,128)} %collective-permute-done.9.above, f32[8,8,4,128]{3,2,1,0:T(4,128)} %copy-done.5, ...), custom_call_target="tpu_custom_call" | custom-call | flops 20971520 | bytes 4194304 | tf_op jit(solution)/shard_map/pallas_call | solution.py:504
  108.5 9.6 %shard_map.68 = (f32[3,8,32,1024]{3,2,1,0:T(8,128)}, f32[8,128]{1,0:T(8,128)}) custom-call(f32[8,8,32,128]{3,2,1,0:T(8,128)} %get-tuple-element.32.gate.moved, f32[3,8,14,48,128]{4,3,2,1,0:T(8,128)} %shard_map.62.gate.ext.ext_ref, f32[8,32,1024]{2,1,0:T(8,128)} %sti.3, f32[10,32,1024]{2,1,0:T(8,128)} %collective-permute-done.planes_below, ...), custom_call_target="tpu_custom_call" | custom-call | flops 20971520 | bytes 4194304 | tf_op jit(solution)/shard_map/pallas_call | solution.py:513
  118.0 2.9 %shard_map.69 = (f32[8,8,32,128]{3,2,1,0:T(8,128)}, f32[8,8,4,128]{3,2,1,0:T(4,128)}, f32[8,8,4,128]{3,2,1,0:T(4,128)}, f32[8,128]{1,0:T(8,128)}) custom-call(f32[8,8,32,128]{3,2,1,0:T(8,128)} %get-tuple-element.32.gate.moved, f32[8,8,32,128]{3,2,1,0:T(8,128)} %all-to-all-done.1.fixed, f32[8,128]{1,0:T(8,128)} %get-tuple-element.33.sums), custom_call_target="tpu_custom_call" | custom-call | bytes 4194304 | tf_op jit(solution)/shard_map/pallas_call | solution.py:521
  120.9 8.8 %collective-permute-start.10 = (f32[8,8,4,128]{3,2,1,0:T(4,128)}, f32[8,8,4,128]{3,2,1,0:T(4,128)S(1)}, u32[]{:S(2)}, u32[]{:S(2)}) collective-permute-start(f32[8,8,4,128]{3,2,1,0:T(4,128)} %get-tuple-element.35), channel_id=1, source_target_pairs={{0,1},{1,2},{2,3},{3,4},{4,5},{5,6},{6,7},{8,9},{9,10},{10,11},{11... | collective-permute-start | bytes 393224 | tf_op jit(solution)/shard_map/ppermute | solution.py:30
  129.8 1.3 collective-permute-start.11
  131.1 1.5 collective-permute-done.10.before.refs_1_
  132.6 5.9 %collective-permute-done.11.after.refs_2_ = f32[8,8,4,128]{3,2,1,0:T(4,128)S(1)} collective-permute-done((f32[8,8,4,128]{3,2,1,0:T(4,128)}, f32[8,8,4,128]{3,2,1,0:T(4,128)S(1)}, u32[]{:S(2)}, u32[]{:S(2)}) %collective-permute-start.11) | collective-permute-done | bytes 131104 | tf_op jit(solution)/shard_map/ppermute | solution.py:31
  139.1 2.3 %shard_map.70 = (f32[8,3,40,128]{3,2,1,0:T(8,128)}, f32[8,3,40,128]{3,2,1,0:T(8,128)}) custom-call(f32[8,8,32,128]{3,2,1,0:T(8,128)} %get-tuple-element.34.field.own, f32[8,8,4,128]{3,2,1,0:T(4,128)} %copy-done.2, f32[8,8,4,128]{3,2,1,0:T(4,128)} %copy-done.3), custom_call_target="tpu_custom_call" | custom-call | bytes 4194304 | tf_op jit(solution)/shard_map/pallas_call | solution.py:444
  141.4 9.2 %collective-permute-start.12 = (f32[8,3,40,128]{3,2,1,0:T(8,128)}, f32[8,3,40,128]{3,2,1,0:T(8,128)S(1)}, u32[]{:S(2)}, u32[]{:S(2)}) collective-permute-start(f32[8,3,40,128]{3,2,1,0:T(8,128)} %get-tuple-element.37), channel_id=1, source_target_pairs={{0,8},{8,16},{16,24},{1,9},{9,17},{17,25},{2,10},{10,18},{18,26},{... | collective-permute-start | bytes 1474568 | tf_op jit(solution)/shard_map/ppermute | solution.py:30
  150.6 1.3 collective-permute-start.13
  151.9 6.8 %collective-permute-start.14 = (f32[8,128]{1,0:T(8,128)}, f32[8,128]{1,0:T(8,128)S(1)}, u32[]{:S(2)}, u32[]{:S(2)}) collective-permute-start(f32[8,128]{1,0:T(8,128)} %shard_map.72), channel_id=1, source_target_pairs={{0,1},{1,0},{2,3},{3,2},{4,5},{5,4},{6,7},{7,6},{8,9},{9,8},{10,11... | collective-permute-start | bytes 12296 | tf_op jit(solution)/shard_map/ppermute | solution.py:457
  158.7 1.8 collective-permute-done.14
  160.5 0.7 add.15
  161.1 2.3 %collective-permute-start.15 = (f32[8,128]{1,0:T(8,128)S(1)}, f32[8,128]{1,0:T(8,128)S(1)}, u32[]{:S(2)}, u32[]{:S(2)}) collective-permute-start(f32[8,128]{1,0:T(8,128)S(1)} %add.15), channel_id=1, source_target_pairs={{0,2},{1,3},{2,0},{3,1},{4,6},{5,7},{6,4},{7,5},{8,10},{9,11},{10,... | collective-permute-start | bytes 12296 | tf_op jit(solution)/shard_map/ppermute | solution.py:457
  163.5 1.6 collective-permute-done.15
  165.1 2.0 %collective-permute-start.16 = (f32[8,128]{1,0:T(8,128)S(1)}, f32[8,128]{1,0:T(8,128)S(1)}, u32[]{:S(2)}, u32[]{:S(2)}) collective-permute-start(f32[8,128]{1,0:T(8,128)S(1)} %add.16), channel_id=1, source_target_pairs={{0,4},{1,5},{2,6},{3,7},{4,0},{5,1},{6,2},{7,3},{8,12},{9,13},{10,... | collective-permute-start | bytes 12296 | tf_op jit(solution)/shard_map/ppermute | solution.py:457
  167.1 2.5 %collective-permute-done.16 = f32[8,128]{1,0:T(8,128)S(1)} collective-permute-done((f32[8,128]{1,0:T(8,128)S(1)}, f32[8,128]{1,0:T(8,128)S(1)}, u32[]{:S(2)}, u32[]{:S(2)}) %collective-permute-start.16) | collective-permute-done | bytes 4128 | tf_op jit(solution)/shard_map/ppermute | solution.py:457
  169.6 1.2 collective-permute-done.17
  170.8 3.5 %collective-permute-start.18 = (f32[8,128]{1,0:T(8,128)S(1)}, f32[8,128]{1,0:T(8,128)S(1)}, u32[]{:S(2)}, u32[]{:S(2)}) collective-permute-start(f32[8,128]{1,0:T(8,128)S(1)} %add.18), channel_id=1, source_target_pairs={{0,16},{8,24},{16,0},{24,8},{1,17},{9,25},{17,1},{25,9},{2,18},{10... | collective-permute-start | bytes 12296 | tf_op jit(solution)/shard_map/ppermute | solution.py:457
  174.2 1.6 collective-permute-done.18
  177.1 0.7 copy-done.7
  178.0 15.0 %shard_map.71 = f32[3,8,32,1024]{3,2,1,0:T(8,128)} custom-call(f32[4]{0:T(128)} %add_convert_fusion.flags, f32[8,8,32,128]{3,2,1,0:T(8,128)} %get-tuple-element.34.field.own, f32[8,3,40,128]{3,2,1,0:T(8,128)} %copy-done.7, f32[8,3,40,128]{3,2,1,0:T(8,128)} %copy-done.8, f32[8,8,4,128]{3,2,1,0:T(4,128)} %copy-done.2, f32[8,8,4,128]{3,2,1,0:T(4,128)} %copy-done.3, ...), custom_call_target="tpu_custom_call" | custom-call | flops 20971520 | bytes 4194304 | tf_op jit(solution)/shard_map/pallas_call | solution.py:525
  (40 shorter events, 3.5 us)
Async XLA Ops:
  3.7 51.4 %all-to-all-start = ((f32[8,8,32,128]{3,2,1,0:T(8,128)}), f32[8,8,32,128]{3,2,1,0:T(8,128)}, u32[]{:S(2)}, u32[]{:S(2)}) async-start(f32[8,8,32,128]{3,2,1,0:T(8,128)} %shard_map.59), calls=%async_computation | async-start | bytes 2097152 | tf_op jit(solution)/shard_map/all_to_all | solution.py:433
  15.2 32.3 %collective-permute-start = (f32[10,32,1024]{2,1,0:T(8,128)}, f32[10,32,1024]{2,1,0:T(8,128)}, u32[]{:S(2)}, u32[]{:S(2)}) collective-permute-start(f32[10,32,1024]{2,1,0:T(8,128)} %get-tuple-element.22), channel_id=1, source_target_pairs={{0,8},{8,16},{16,24},{1,9},{9,17},{17,25},{2,10},{10,18},{18,26},{... | collective-permute-start | bytes 3932168 | tf_op jit(solution)/shard_map/ppermute | solution.py:30
  17.8 29.8 %collective-permute-start.1 = (f32[10,32,1024]{2,1,0:T(8,128)}, f32[10,32,1024]{2,1,0:T(8,128)}, u32[]{:S(2)}, u32[]{:S(2)}) collective-permute-start(f32[10,32,1024]{2,1,0:T(8,128)} %get-tuple-element.23), channel_id=1, source_target_pairs={{8,0},{16,8},{24,16},{9,1},{17,9},{25,17},{10,2},{18,10},{26,18},{... | collective-permute-start | bytes 3932168 | tf_op jit(solution)/shard_map/ppermute | solution.py:31
  19.0 16.0 %collective-permute-start.2 = (f32[80,1024]{1,0:T(8,128)}, f32[80,1024]{1,0:T(8,128)S(1)}, u32[]{:S(2)}, u32[]{:S(2)}) collective-permute-start(f32[80,1024]{1,0:T(8,128)} %get-tuple-element.24), channel_id=1, source_target_pairs={{0,1},{1,2},{2,3},{3,4},{4,5},{5,6},{6,7},{8,9},{9,10},{10,11},{11... | collective-permute-start | bytes 983048 | tf_op jit(solution)/shard_map/ppermute | solution.py:30
  22.8 13.9 %collective-permute-start.3 = (f32[80,1024]{1,0:T(8,128)}, f32[80,1024]{1,0:T(8,128)S(1)}, u32[]{:S(2)}, u32[]{:S(2)}) collective-permute-start(f32[80,1024]{1,0:T(8,128)} %get-tuple-element.25), channel_id=1, source_target_pairs={{1,0},{2,1},{3,2},{4,3},{5,4},{6,5},{7,6},{9,8},{10,9},{11,10},{12... | collective-permute-start | bytes 983048 | tf_op jit(solution)/shard_map/ppermute | solution.py:31
  35.0 1.7 copy-start
  36.7 0.8 copy-start.1
  39.4 7.2 %collective-permute-start.4 = (f32[54,1024]{1,0:T(8,128)}, f32[54,1024]{1,0:T(8,128)S(1)}, u32[]{:S(2)}, u32[]{:S(2)}) collective-permute-start(f32[54,1024]{1,0:T(8,128)} %get-tuple-element.26), channel_id=1, source_target_pairs={{0,8},{8,16},{16,24},{1,9},{9,17},{17,25},{2,10},{10,18},{18,26},{... | collective-permute-start | bytes 663560 | tf_op jit(solution)/shard_map/ppermute | solution.py:30
  42.4 5.1 %collective-permute-start.5 = (f32[54,1024]{1,0:T(8,128)}, f32[54,1024]{1,0:T(8,128)S(1)}, u32[]{:S(2)}, u32[]{:S(2)}) collective-permute-start(f32[54,1024]{1,0:T(8,128)} %get-tuple-element.27), channel_id=1, source_target_pairs={{8,0},{16,8},{24,16},{9,1},{17,9},{25,17},{10,2},{18,10},{26,18},{... | collective-permute-start | bytes 663560 | tf_op jit(solution)/shard_map/ppermute | solution.py:31
  46.7 0.9 copy-start.9
  47.5 0.7 copy-start.10
  57.0 11.3 %copy-start.12 = (f32[8,8,4,128]{3,2,1,0:T(4,128)S(1)}, f32[8,8,4,128]{3,2,1,0:T(4,128)}, u32[]{:S(2)}) copy-start(f32[8,8,4,128]{3,2,1,0:T(4,128)} %get-tuple-element.28) | copy-start | bytes 393220
  57.0 15.2 %copy-start.11 = (f32[8,8,4,128]{3,2,1,0:T(4,128)S(1)}, f32[8,8,4,128]{3,2,1,0:T(4,128)}, u32[]{:S(2)}) copy-start(f32[8,8,4,128]{3,2,1,0:T(4,128)} %get-tuple-element.29.refs_1_) | copy-start | bytes 393220
  57.0 61.0 %all-to-all-start.1 = ((f32[8,8,32,128]{3,2,1,0:T(8,128)}), f32[8,8,32,128]{3,2,1,0:T(8,128)}, u32[]{:S(2)}, u32[]{:S(2)}) async-start(f32[8,8,32,128]{3,2,1,0:T(8,128)} %shard_map.67), calls=%async_computation.1 | async-start | bytes 2097152 | tf_op jit(solution)/shard_map/all_to_all | solution.py:433
  68.3 12.7 %collective-permute-start.6 = (f32[8,8,4,128]{3,2,1,0:T(4,128)S(1)}, f32[8,8,4,128]{3,2,1,0:T(4,128)S(1)}, u32[]{:S(2)}, u32[]{:S(2)}) collective-permute-start(f32[8,8,4,128]{3,2,1,0:T(4,128)S(1)} %copy-done.12), channel_id=1, source_target_pairs={{0,1},{1,2},{2,3},{3,4},{4,5},{5,6},{6,7},{8,9},{9,10},{10,11},{11... | collective-permute-start | bytes 393224 | tf_op jit(solution)/shard_map/ppermute | solution.py:30
  72.2 8.8 %collective-permute-start.7 = (f32[8,8,4,128]{3,2,1,0:T(4,128)S(1)}, f32[8,8,4,128]{3,2,1,0:T(4,128)S(1)}, u32[]{:S(2)}, u32[]{:S(2)}) collective-permute-start(f32[8,8,4,128]{3,2,1,0:T(4,128)S(1)} %copy-done.11), channel_id=1, source_target_pairs={{1,0},{2,1},{3,2},{4,3},{5,4},{6,5},{7,6},{9,8},{10,9},{11,10},{12... | collective-permute-start | bytes 393224 | tf_op jit(solution)/shard_map/ppermute | solution.py:31
  81.0 0.7 copy-start.5
  81.7 0.7 copy-start.6
  84.8 7.9 %collective-permute-start.8 = (f32[8,4,40,128]{3,2,1,0:T(8,128)}, f32[8,4,40,128]{3,2,1,0:T(8,128)S(1)}, u32[]{:S(2)}, u32[]{:S(2)}) collective-permute-start(f32[8,4,40,128]{3,2,1,0:T(8,128)} %get-tuple-element.30), channel_id=1, source_target_pairs={{0,8},{8,16},{16,24},{1,9},{9,17},{17,25},{2,10},{10,18},{18,26},{... | collective-permute-start | bytes 1966088 | tf_op jit(solution)/shard_map/ppermute | solution.py:30
  90.7 4.8 %collective-permute-start.9 = (f32[8,4,40,128]{3,2,1,0:T(8,128)}, f32[8,4,40,128]{3,2,1,0:T(8,128)}, u32[]{:S(2)}, u32[]{:S(2)}) collective-permute-start(f32[8,4,40,128]{3,2,1,0:T(8,128)} %get-tuple-element.31), channel_id=1, source_target_pairs={{8,0},{16,8},{24,16},{9,1},{17,9},{25,17},{10,2},{18,10},{26,18},{... | collective-permute-start | bytes 1966088 | tf_op jit(solution)/shard_map/ppermute | solution.py:31
  92.7 2.8 %copy-start.4 = (f32[8,4,40,128]{3,2,1,0:T(8,128)}, f32[8,4,40,128]{3,2,1,0:T(8,128)S(1)}, u32[]{:S(2)}) copy-start(f32[8,4,40,128]{3,2,1,0:T(8,128)S(1)} %collective-permute-done.8.below) | copy-start | bytes 1966084
  120.9 11.7 %collective-permute-start.10 = (f32[8,8,4,128]{3,2,1,0:T(4,128)}, f32[8,8,4,128]{3,2,1,0:T(4,128)S(1)}, u32[]{:S(2)}, u32[]{:S(2)}) collective-permute-start(f32[8,8,4,128]{3,2,1,0:T(4,128)} %get-tuple-element.35), channel_id=1, source_target_pairs={{0,1},{1,2},{2,3},{3,4},{4,5},{5,6},{6,7},{8,9},{9,10},{10,11},{11... | collective-permute-start | bytes 393224 | tf_op jit(solution)/shard_map/ppermute | solution.py:30
  129.8 8.7 %collective-permute-start.11 = (f32[8,8,4,128]{3,2,1,0:T(4,128)}, f32[8,8,4,128]{3,2,1,0:T(4,128)S(1)}, u32[]{:S(2)}, u32[]{:S(2)}) collective-permute-start(f32[8,8,4,128]{3,2,1,0:T(4,128)} %get-tuple-element.36), channel_id=1, source_target_pairs={{1,0},{2,1},{3,2},{4,3},{5,4},{6,5},{7,6},{9,8},{10,9},{11,10},{12... | collective-permute-start | bytes 393224 | tf_op jit(solution)/shard_map/ppermute | solution.py:31
  132.6 5.9 %copy-start.2 = (f32[8,8,4,128]{3,2,1,0:T(4,128)}, f32[8,8,4,128]{3,2,1,0:T(4,128)S(1)}, u32[]{:S(2)}) copy-start(f32[8,8,4,128]{3,2,1,0:T(4,128)S(1)} %collective-permute-done.10.before.refs_1_) | copy-start | bytes 393220
  138.5 0.6 copy-start.3
  141.4 35.6 %collective-permute-start.12 = (f32[8,3,40,128]{3,2,1,0:T(8,128)}, f32[8,3,40,128]{3,2,1,0:T(8,128)S(1)}, u32[]{:S(2)}, u32[]{:S(2)}) collective-permute-start(f32[8,3,40,128]{3,2,1,0:T(8,128)} %get-tuple-element.37), channel_id=1, source_target_pairs={{0,8},{8,16},{16,24},{1,9},{9,17},{17,25},{2,10},{10,18},{18,26},{... | collective-permute-start | bytes 1474568 | tf_op jit(solution)/shard_map/ppermute | solution.py:30
  150.6 26.5 %collective-permute-start.13 = (f32[8,3,40,128]{3,2,1,0:T(8,128)}, f32[8,3,40,128]{3,2,1,0:T(8,128)S(1)}, u32[]{:S(2)}, u32[]{:S(2)}) collective-permute-start(f32[8,3,40,128]{3,2,1,0:T(8,128)} %get-tuple-element.38), channel_id=1, source_target_pairs={{8,0},{16,8},{24,16},{9,1},{17,9},{25,17},{10,2},{18,10},{26,18},{... | collective-permute-start | bytes 1474568 | tf_op jit(solution)/shard_map/ppermute | solution.py:31
  151.9 8.5 %collective-permute-start.14 = (f32[8,128]{1,0:T(8,128)}, f32[8,128]{1,0:T(8,128)S(1)}, u32[]{:S(2)}, u32[]{:S(2)}) collective-permute-start(f32[8,128]{1,0:T(8,128)} %shard_map.72), channel_id=1, source_target_pairs={{0,1},{1,0},{2,3},{3,2},{4,5},{5,4},{6,7},{7,6},{8,9},{9,8},{10,11... | collective-permute-start | bytes 12296 | tf_op jit(solution)/shard_map/ppermute | solution.py:457
  161.1 3.9 %collective-permute-start.15 = (f32[8,128]{1,0:T(8,128)S(1)}, f32[8,128]{1,0:T(8,128)S(1)}, u32[]{:S(2)}, u32[]{:S(2)}) collective-permute-start(f32[8,128]{1,0:T(8,128)S(1)} %add.15), channel_id=1, source_target_pairs={{0,2},{1,3},{2,0},{3,1},{4,6},{5,7},{6,4},{7,5},{8,10},{9,11},{10,... | collective-permute-start | bytes 12296 | tf_op jit(solution)/shard_map/ppermute | solution.py:457
  165.1 4.5 %collective-permute-start.16 = (f32[8,128]{1,0:T(8,128)S(1)}, f32[8,128]{1,0:T(8,128)S(1)}, u32[]{:S(2)}, u32[]{:S(2)}) collective-permute-start(f32[8,128]{1,0:T(8,128)S(1)} %add.16), channel_id=1, source_target_pairs={{0,4},{1,5},{2,6},{3,7},{4,0},{5,1},{6,2},{7,3},{8,12},{9,13},{10,... | collective-permute-start | bytes 12296 | tf_op jit(solution)/shard_map/ppermute | solution.py:457
  169.6 1.2 collective-permute-start.17
  170.8 5.1 %collective-permute-start.18 = (f32[8,128]{1,0:T(8,128)S(1)}, f32[8,128]{1,0:T(8,128)S(1)}, u32[]{:S(2)}, u32[]{:S(2)}) collective-permute-start(f32[8,128]{1,0:T(8,128)S(1)} %add.18), channel_id=1, source_target_pairs={{0,16},{8,24},{16,0},{24,8},{1,17},{9,25},{17,1},{25,9},{2,18},{10... | collective-permute-start | bytes 12296 | tf_op jit(solution)/shard_map/ppermute | solution.py:457
  177.1 0.8 copy-start.7
  177.1 0.9 copy-start.8

commit v3 on v2

--- a/solution.py
+++ b/solution.py
@@ -13,7 +13,7 @@
 
 LANES = 128
 TILE = 8
-GAP = 8
+GAP = 4
 SENT = 4
 WIDE = STEPS - 1
 WEIGHT = DT * KAPPA
@@ -48,52 +48,54 @@
 
 def fill(out, own, below, above, before, after, width):
     blocks, sections, rows, _ = own.shape
-    top, bottom = pl.ds(GAP - SENT, SENT), pl.ds(GAP + rows, SENT)
 
     def whole(z, _):
         for i in range(blocks):
             out[i, z + width, pl.ds(GAP, rows), :] = own[i, z, :, :]
-            out[i, z + width, top, :] = before[i, z, :, :]
-            out[i, z + width, bottom, :] = after[i, z, :, :]
+            out[i, z + width, pl.ds(0, SENT), :] = before[i, z, :, :]
+            out[i, z + width, pl.ds(GAP + rows, SENT), :] = after[i, z, :, :]
         return 0
 
     def halo(z, _):
         for planes, at in ((below, z), (above, z + width + sections)):
             for i in range(blocks):
-                out[i, at, pl.ds(GAP, rows), :] = planes[i, z, pl.ds(0, rows), :]
-                out[i, at, top, :] = planes[i, z, pl.ds(rows, SENT), :]
-                out[i, at, bottom, :] = planes[i, z, pl.ds(rows + SENT, SENT), :]
+                out[i, at, :, :] = planes[i, z, :, :]
         return 0
 
     lax.fori_loop(0, sections, whole, 0)
     lax.fori_loop(0, width, halo, 0)
 
 
-def block_kernel(scan, out):
+def block_kernel(scan, gate, out, turned):
+    del gate
     sections, width, rows = scan.shape
-    own = out.shape[2]
+    count, _, tall, _ = out.shape
+    own = rows // count
+    first = TILE - (tall - own) // 2
+    zero = jnp.zeros((TILE, width), jnp.float32)
+    turned[pl.ds(0, TILE), :] = zero
+    turned[pl.ds(TILE + rows, TILE), :] = zero
 
     def section(z, _):
         for cut in range(0, rows, width):
-            turned = scan[z, :, pl.ds(cut, width)].T
-            for r in range(0, width, own):
-                out[(cut + r) // own, z, :, :] = turned[r : r + own]
+            turned[pl.ds(TILE + cut, width), :] = scan[z, :, pl.ds(cut, width)].T
+        for j in range(count):
+            out[j, z, :, :] = turned[pl.ds(first + j * own, tall), :]
         return 0
 
     lax.fori_loop(0, sections, section, 0)
 
 
-def end_kernel(field, gate, low_rows, high_rows):
-    del gate
-    blocks, sections, rows, _ = field.shape
-
-    def section(z, _):
-        for i in range(blocks):
-            low_rows[i, z, :, :] = field[i, z, pl.ds(0, SENT), :]
-            high_rows[i, z, :, :] = field[i, z, pl.ds(rows - SENT, SENT), :]
-        return 0
-
-    lax.fori_loop(0, sections, section, 0)
+def slice_kernel(field, low, high, sem):
+    sections, width = field.shape[1], low.shape[1]
+    copies = [
+        pltpu.make_async_copy(field.at[:, pl.ds(0, width)], low, sem.at[0]),
+        pltpu.make_async_copy(field.at[:, pl.ds(sections - width, width)], high, sem.at[1]),
+    ]
+    for copy in copies:
+        copy.start()
+    for copy in copies:
+        copy.wait()
 
 
 def plane_kernel(field, before, after, low, high):
@@ -103,9 +105,9 @@
     def plane(z, _):
         for out, at in ((low, z), (high, z + sections - width)):
             for i in range(blocks):
-                out[i, z, pl.ds(0, rows), :] = field[i, at, :, :]
-                out[i, z, pl.ds(rows, SENT), :] = before[i, at, :, :]
-                out[i, z, pl.ds(rows + SENT, SENT), :] = after[i, at, :, :]
+                out[i, z, pl.ds(0, SENT), :] = before[i, at, :, :]
+                out[i, z, pl.ds(GAP, rows), :] = field[i, at, :, :]
+                out[i, z, pl.ds(GAP + rows, SENT), :] = after[i, at, :, :]
         return 0
 
     lax.fori_loop(0, width, plane, 0)
@@ -130,8 +132,19 @@
     total_ref[...] = 0.5 * (lax.fori_loop(0, sections, section, zero) + sums[...])
 
 
-def pack_kernel(vel, sti, low_rows, high_rows, low, high):
+def pack_kernel(vel, sti, low_rows, high_rows, low, high, sem):
     _, sections, rows, _ = vel.shape
+    copies = []
+    for half, (out, at, one) in enumerate(((low, 0, 0), (high, sections - WIDE, sections - 1))):
+        for c in range(3):
+            copies.append(pltpu.make_async_copy(
+                vel.at[c, pl.ds(at, WIDE)], out.at[pl.ds(c * WIDE, WIDE)], sem.at[4 * half + c]
+            ))
+        copies.append(pltpu.make_async_copy(
+            sti.at[pl.ds(one, 1)], out.at[pl.ds(3 * WIDE, 1)], sem.at[4 * half + 3]
+        ))
+    for copy in copies:
+        copy.start()
     for c in range(3):
         for z in range(sections):
             at = pl.ds((c * sections + z) * WIDE, WIDE)
@@ -141,16 +154,8 @@
         at = pl.ds(3 * sections * WIDE + z, 1)
         low_rows[at, :] = sti[z, pl.ds(0, 1), :]
         high_rows[at, :] = sti[z, pl.ds(rows - 1, 1), :]
-
-    def plane(z, _):
-        for c in range(3):
-            low[c * WIDE + z, :, :] = vel[c, z, :, :]
-            high[c * WIDE + z, :, :] = vel[c, sections - WIDE + z, :, :]
-        return 0
-
-    lax.fori_loop(0, WIDE, plane, 0)
-    low[3 * WIDE, :, :] = sti[0, :, :]
-    high[3 * WIDE, :, :] = sti[sections - 1, :, :]
+    for copy in copies:
+        copy.wait()
 
 
 def corner_kernel(before, after, low, high):
@@ -166,7 +171,7 @@
 def groups(rows, reach):
     if reach == 0:
         return [GAP + g for g in range(0, rows, TILE)]
-    return [GAP - SENT + g for g in range(0, rows + TILE, TILE)]
+    return [1 + g for g in range(0, rows, TILE)] + [rows + 2 * GAP - 1 - TILE]
 
 
 def masked(value, start, rows, flags):
@@ -183,25 +188,33 @@
     return SELF * factor, WEIGHT * factor
 
 
-def forward_kernel(flags, own, below, above, before, after, ext, moved_ref, kept, *scratch):
-    levels, vel, vel_sem, kept_sem = scratch[:STEPS], scratch[STEPS], scratch[STEPS + 1], scratch[STEPS + 2]
-    blocks, sections, rows, _ = own.shape
+def forward_kernel(flags, own, below, above, ext, moved_ref, kept, *scratch):
+    levels, (vel, own_sem, vel_sem, kept_sem) = scratch[:STEPS], scratch[STEPS:]
+    blocks, sections, rows, _ = moved_ref.shape
+    first = [
+        pltpu.make_async_copy(src, levels[0].at[:, pl.ds(at, src.shape[1])], own_sem.at[n])
+        for n, (src, at) in enumerate(((below, 0), (own, STEPS), (above, STEPS + sections)))
+    ]
 
     def load(z):
         return pltpu.make_async_copy(ext.at[:, :, z], vel.at[:, :, z], vel_sem.at[z])
 
+    for copy in first:
+        copy.start()
     for z in range(sections + 2 * WIDE):
         load(z).start()
-    fill(levels[0], own, below, above, before, after, STEPS)
+    for copy in first:
+        copy.wait()
     copies = []
     for step in range(STEPS):
         src = levels[step]
-        copies.append(
-            pltpu.make_async_copy(
-                src.at[:, pl.ds(STEPS - 1, sections + 2)], kept.at[step], kept_sem.at[step]
+        if step > 0:
+            copies.append(
+                pltpu.make_async_copy(
+                    src.at[:, pl.ds(STEPS - 1, sections + 2)], kept.at[step - 1], kept_sem.at[step - 1]
+                )
             )
-        )
-        copies[-1].start()
+            copies[-1].start()
         reach = STEPS - 1 - step
 
         def plane(z, _, src=src, step=step, reach=reach):
@@ -231,7 +244,9 @@
         copy.wait()
 
 
-def adjoint_kernel(flags, own, below, above, before, after, ext, kept_all, reg_all, grad_all, *scratch):
+def adjoint_kernel(flags, own, below, above, before, after, ext, start, start_below, start_above,
+                   kept_all, reg_all, gate, grad_all, *scratch):
+    del gate
     levels, (vel, kept, reg, grad_ref, vel_sem, kept_sem, reg_sem, grad_sem) = scratch[:STEPS], scratch[STEPS:]
     blocks, sections, rows, _ = own.shape
 
@@ -242,7 +257,14 @@
         return pltpu.make_async_copy(grad_ref.at[:, z], grad_all.at[:, z], grad_sem.at[z])
 
     later = [
-        pltpu.make_async_copy(kept_all.at[k], kept.at[k], kept_sem.at[k]) for k in range(STEPS)
+        pltpu.make_async_copy(src, kept.at[0, :, pl.ds(at, src.shape[1])], kept_sem.at[STEPS - 1 + n])
+        for n, (src, at) in enumerate((
+            (start_below.at[:, pl.ds(STEPS - 1, 1)], 0),
+            (start, 1),
+            (start_above.at[:, pl.ds(0, 1)], sections + 1),
+        ))
+    ] + [
+        pltpu.make_async_copy(kept_all.at[k], kept.at[k + 1], kept_sem.at[k]) for k in range(STEPS - 1)
     ] + [pltpu.make_async_copy(reg_all, reg, reg_sem.at[0])]
     for z in range(sections + 2 * WIDE):
         load(z).start()
@@ -420,13 +442,17 @@
     )(value, *gates)
 
 
-def to_blocks(scan):
+def to_blocks(scan, extra, gate):
     count = lax.axis_size("row")
     sections, width, rows = scan.shape
     own = rows // count
-    if width == LANES and rows % width == 0 and width % own == 0:
-        return call(block_kernel, [(count, sections, own, width)], [VMEM])(scan)[0]
-    return jnp.swapaxes(scan, 1, 2).reshape(sections, count, own, width).transpose(1, 0, 2, 3)
+    tall = own + 2 * extra
+    if width == LANES and rows % width == 0:
+        return call(
+            block_kernel, [(count, sections, tall, width)], [VMEM, ANY], [(rows + 2 * TILE, width)]
+        )(scan, gate)[0]
+    turned = jnp.pad(jnp.swapaxes(scan, 1, 2), ((0, 0), (extra, extra), (0, 0)))
+    return jnp.stack([turned[:, j * own : j * own + tall] for j in range(count)])
 
 
 def to_rows(parts):
@@ -438,25 +464,26 @@
     return whole.transpose(2, 0, 1, 3)
 
 
-def halos(field, width, low_rows, high_rows):
-    blocks, _, rows, _ = field.shape
-    before, after_ = exchange(low_rows, high_rows, "row")
-    low, high = call(plane_kernel, [(blocks, width, rows + 2 * SENT, LANES)] * 2, [VMEM] * 3)(
-        field, before, after_
-    )
-    return exchange(low, high, "sec") + (before, after_)
-
-
-def everywhere(part):
-    for axis in ("row", "sec"):
-        count, near = lax.axis_size(axis), 1
-        if count & (count - 1):
-            part = lax.psum(part, axis)
-            continue
-        while near < count:
-            part = part + lax.ppermute(part, axis, [(i, i ^ near) for i in range(count)])
+def summed(part, axis, lows):
+    count = lax.axis_size(axis)
+    got = [lax.ppermute(part, axis, [(i, i ^ low) for i in range(count)]) for low in lows]
+    if len(got) == 3:
+        place = lax.axis_index(axis) // lows[0] % 4
+        pairs = (part + got[0], got[1] + got[2])
+        return jnp.where(place < 2, pairs[0], pairs[1]) + jnp.where(place < 2, pairs[1], pairs[0])
+    return part + got[0]
+
+
+def stages(axis):
+    count, near, found = lax.axis_size(axis), 1, []
+    while near < count:
+        if count % (4 * near) == 0:
+            found.append((axis, (near, 2 * near, 3 * near)))
+            near *= 4
+        else:
+            found.append((axis, (near,)))
             near *= 2
-    return part
+    return found
 
 
 def call(kernel, shapes, ins, scratch=(), outs=None, flops=0):
@@ -485,30 +512,35 @@
         sec > 0, sec < lax.axis_size("sec") - 1, row > 0, row < lax.axis_size("row") - 1
     ]).astype(jnp.float32)
 
-    template = to_rows(to_blocks(template_scan))
-
     lines = (3 * WIDE + 1) * sections
     low_rows, high_rows, low, high = call(
-        pack_kernel, [(lines, width)] * 2 + [(3 * WIDE + 1, rows, width)] * 2, [VMEM] * 2
+        pack_kernel,
+        [(lines, width)] * 2 + [(3 * WIDE + 1, rows, width)] * 2,
+        [VMEM] * 2,
+        [8],
+        [VMEM] * 2 + [ANY] * 2,
     )(velocity, stiffness)
     before, after_ = exchange(low_rows, high_rows, "row")
+    template = to_rows(to_blocks(template_scan, SENT, low_rows))
     below, above = exchange(low, high, "sec")
     corners = call(corner_kernel, [(6 * WIDE * WIDE, width)] * 2, [VMEM] * 2)(before, after_)
     (extended,) = call(extend_kernel, [(3, blocks, deep, tall, LANES)], [VMEM] * 7)(
         velocity, below, above, before, after_, *exchange(*corners, "sec")
     )
 
-    parts = call(end_kernel, [ends] * 2, [VMEM, ANY])(template, extended)
-    fixed = to_rows(after(to_blocks(reference_scan), parts[0]))
+    fixed_blocks = to_blocks(reference_scan, 0, corners[0])
+    low, high = call(slice_kernel, [(blocks, STEPS, tall, LANES)] * 2, [ANY], [2], [ANY] * 2)(template)
+    start = (template,) + exchange(low, high, "sec")
+    fixed = to_rows(after(fixed_blocks, low))
     level = (blocks, sections + 2 * STEPS, tall, LANES)
     moved, kept = call(
         forward_kernel,
-        [own, (STEPS, blocks, sections + 2, tall, LANES)],
-        [SMEM] + [VMEM] * 5 + [ANY],
-        [level] * STEPS + [(3, blocks, deep, tall, LANES), deep, STEPS],
+        [own, (STEPS - 1, blocks, sections + 2, tall, LANES)],
+        [SMEM] + [ANY] * 4,
+        [level] * STEPS + [(3, blocks, deep, tall, LANES), 3, deep, STEPS - 1],
         [VMEM, ANY],
         20 << 20,
-    )(flags, template, *halos(template, STEPS, *parts), extended)
+    )(flags, *start, extended)
 
     reg, reg_sums = call(
         regular_kernel,
@@ -518,23 +550,31 @@
         flops=20 << 20,
     )(moved, extended, stiffness, below, above, before, after_)
 
-    misfit, *parts, partial = call(misfit_kernel, [own, ends, ends, (TILE, LANES)], [VMEM] * 3)(
+    misfit, low_rows, high_rows, partial = call(misfit_kernel, [own, ends, ends, (TILE, LANES)], [VMEM] * 3)(
         moved, fixed, reg_sums
     )
-    around = halos(misfit, WIDE, *parts)
+    before, after_ = exchange(low_rows, high_rows, "row")
+    low, high = call(plane_kernel, [(blocks, WIDE, tall, LANES)] * 2, [VMEM] * 3)(misfit, before, after_)
+    below, above = exchange(low, high, "sec")
+    partial = after(partial, low)
+    for stage in stages("row"):
+        partial = summed(partial, *stage)
+    partial = after(partial, below, above)
     (gradient,) = call(
         adjoint_kernel,
         [velocity.shape],
-        [SMEM] + [VMEM] * 5 + [ANY] * 3,
+        [SMEM] + [VMEM] * 5 + [ANY] * 7,
         [(blocks, deep, tall, LANES)] * STEPS
         + [(3, blocks, deep, tall, LANES), (STEPS, blocks, sections + 2, tall, LANES)]
-        + [velocity.shape] * 2 + [deep, STEPS, 1, sections],
+        + [velocity.shape] * 2 + [deep, STEPS + 2, 1, sections],
         [ANY],
         20 << 20,
-    )(flags, misfit, *around, extended, kept, reg)
+    )(flags, misfit, below, above, before, after_, extended, *start, kept, reg, partial)
+    for stage in stages("sec"):
+        partial = summed(partial, *stage)
 
     voxels = sections * rows * width * lax.axis_size("sec") * lax.axis_size("row")
-    objective = jnp.sum(everywhere(after(partial, around[2], around[3]))) / voxels
+    objective = jnp.sum(partial) / voxels
     return (gradient, objective)
 
 

time: 195 us -> 225 us (1.15)
  Pallas kernels: 66.3 us -> 102 us
  starting transfers between devices: 79.2 us -> 62.3 us
  waiting for transfers between devices: 39.8 us -> 50.2 us
    pallas_call x7 -> x6, Pallas kernels: 40.8 us -> 76.7 us  [the longest x1 40.8 us: local(): call(slice_kernel, [(blocks, STEPS, tall, LANES)] * 2, [ANY], [2], [ANY]...]
    ppermute x7 -> x6, starting transfers between devices: 37.1 us -> 23.9 us  [exchange(): lax.ppermute(high_part, axis, [(i, i + 1) for i in range(count - 1)])]
    ppermute x7 -> x6, waiting for transfers between devices: 11.2 us -> 18.9 us  [exchange(): above = lax.ppermute(low_part, axis, [(i + 1, i) for i in range(count - 1)])]
    ppermute x7 -> x6, waiting for transfers between devices: 19.9 us -> 25.4 us  [exchange(): lax.ppermute(high_part, axis, [(i, i + 1) for i in range(count - 1)])]
    ppermute x5 -> x7, starting transfers between devices: 14.6 us -> 9.95 us  [summed(): lax.ppermute(part, axis, [(i, i ^ low) for i in range(count)])]
    ppermute x5 -> x7, waiting for transfers between devices: 8.64 us -> 5.87 us  [summed(): lax.ppermute(part, axis, [(i, i ^ low) for i in range(count)])]
    ppermute x7 -> x6, starting transfers between devices: 9.03 us -> 7.73 us  [exchange(): above = lax.ppermute(low_part, axis, [(i + 1, i) for i in range(count - 1)])]
    unnamed x26 -> x30, local copies, waits for them, and re-layouts: 4.34 us -> 5.3 us
  transfers between devices with their start and end apart: 21 -> 21, of which waited for: 12 -> 9; matrix products, arithmetic and copies ran while one was open for 1% -> 1% of each run, Pallas kernels for 21% -> 21%
where the time goes in v3:
time: 225 us
  Pallas kernels  102 us (45%)
  starting transfers between devices  62.3 us (28%)
  waiting for transfers between devices  50.2 us (22%)
  local copies, waits for them, and re-layouts  5.3 us (2%)
  between operations  2.67 us (1%)
  other arithmetic  2.47 us (1%)
    pallas_call x1, Pallas kernels, local(): call(slice_kernel, [(blocks, STEPS, tall, LANES)] * 2, [ANY], [2], [ANY]...  40.8 us
    ppermute x6, waiting for transfers between devices, exchange(): lax.ppermute(high_part, axis, [(i, i + 1) for i in range(count - 1)])  25.4 us
    ppermute x6, starting transfers between devices, exchange(): lax.ppermute(high_part, axis, [(i, i + 1) for i in range(count - 1)])  23.9 us
    all_to_all x2, starting transfers between devices, to_rows(): lax.all_to_all(parts, 'row', split_axis=0, concat_axis=0, tiled=True)  20.7 us
    ppermute x6, waiting for transfers between devices, exchange(): above = lax.ppermute(low_part, axis, [(i + 1, i) for i in range(count - 1)])  18.9 us
    pallas_call x1, Pallas kernels, local(): call(adjoint_kernel, [velocity.shape], [SMEM] + [VMEM] * 5 + [ANY] * 7, [...  13.9 us
    pallas_call x1, Pallas kernels, local(): call(forward_kernel, [own, (STEPS - 1, blocks, sections + 2, tall, LANES)...  13.3 us
    ppermute x7, starting transfers between devices, summed(): lax.ppermute(part, axis, [(i, i ^ low) for i in range(count)])  9.95 us
  transfers between devices with their start and end apart: 21, of which 9 were waited for; matrix products, arithmetic and copies ran while one was open for 1% of the time, Pallas kernels for 21%

profile of v3, /device:TPU:0, one launch (start us, length us, event | category | flops | bytes accessed | tf_op | source)
XLA Modules:
  0.0 224.6 jit_solution(8593273979287676644)
XLA Ops:
  0.6 4.5 %shard_map.59 = (f32[80,1024]{1,0:T(8,128)}, f32[80,1024]{1,0:T(8,128)}, f32[10,32,1024]{2,1,0:T(8,128)}, f32[10,32,1024]{2,1,0:T(8,128)}) custom-call(f32[3,8,32,1024]{3,2,1,0:T(8,128)} %vel.3, f32[8,32,1024]{2,1,0:T(8,128)} %sti.3), custom_call_target="tpu_custom_call" | custom-call | bytes 4194304 | tf_op jit(solution)/shard_map/pallas_call | solution.py:516
  5.2 3.3 %shard_map.60 = f32[8,8,40,128]{3,2,1,0:T(8,128)} custom-call(f32[8,128,256]{2,1,0:T(8,128)} %scan.2, f32[80,1024]{1,0:T(8,128)} %get-tuple-element.20.gate), custom_call_target="tpu_custom_call" | custom-call | bytes 4194304 | tf_op jit(solution)/shard_map/pallas_call | solution.py:451
  8.5 7.4 %all-to-all-start = ((f32[8,8,40,128]{3,2,1,0:T(8,128)}), f32[8,8,40,128]{3,2,1,0:T(8,128)}, u32[]{:S(2)}, u32[]{:S(2)}) async-start(f32[8,8,40,128]{3,2,1,0:T(8,128)} %shard_map.60), calls=%async_computation | async-start | bytes 2621440 | tf_op jit(solution)/shard_map/all_to_all | solution.py:459
  15.9 3.9 %collective-permute-start.4 = (f32[80,1024]{1,0:T(8,128)S(1)}, f32[80,1024]{1,0:T(8,128)S(1)}, u32[]{:S(2)}, u32[]{:S(2)}) collective-permute-start(f32[80,1024]{1,0:T(8,128)S(1)} %copy-done.13), channel_id=1, source_target_pairs={{0,1},{1,2},{2,3},{3,4},{4,5},{5,6},{6,7},{8,9},{9,10},{10,11},{11... | collective-permute-start | bytes 983048 | tf_op jit(solution)/shard_map/ppermute | solution.py:30
  19.8 1.3 collective-permute-start.5
  21.1 22.8 %collective-permute-done.4.before = f32[80,1024]{1,0:T(8,128)S(1)} collective-permute-done((f32[80,1024]{1,0:T(8,128)S(1)}, f32[80,1024]{1,0:T(8,128)S(1)}, u32[]{:S(2)}, u32[]{:S(2)}) %collective-permute-start.4) | collective-permute-done | bytes 327712 | tf_op jit(solution)/shard_map/ppermute | solution.py:30
  43.9 0.7 copy-done
  44.7 0.7 copy-done.1
  45.4 2.0 shard_map.62
  47.4 3.0 %shard_map.65.refs_0_ = f32[8,8,32,128]{3,2,1,0:T(8,128)} custom-call(f32[8,128,256]{2,1,0:T(8,128)} %scan.3, f32[54,1024]{1,0:T(8,128)} %get-tuple-element.27.gate), custom_call_target="tpu_custom_call" | custom-call | bytes 4194304 | tf_op jit(solution)/shard_map/pallas_call | solution.py:451
  50.4 40.8 %shard_map.61 = (f32[8,4,40,128]{3,2,1,0:T(8,128)}, f32[8,4,40,128]{3,2,1,0:T(8,128)}) custom-call(f32[8,8,40,128]{3,2,1,0:T(8,128)} %all-to-all-done.field.own.start), custom_call_target="tpu_custom_call" | custom-call | bytes 4194304 | tf_op jit(solution)/shard_map/pallas_call | solution.py:532
  91.3 13.3 %all-to-all-start.1 = ((f32[8,8,32,128]{3,2,1,0:T(8,128)}), f32[8,8,32,128]{3,2,1,0:T(8,128)}, u32[]{:S(2)}, u32[]{:S(2)}) async-start(f32[8,8,32,128]{3,2,1,0:T(8,128)} %shard_map.66), calls=%async_computation.1 | async-start | bytes 2097152 | tf_op jit(solution)/shard_map/all_to_all | solution.py:459
  104.5 2.7 %collective-permute-start.2 = (f32[10,32,1024]{2,1,0:T(8,128)}, f32[10,32,1024]{2,1,0:T(8,128)}, u32[]{:S(2)}, u32[]{:S(2)}) collective-permute-start(f32[10,32,1024]{2,1,0:T(8,128)} %get-tuple-element.23), channel_id=1, source_target_pairs={{0,8},{8,16},{16,24},{1,9},{9,17},{17,25},{2,10},{10,18},{18,26},{... | collective-permute-start | bytes 3932168 | tf_op jit(solution)/shard_map/ppermute | solution.py:30
  107.3 1.3 collective-permute-start.3
  108.6 3.4 %collective-permute-start = (f32[8,4,40,128]{3,2,1,0:T(8,128)}, f32[8,4,40,128]{3,2,1,0:T(8,128)S(1)}, u32[]{:S(2)}, u32[]{:S(2)}) collective-permute-start(f32[8,4,40,128]{3,2,1,0:T(8,128)} %get-tuple-element.21), channel_id=1, source_target_pairs={{0,8},{8,16},{16,24},{1,9},{9,17},{17,25},{2,10},{10,18},{18,26},{... | collective-permute-start | bytes 1966088 | tf_op jit(solution)/shard_map/ppermute | solution.py:30
  111.9 1.3 collective-permute-start.1
  113.2 4.2 %collective-permute-start.6 = (f32[54,1024]{1,0:T(8,128)S(1)}, f32[54,1024]{1,0:T(8,128)S(1)}, u32[]{:S(2)}, u32[]{:S(2)}) collective-permute-start(f32[54,1024]{1,0:T(8,128)S(1)} %copy-done.14), channel_id=1, source_target_pairs={{0,8},{8,16},{16,24},{1,9},{9,17},{17,25},{2,10},{10,18},{18,26},{... | collective-permute-start | bytes 663560 | tf_op jit(solution)/shard_map/ppermute | solution.py:30
  117.5 1.1 collective-permute-done.6.corners_below
  118.6 1.3 collective-permute-start.7
  119.9 0.6 add_convert_fusion.flags
  120.5 14.7 %collective-permute-done.7.corners_above = f32[54,1024]{1,0:T(8,128)S(1)} collective-permute-done((f32[54,1024]{1,0:T(8,128)S(1)}, f32[54,1024]{1,0:T(8,128)S(1)}, u32[]{:S(2)}, u32[]{:S(2)}) %collective-permute-start.7) | collective-permute-done | bytes 221216 | tf_op jit(solution)/shard_map/ppermute | solution.py:31
  135.1 0.7 copy-done.10
  135.9 6.4 %shard_map.63.ext.ext_ref = f32[3,8,14,40,128]{4,3,2,1,0:T(8,128)} custom-call(f32[3,8,32,1024]{3,2,1,0:T(8,128)} %vel.3, f32[10,32,1024]{2,1,0:T(8,128)} %collective-permute-done.2.planes_below, f32[10,32,1024]{2,1,0:T(8,128)} %collective-permute-done.3.planes_above, f32[80,1024]{1,0:T(8,128)} %copy-done, f32[80,1024]{1,0:T(8,128)} %copy-done.1, ...), custom_call_target="tpu_custom_call" | custom-call | bytes 4194304 | tf_op jit(solution)/shard_map/pallas_call | solution.py:527
  142.3 0.9 copy-done.2
  143.1 13.3 %shard_map.64 = (f32[8,8,32,128]{3,2,1,0:T(8,128)}, f32[3,8,10,40,128]{4,3,2,1,0:T(8,128)}) custom-call(f32[4]{0:T(128)} %add_convert_fusion.flags, f32[8,8,40,128]{3,2,1,0:T(8,128)} %all-to-all-done.field.own.start, f32[8,4,40,128]{3,2,1,0:T(8,128)} %copy-done.2, f32[8,4,40,128]{3,2,1,0:T(8,128)} %collective-permute-done.1.above.start_above, ...), custom_call_target="tpu_custom_call" | custom-call | flops 20971520 | bytes 4194304 | tf_op jit(solution)/shard_map/pallas_call | solution.py:536
  156.5 9.2 %shard_map.67 = (f32[3,8,32,1024]{3,2,1,0:T(8,128)}, f32[8,128]{1,0:T(8,128)}) custom-call(f32[8,8,32,128]{3,2,1,0:T(8,128)} %get-tuple-element.28.gate.moved, f32[3,8,14,40,128]{4,3,2,1,0:T(8,128)} %shard_map.63.ext.ext_ref, f32[8,32,1024]{2,1,0:T(8,128)} %sti.3, f32[10,32,1024]{2,1,0:T(8,128)} %collective-permute-done.2.planes_below, ...), custom_call_target="tpu_custom_call" | custom-call | flops 20971520 | bytes 4194304 | tf_op jit(solution)/shard_map/pallas_call | solution.py:545
  165.7 2.9 %shard_map.68 = (f32[8,8,32,128]{3,2,1,0:T(8,128)}, f32[8,8,4,128]{3,2,1,0:T(4,128)}, f32[8,8,4,128]{3,2,1,0:T(4,128)}, f32[8,128]{1,0:T(8,128)}) custom-call(f32[8,8,32,128]{3,2,1,0:T(8,128)} %get-tuple-element.28.gate.moved, f32[8,8,32,128]{3,2,1,0:T(8,128)} %all-to-all-done.1.fixed, f32[8,128]{1,0:T(8,128)} %get-tuple-element.29.sums), custom_call_target="tpu_custom_call" | custom-call | bytes 4194304 | tf_op jit(solution)/shard_map/pallas_call | solution.py:553
  168.6 3.9 %collective-permute-start.8 = (f32[8,8,4,128]{3,2,1,0:T(4,128)}, f32[8,8,4,128]{3,2,1,0:T(4,128)S(1)}, u32[]{:S(2)}, u32[]{:S(2)}) collective-permute-start(f32[8,8,4,128]{3,2,1,0:T(4,128)} %get-tuple-element.31), channel_id=1, source_target_pairs={{0,1},{1,2},{2,3},{3,4},{4,5},{5,6},{6,7},{8,9},{9,10},{10,11},{11... | collective-permute-start | bytes 393224 | tf_op jit(solution)/shard_map/ppermute | solution.py:30
  172.5 1.3 collective-permute-start.9
  173.8 1.5 collective-permute-done.8.before
  175.4 4.3 %collective-permute-done.9.after = f32[8,8,4,128]{3,2,1,0:T(4,128)S(1)} collective-permute-done((f32[8,8,4,128]{3,2,1,0:T(4,128)}, f32[8,8,4,128]{3,2,1,0:T(4,128)S(1)}, u32[]{:S(2)}, u32[]{:S(2)}) %collective-permute-start.9) | collective-permute-done | bytes 131104 | tf_op jit(solution)/shard_map/ppermute | solution.py:31
  179.6 0.6 copy-done.6
  180.3 2.3 %shard_map.69 = (f32[8,3,40,128]{3,2,1,0:T(8,128)}, f32[8,3,40,128]{3,2,1,0:T(8,128)}) custom-call(f32[8,8,32,128]{3,2,1,0:T(8,128)} %get-tuple-element.30.field.own, f32[8,8,4,128]{3,2,1,0:T(4,128)} %copy-done.5, f32[8,8,4,128]{3,2,1,0:T(4,128)} %copy-done.6), custom_call_target="tpu_custom_call" | custom-call | bytes 4194304 | tf_op jit(solution)/shard_map/pallas_call | solution.py:557
  182.6 5.7 %collective-permute-start.10 = (f32[8,3,40,128]{3,2,1,0:T(8,128)}, f32[8,3,40,128]{3,2,1,0:T(8,128)S(1)}, u32[]{:S(2)}, u32[]{:S(2)}) collective-permute-start(f32[8,3,40,128]{3,2,1,0:T(8,128)} %get-tuple-element.33), channel_id=1, source_target_pairs={{0,8},{8,16},{16,24},{1,9},{9,17},{17,25},{2,10},{10,18},{18,26},{... | collective-permute-start | bytes 1474568 | tf_op jit(solution)/shard_map/ppermute | solution.py:30
  188.3 1.3 collective-permute-start.11
  189.6 3.3 %collective-permute-start.14 = (f32[8,128]{1,0:T(8,128)}, f32[8,128]{1,0:T(8,128)S(1)}, u32[]{:S(2)}, u32[]{:S(2)}) collective-permute-start(f32[8,128]{1,0:T(8,128)} %shard_map.70), channel_id=1, source_target_pairs={{0,3},{1,2},{2,1},{3,0},{4,7},{5,6},{6,5},{7,4},{8,11},{9,10},{10,... | collective-permute-start | bytes 12296 | tf_op jit(solution)/shard_map/ppermute | solution.py:469
  193.0 0.5 collective-permute-start.13
  193.6 1.2 collective-permute-done.14
  194.8 2.0 collective-permute-done.13
  197.3 0.7 select_add_fusion
  198.0 2.4 %collective-permute-start.15 = (f32[8,128]{1,0:T(8,128)S(1)}, f32[8,128]{1,0:T(8,128)S(1)}, u32[]{:S(2)}, u32[]{:S(2)}) collective-permute-start(f32[8,128]{1,0:T(8,128)S(1)} %select_add_fusion), channel_id=1, source_target_pairs={{0,4},{1,5},{2,6},{3,7},{4,0},{5,1},{6,2},{7,3},{8,12},{9,13},{10,... | collective-permute-start | bytes 12296 | tf_op jit(solution)/shard_map/ppermute | solution.py:469
  200.4 2.1 collective-permute-done.15
  202.5 0.6 add.34.refs_0_
  203.1 0.8 copy-done.3
  203.9 0.8 copy-done.4
  204.7 3.5 %collective-permute-start.17 = (f32[8,128]{1,0:T(8,128)}, f32[8,128]{1,0:T(8,128)S(1)}, u32[]{:S(2)}, u32[]{:S(2)}) collective-permute-start(f32[8,128]{1,0:T(8,128)} %shard_map.71.gate), channel_id=1, source_target_pairs={{0,16},{8,24},{16,0},{24,8},{1,17},{9,25},{17,1},{25,9},{2,18},{10... | collective-permute-start | bytes 12296 | tf_op jit(solution)/shard_map/ppermute | solution.py:469
  208.3 13.9 %shard_map.72 = f32[3,8,32,1024]{3,2,1,0:T(8,128)} custom-call(f32[4]{0:T(128)} %add_convert_fusion.flags, f32[8,8,32,128]{3,2,1,0:T(8,128)} %get-tuple-element.30.field.own, f32[8,3,40,128]{3,2,1,0:T(8,128)} %copy-done.3, f32[8,3,40,128]{3,2,1,0:T(8,128)} %copy-done.4, f32[8,8,4,128]{3,2,1,0:T(4,128)} %copy-done.5, f32[8,8,4,128]{3,2,1,0:T(4,128)} %copy-done.6, ...), custom_call_target="tpu_custom_call" | custom-call | flops 20971520 | bytes 4194304 | tf_op jit(solution)/shard_map/pallas_call | solution.py:563
  222.2 0.6 add_reduce_fusion
  (42 shorter events, 0.8 us)
Async XLA Ops:
  8.5 7.4 %copy-start.13 = (f32[80,1024]{1,0:T(8,128)S(1)}, f32[80,1024]{1,0:T(8,128)}, u32[]{:S(2)}) copy-start(f32[80,1024]{1,0:T(8,128)} %get-tuple-element.25) | copy-start | bytes 983044
  8.5 11.4 %copy-start.7 = (f32[80,1024]{1,0:T(8,128)S(1)}, f32[80,1024]{1,0:T(8,128)}, u32[]{:S(2)}) copy-start(f32[80,1024]{1,0:T(8,128)} %get-tuple-element.20.gate) | copy-start | bytes 983044
  8.5 41.9 %all-to-all-start = ((f32[8,8,40,128]{3,2,1,0:T(8,128)}), f32[8,8,40,128]{3,2,1,0:T(8,128)}, u32[]{:S(2)}, u32[]{:S(2)}) async-start(f32[8,8,40,128]{3,2,1,0:T(8,128)} %shard_map.60), calls=%async_computation | async-start | bytes 2621440 | tf_op jit(solution)/shard_map/all_to_all | solution.py:459
  15.9 28.1 %collective-permute-start.4 = (f32[80,1024]{1,0:T(8,128)S(1)}, f32[80,1024]{1,0:T(8,128)S(1)}, u32[]{:S(2)}, u32[]{:S(2)}) collective-permute-start(f32[80,1024]{1,0:T(8,128)S(1)} %copy-done.13), channel_id=1, source_target_pairs={{0,1},{1,2},{2,3},{3,4},{4,5},{5,6},{6,7},{8,9},{9,10},{10,11},{11... | collective-permute-start | bytes 983048 | tf_op jit(solution)/shard_map/ppermute | solution.py:30
  19.8 24.1 %collective-permute-start.5 = (f32[80,1024]{1,0:T(8,128)S(1)}, f32[80,1024]{1,0:T(8,128)S(1)}, u32[]{:S(2)}, u32[]{:S(2)}) collective-permute-start(f32[80,1024]{1,0:T(8,128)S(1)} %copy-done.7), channel_id=1, source_target_pairs={{1,0},{2,1},{3,2},{4,3},{5,4},{6,5},{7,6},{9,8},{10,9},{11,10},{12... | collective-permute-start | bytes 983048 | tf_op jit(solution)/shard_map/ppermute | solution.py:31
  43.9 0.7 copy-start
  44.7 0.7 copy-start.1
  91.2 16.0 %copy-start.12 = (f32[10,32,1024]{2,1,0:T(8,128)S(1)}, f32[10,32,1024]{2,1,0:T(8,128)}, u32[]{:S(2)}) copy-start(f32[10,32,1024]{2,1,0:T(8,128)} %get-tuple-element.24) | copy-start | bytes 3932164
  91.2 22.0 %copy-start.14 = (f32[54,1024]{1,0:T(8,128)S(1)}, f32[54,1024]{1,0:T(8,128)}, u32[]{:S(2)}) copy-start(f32[54,1024]{1,0:T(8,128)} %get-tuple-element.26) | copy-start | bytes 663556
  91.3 27.3 %copy-start.8 = (f32[54,1024]{1,0:T(8,128)S(1)}, f32[54,1024]{1,0:T(8,128)}, u32[]{:S(2)}) copy-start(f32[54,1024]{1,0:T(8,128)} %get-tuple-element.27.gate) | copy-start | bytes 663556
  91.3 74.4 %all-to-all-start.1 = ((f32[8,8,32,128]{3,2,1,0:T(8,128)}), f32[8,8,32,128]{3,2,1,0:T(8,128)}, u32[]{:S(2)}, u32[]{:S(2)}) async-start(f32[8,8,32,128]{3,2,1,0:T(8,128)} %shard_map.66), calls=%async_computation.1 | async-start | bytes 2097152 | tf_op jit(solution)/shard_map/all_to_all | solution.py:459
  104.5 31.3 %collective-permute-start.2 = (f32[10,32,1024]{2,1,0:T(8,128)}, f32[10,32,1024]{2,1,0:T(8,128)}, u32[]{:S(2)}, u32[]{:S(2)}) collective-permute-start(f32[10,32,1024]{2,1,0:T(8,128)} %get-tuple-element.23), channel_id=1, source_target_pairs={{0,8},{8,16},{16,24},{1,9},{9,17},{17,25},{2,10},{10,18},{18,26},{... | collective-permute-start | bytes 3932168 | tf_op jit(solution)/shard_map/ppermute | solution.py:30
  107.3 28.6 %collective-permute-start.3 = (f32[10,32,1024]{2,1,0:T(8,128)S(1)}, f32[10,32,1024]{2,1,0:T(8,128)}, u32[]{:S(2)}, u32[]{:S(2)}) collective-permute-start(f32[10,32,1024]{2,1,0:T(8,128)S(1)} %copy-done.12), channel_id=1, source_target_pairs={{8,0},{16,8},{24,16},{9,1},{17,9},{25,17},{10,2},{18,10},{26,18},{... | collective-permute-start | bytes 3932168 | tf_op jit(solution)/shard_map/ppermute | solution.py:31
  108.6 33.7 %collective-permute-start = (f32[8,4,40,128]{3,2,1,0:T(8,128)}, f32[8,4,40,128]{3,2,1,0:T(8,128)S(1)}, u32[]{:S(2)}, u32[]{:S(2)}) collective-permute-start(f32[8,4,40,128]{3,2,1,0:T(8,128)} %get-tuple-element.21), channel_id=1, source_target_pairs={{0,8},{8,16},{16,24},{1,9},{9,17},{17,25},{2,10},{10,18},{18,26},{... | collective-permute-start | bytes 1966088 | tf_op jit(solution)/shard_map/ppermute | solution.py:30
  111.9 30.3 %collective-permute-start.1 = (f32[8,4,40,128]{3,2,1,0:T(8,128)}, f32[8,4,40,128]{3,2,1,0:T(8,128)}, u32[]{:S(2)}, u32[]{:S(2)}) collective-permute-start(f32[8,4,40,128]{3,2,1,0:T(8,128)} %get-tuple-element.22.refs_1_), channel_id=1, source_target_pairs={{8,0},{16,8},{24,16},{9,1},{17,9},{25,17},{10,2},{18,10},{26,18},{... | collective-permute-start | bytes 1966088 | tf_op jit(solution)/shard_map/ppermute | solution.py:31
  113.2 5.3 %collective-permute-start.6 = (f32[54,1024]{1,0:T(8,128)S(1)}, f32[54,1024]{1,0:T(8,128)S(1)}, u32[]{:S(2)}, u32[]{:S(2)}) collective-permute-start(f32[54,1024]{1,0:T(8,128)S(1)} %copy-done.14), channel_id=1, source_target_pairs={{0,8},{8,16},{16,24},{1,9},{9,17},{17,25},{2,10},{10,18},{18,26},{... | collective-permute-start | bytes 663560 | tf_op jit(solution)/shard_map/ppermute | solution.py:30
  118.6 17.3 %copy-start.9 = (f32[54,1024]{1,0:T(8,128)}, f32[54,1024]{1,0:T(8,128)S(1)}, u32[]{:S(2)}) copy-start(f32[54,1024]{1,0:T(8,128)S(1)} %collective-permute-done.6.corners_below) | copy-start | bytes 663556
  118.6 16.6 %collective-permute-start.7 = (f32[54,1024]{1,0:T(8,128)S(1)}, f32[54,1024]{1,0:T(8,128)S(1)}, u32[]{:S(2)}, u32[]{:S(2)}) collective-permute-start(f32[54,1024]{1,0:T(8,128)S(1)} %copy-done.8), channel_id=1, source_target_pairs={{8,0},{16,8},{24,16},{9,1},{17,9},{25,17},{10,2},{18,10},{26,18},{... | collective-permute-start | bytes 663560 | tf_op jit(solution)/shard_map/ppermute | solution.py:31
  135.1 0.7 copy-start.10
  142.2 0.9 copy-start.2
  168.6 6.7 %collective-permute-start.8 = (f32[8,8,4,128]{3,2,1,0:T(4,128)}, f32[8,8,4,128]{3,2,1,0:T(4,128)S(1)}, u32[]{:S(2)}, u32[]{:S(2)}) collective-permute-start(f32[8,8,4,128]{3,2,1,0:T(4,128)} %get-tuple-element.31), channel_id=1, source_target_pairs={{0,1},{1,2},{2,3},{3,4},{4,5},{5,6},{6,7},{8,9},{9,10},{10,11},{11... | collective-permute-start | bytes 393224 | tf_op jit(solution)/shard_map/ppermute | solution.py:30
  172.5 7.1 %collective-permute-start.9 = (f32[8,8,4,128]{3,2,1,0:T(4,128)}, f32[8,8,4,128]{3,2,1,0:T(4,128)S(1)}, u32[]{:S(2)}, u32[]{:S(2)}) collective-permute-start(f32[8,8,4,128]{3,2,1,0:T(4,128)} %get-tuple-element.32), channel_id=1, source_target_pairs={{1,0},{2,1},{3,2},{4,3},{5,4},{6,5},{7,6},{9,8},{10,9},{11,10},{12... | collective-permute-start | bytes 393224 | tf_op jit(solution)/shard_map/ppermute | solution.py:31
  175.4 4.3 %copy-start.5 = (f32[8,8,4,128]{3,2,1,0:T(4,128)}, f32[8,8,4,128]{3,2,1,0:T(4,128)S(1)}, u32[]{:S(2)}) copy-start(f32[8,8,4,128]{3,2,1,0:T(4,128)S(1)} %collective-permute-done.8.before) | copy-start | bytes 393220
  179.6 0.7 copy-start.6
  182.6 20.5 %collective-permute-start.10 = (f32[8,3,40,128]{3,2,1,0:T(8,128)}, f32[8,3,40,128]{3,2,1,0:T(8,128)S(1)}, u32[]{:S(2)}, u32[]{:S(2)}) collective-permute-start(f32[8,3,40,128]{3,2,1,0:T(8,128)} %get-tuple-element.33), channel_id=1, source_target_pairs={{0,8},{8,16},{16,24},{1,9},{9,17},{17,25},{2,10},{10,18},{18,26},{... | collective-permute-start | bytes 1474568 | tf_op jit(solution)/shard_map/ppermute | solution.py:30
  188.3 14.8 %collective-permute-start.11 = (f32[8,3,40,128]{3,2,1,0:T(8,128)}, f32[8,3,40,128]{3,2,1,0:T(8,128)S(1)}, u32[]{:S(2)}, u32[]{:S(2)}) collective-permute-start(f32[8,3,40,128]{3,2,1,0:T(8,128)} %get-tuple-element.34.refs_1_), channel_id=1, source_target_pairs={{8,0},{16,8},{24,16},{9,1},{17,9},{25,17},{10,2},{18,10},{26,18},{... | collective-permute-start | bytes 1474568 | tf_op jit(solution)/shard_map/ppermute | solution.py:31
  189.6 5.1 %collective-permute-start.14 = (f32[8,128]{1,0:T(8,128)}, f32[8,128]{1,0:T(8,128)S(1)}, u32[]{:S(2)}, u32[]{:S(2)}) collective-permute-start(f32[8,128]{1,0:T(8,128)} %shard_map.70), channel_id=1, source_target_pairs={{0,3},{1,2},{2,1},{3,0},{4,7},{5,6},{6,5},{7,4},{8,11},{9,10},{10,... | collective-permute-start | bytes 12296 | tf_op jit(solution)/shard_map/ppermute | solution.py:469
  193.0 3.8 %collective-permute-start.13 = (f32[8,128]{1,0:T(8,128)}, f32[8,128]{1,0:T(8,128)S(1)}, u32[]{:S(2)}, u32[]{:S(2)}) collective-permute-start(f32[8,128]{1,0:T(8,128)} %shard_map.70), channel_id=1, source_target_pairs={{0,2},{1,3},{2,0},{3,1},{4,6},{5,7},{6,4},{7,5},{8,10},{9,11},{10,... | collective-permute-start | bytes 12296 | tf_op jit(solution)/shard_map/ppermute | solution.py:469
  193.5 3.8 %collective-permute-start.12 = (f32[8,128]{1,0:T(8,128)}, f32[8,128]{1,0:T(8,128)S(1)}, u32[]{:S(2)}, u32[]{:S(2)}) collective-permute-start(f32[8,128]{1,0:T(8,128)} %shard_map.70), channel_id=1, source_target_pairs={{0,1},{1,0},{2,3},{3,2},{4,5},{5,4},{6,7},{7,6},{8,9},{9,8},{10,11... | collective-permute-start | bytes 12296 | tf_op jit(solution)/shard_map/ppermute | solution.py:469
  198.0 4.5 %collective-permute-start.15 = (f32[8,128]{1,0:T(8,128)S(1)}, f32[8,128]{1,0:T(8,128)S(1)}, u32[]{:S(2)}, u32[]{:S(2)}) collective-permute-start(f32[8,128]{1,0:T(8,128)S(1)} %select_add_fusion), channel_id=1, source_target_pairs={{0,4},{1,5},{2,6},{3,7},{4,0},{5,1},{6,2},{7,3},{8,12},{9,13},{10,... | collective-permute-start | bytes 12296 | tf_op jit(solution)/shard_map/ppermute | solution.py:469
  203.1 0.8 copy-start.3
  203.9 0.8 copy-start.4
  204.7 17.5 %collective-permute-start.18 = (f32[8,128]{1,0:T(8,128)}, f32[8,128]{1,0:T(8,128)S(1)}, u32[]{:S(2)}, u32[]{:S(2)}) collective-permute-start(f32[8,128]{1,0:T(8,128)} %shard_map.71.gate), channel_id=1, source_target_pairs={{0,24},{8,16},{16,8},{24,0},{1,25},{9,17},{17,9},{25,1},{2,26},{10... | collective-permute-start | bytes 12296 | tf_op jit(solution)/shard_map/ppermute | solution.py:469
  204.7 17.5 %collective-permute-start.17 = (f32[8,128]{1,0:T(8,128)}, f32[8,128]{1,0:T(8,128)S(1)}, u32[]{:S(2)}, u32[]{:S(2)}) collective-permute-start(f32[8,128]{1,0:T(8,128)} %shard_map.71.gate), channel_id=1, source_target_pairs={{0,16},{8,24},{16,0},{24,8},{1,17},{9,25},{17,1},{25,9},{2,18},{10... | collective-permute-start | bytes 12296 | tf_op jit(solution)/shard_map/ppermute | solution.py:469
  208.2 14.0 %collective-permute-start.16 = (f32[8,128]{1,0:T(8,128)}, f32[8,128]{1,0:T(8,128)S(1)}, u32[]{:S(2)}, u32[]{:S(2)}) collective-permute-start(f32[8,128]{1,0:T(8,128)} %shard_map.71.gate), channel_id=1, source_target_pairs={{0,8},{8,0},{16,24},{24,16},{1,9},{9,1},{17,25},{25,17},{2,10},{10... | collective-permute-start | bytes 12296 | tf_op jit(solution)/shard_map/ppermute | solution.py:469
  208.3 13.9 %copy-start.11 = (f32[8,128]{1,0:T(8,128)S(1)}, f32[8,128]{1,0:T(8,128)}, u32[]{:S(2)}) copy-start(f32[8,128]{1,0:T(8,128)} %shard_map.71.gate) | copy-start | bytes 12292

commit v4 on v3

--- a/solution.py
+++ b/solution.py
@@ -86,16 +86,18 @@
     lax.fori_loop(0, sections, section, 0)
 
 
-def slice_kernel(field, low, high, sem):
-    sections, width = field.shape[1], low.shape[1]
-    copies = [
-        pltpu.make_async_copy(field.at[:, pl.ds(0, width)], low, sem.at[0]),
-        pltpu.make_async_copy(field.at[:, pl.ds(sections - width, width)], high, sem.at[1]),
-    ]
-    for copy in copies:
-        copy.start()
-    for copy in copies:
-        copy.wait()
+def slice_kernel(field, gate_below, gate_above, low, high):
+    del gate_below, gate_above
+    blocks, sections = field.shape[:2]
+    width = low.shape[1]
+
+    def plane(z, _):
+        for out, at in ((low, z), (high, z + sections - width)):
+            for i in range(blocks):
+                out[i, z, :, :] = field[i, at, :, :]
+        return 0
+
+    lax.fori_loop(0, width, plane, 0)
 
 
 def plane_kernel(field, before, after, low, high):
@@ -529,7 +531,9 @@
     )
 
     fixed_blocks = to_blocks(reference_scan, 0, corners[0])
-    low, high = call(slice_kernel, [(blocks, STEPS, tall, LANES)] * 2, [ANY], [2], [ANY] * 2)(template)
+    low, high = call(slice_kernel, [(blocks, STEPS, tall, LANES)] * 2, [VMEM, ANY, ANY])(
+        template, below, above
+    )
     start = (template,) + exchange(low, high, "sec")
     fixed = to_rows(after(fixed_blocks, low))
     level = (blocks, sections + 2 * STEPS, tall, LANES)
@@ -556,8 +560,9 @@
     before, after_ = exchange(low_rows, high_rows, "row")
     low, high = call(plane_kernel, [(blocks, WIDE, tall, LANES)] * 2, [VMEM] * 3)(misfit, before, after_)
     below, above = exchange(low, high, "sec")
-    partial = after(partial, low)
-    for stage in stages("row"):
+    along = stages("row")
+    partial = after(summed(partial, *along[0]), low)
+    for stage in along[1:]:
         partial = summed(partial, *stage)
     partial = after(partial, below, above)
     (gradient,) = call(

time: 225 us -> 169 us (0.75)
  Pallas kernels: 102 us -> 63.3 us
  waiting for transfers between devices: 50.2 us -> 33.7 us
    pallas_call x1, Pallas kernels: 40.8 us -> 2.47 us  [local(): call(slice_kernel, [(blocks, STEPS, tall, LANES)] * 2, [VMEM, ANY, ANY])]
    ppermute x6, waiting for transfers between devices: 18.9 us -> 7.05 us  [exchange(): above = lax.ppermute(low_part, axis, [(i + 1, i) for i in range(count - 1)])]
    ppermute x6, waiting for transfers between devices: 25.4 us -> 20.4 us  [exchange(): lax.ppermute(high_part, axis, [(i, i + 1) for i in range(count - 1)])]
    unnamed x30 -> x28, local copies, waits for them, and re-layouts: 5.3 us -> 4.54 us
  transfers between devices with their start and end apart: 21 -> 21, of which waited for: 9 -> 8; matrix products, arithmetic and copies ran while one was open for 1% -> 1% of each run, Pallas kernels for 21% -> 28%
where the time goes in v4:
time: 169 us; the launch traced here: 168 us
  Pallas kernels  63.3 us (37%)
  starting transfers between devices  61.1 us (36%)
  waiting for transfers between devices  33.7 us (20%)
  local copies, waits for them, and re-layouts  4.54 us (3%)
  other arithmetic  3.1 us (2%)
  between operations  2.64 us (2%)
    ppermute x6, starting transfers between devices, exchange(): lax.ppermute(high_part, axis, [(i, i + 1) for i in range(count - 1)])  23 us
    all_to_all x2, starting transfers between devices, to_rows(): lax.all_to_all(parts, 'row', split_axis=0, concat_axis=0, tiled=True)  20.8 us
    ppermute x6, waiting for transfers between devices, exchange(): lax.ppermute(high_part, axis, [(i, i + 1) for i in range(count - 1)])  20.4 us
    pallas_call x1, Pallas kernels, local(): call(adjoint_kernel, [velocity.shape], [SMEM] + [VMEM] * 5 + [ANY] * 7, [...  13.8 us
    pallas_call x1, Pallas kernels, local(): call(forward_kernel, [own, (STEPS - 1, blocks, sections + 2, tall, LANES)...  13.3 us
    ppermute x7, starting transfers between devices, summed(): lax.ppermute(part, axis, [(i, i ^ low) for i in range(count)])  9.53 us
    pallas_call x1, Pallas kernels, local(): call(regular_kernel, [velocity.shape, (TILE, LANES)], [ANY] + [VMEM] * 6,...  9.21 us
    ppermute x6, starting transfers between devices, exchange(): above = lax.ppermute(low_part, axis, [(i + 1, i) for i in range(count - 1)])  7.74 us
  transfers between devices with their start and end apart: 21, of which 8 were waited for; matrix products, arithmetic and copies ran while one was open for 1% of the time, Pallas kernels for 28%

profile of v4, /device:TPU:0, one launch (start us, length us, event | category | flops | bytes accessed | tf_op | source)
XLA Modules:
  0.0 168.3 jit_solution(7283971153641458023)
XLA Ops:
  0.6 4.5 %shard_map.59 = (f32[80,1024]{1,0:T(8,128)}, f32[80,1024]{1,0:T(8,128)}, f32[10,32,1024]{2,1,0:T(8,128)}, f32[10,32,1024]{2,1,0:T(8,128)}) custom-call(f32[3,8,32,1024]{3,2,1,0:T(8,128)} %vel.3, f32[8,32,1024]{2,1,0:T(8,128)} %sti.3), custom_call_target="tpu_custom_call" | custom-call | bytes 4194304 | tf_op jit(solution)/shard_map/pallas_call | solution.py:518
  5.2 3.3 %shard_map.60 = f32[8,8,40,128]{3,2,1,0:T(8,128)} custom-call(f32[8,128,256]{2,1,0:T(8,128)} %scan.2, f32[80,1024]{1,0:T(8,128)} %get-tuple-element.20.gate), custom_call_target="tpu_custom_call" | custom-call | bytes 4194304 | tf_op jit(solution)/shard_map/pallas_call | solution.py:453
  8.4 7.4 %all-to-all-start = ((f32[8,8,40,128]{3,2,1,0:T(8,128)}), f32[8,8,40,128]{3,2,1,0:T(8,128)}, u32[]{:S(2)}, u32[]{:S(2)}) async-start(f32[8,8,40,128]{3,2,1,0:T(8,128)} %shard_map.60), calls=%async_computation | async-start | bytes 2621440 | tf_op jit(solution)/shard_map/all_to_all | solution.py:461
  15.8 2.5 %collective-permute-start = (f32[10,32,1024]{2,1,0:T(8,128)}, f32[10,32,1024]{2,1,0:T(8,128)}, u32[]{:S(2)}, u32[]{:S(2)}) collective-permute-start(f32[10,32,1024]{2,1,0:T(8,128)} %get-tuple-element.21), channel_id=1, source_target_pairs={{0,8},{8,16},{16,24},{1,9},{9,17},{17,25},{2,10},{10,18},{18,26},{... | collective-permute-start | bytes 3932168 | tf_op jit(solution)/shard_map/ppermute | solution.py:30
  18.4 1.3 collective-permute-start.1
  19.7 3.8 %collective-permute-start.4 = (f32[80,1024]{1,0:T(8,128)S(1)}, f32[80,1024]{1,0:T(8,128)S(1)}, u32[]{:S(2)}, u32[]{:S(2)}) collective-permute-start(f32[80,1024]{1,0:T(8,128)S(1)} %copy-done.12), channel_id=1, source_target_pairs={{0,1},{1,2},{2,3},{3,4},{4,5},{5,6},{6,7},{8,9},{9,10},{10,11},{11... | collective-permute-start | bytes 983048 | tf_op jit(solution)/shard_map/ppermute | solution.py:30
  23.5 1.3 collective-permute-start.5
  24.8 18.9 %collective-permute-done.4.before = f32[80,1024]{1,0:T(8,128)S(1)} collective-permute-done((f32[80,1024]{1,0:T(8,128)S(1)}, f32[80,1024]{1,0:T(8,128)S(1)}, u32[]{:S(2)}, u32[]{:S(2)}) %collective-permute-start.4) | collective-permute-done | bytes 327712 | tf_op jit(solution)/shard_map/ppermute | solution.py:30
  43.7 0.7 copy-done
  44.4 0.7 copy-done.1
  45.1 2.0 %shard_map.62 = (f32[54,1024]{1,0:T(8,128)}, f32[54,1024]{1,0:T(8,128)}) custom-call(f32[80,1024]{1,0:T(8,128)} %copy-done, f32[80,1024]{1,0:T(8,128)} %copy-done.1), custom_call_target="tpu_custom_call" | custom-call | bytes 4194304 | tf_op jit(solution)/shard_map/pallas_call | solution.py:528
  47.1 3.0 %shard_map.65.refs_0_ = f32[8,8,32,128]{3,2,1,0:T(8,128)} custom-call(f32[8,128,256]{2,1,0:T(8,128)} %scan.3, f32[54,1024]{1,0:T(8,128)} %get-tuple-element.27.gate), custom_call_target="tpu_custom_call" | custom-call | bytes 4194304 | tf_op jit(solution)/shard_map/pallas_call | solution.py:453
  50.1 2.5 %shard_map.61 = (f32[8,4,40,128]{3,2,1,0:T(8,128)}, f32[8,4,40,128]{3,2,1,0:T(8,128)}) custom-call(f32[8,8,40,128]{3,2,1,0:T(8,128)} %all-to-all-done.field.own.start, f32[10,32,1024]{2,1,0:T(8,128)} %collective-permute-done.gate_below.planes_below, f32[10,32,1024]{2,1,0:T(8,128)} %collective-permute-done.1.gate_above.planes_above), custom_call_target="tpu_custom_call" | custom-call | bytes 4194304 | tf_op jit(solution)/shard_map/pallas_call | solution.py:534
  52.6 13.4 %all-to-all-start.1 = ((f32[8,8,32,128]{3,2,1,0:T(8,128)}), f32[8,8,32,128]{3,2,1,0:T(8,128)}, u32[]{:S(2)}, u32[]{:S(2)}) async-start(f32[8,8,32,128]{3,2,1,0:T(8,128)} %shard_map.66), calls=%async_computation.1 | async-start | bytes 2097152 | tf_op jit(solution)/shard_map/all_to_all | solution.py:461
  66.0 1.7 collective-permute-start.2
  67.7 1.3 collective-permute-start.3
  69.0 4.4 %collective-permute-start.6 = (f32[54,1024]{1,0:T(8,128)S(1)}, f32[54,1024]{1,0:T(8,128)S(1)}, u32[]{:S(2)}, u32[]{:S(2)}) collective-permute-start(f32[54,1024]{1,0:T(8,128)S(1)} %copy-done.13), channel_id=1, source_target_pairs={{0,8},{8,16},{16,24},{1,9},{9,17},{17,25},{2,10},{10,18},{18,26},{... | collective-permute-start | bytes 663560 | tf_op jit(solution)/shard_map/ppermute | solution.py:30
  73.4 1.3 collective-permute-start.7
  74.7 0.6 add_convert_fusion.flags
  75.4 2.8 %collective-permute-done.7.corners_above = f32[54,1024]{1,0:T(8,128)} collective-permute-done((f32[54,1024]{1,0:T(8,128)S(1)}, f32[54,1024]{1,0:T(8,128)}, u32[]{:S(2)}, u32[]{:S(2)}) %collective-permute-start.7) | collective-permute-done | bytes 221216 | tf_op jit(solution)/shard_map/ppermute | solution.py:31
  78.2 6.4 %shard_map.63.ext.ext_ref = f32[3,8,14,40,128]{4,3,2,1,0:T(8,128)} custom-call(f32[3,8,32,1024]{3,2,1,0:T(8,128)} %vel.3, f32[10,32,1024]{2,1,0:T(8,128)} %collective-permute-done.gate_below.planes_below, f32[10,32,1024]{2,1,0:T(8,128)} %collective-permute-done.1.gate_above.planes_above, f32[80,1024]{1,0:T(8,128)} %copy-done, f32[80,1024]{1,0:T(8,128)} %copy-done.1, ...), custom_call_target="tpu_custom_call" | custom-call | bytes 4194304 | tf_op jit(solution)/shard_map/pallas_call | solution.py:529
  84.6 0.9 copy-done.2
  85.4 13.3 %shard_map.64 = (f32[8,8,32,128]{3,2,1,0:T(8,128)}, f32[3,8,10,40,128]{4,3,2,1,0:T(8,128)}) custom-call(f32[4]{0:T(128)} %add_convert_fusion.flags, f32[8,8,40,128]{3,2,1,0:T(8,128)} %all-to-all-done.field.own.start, f32[8,4,40,128]{3,2,1,0:T(8,128)} %copy-done.2, f32[8,4,40,128]{3,2,1,0:T(8,128)} %collective-permute-done.3.above.start_above, ...), custom_call_target="tpu_custom_call" | custom-call | flops 20971520 | bytes 4194304 | tf_op jit(solution)/shard_map/pallas_call | solution.py:540
  98.8 9.2 %shard_map.67 = (f32[3,8,32,1024]{3,2,1,0:T(8,128)}, f32[8,128]{1,0:T(8,128)}) custom-call(f32[8,8,32,128]{3,2,1,0:T(8,128)} %get-tuple-element.28.gate.moved, f32[3,8,14,40,128]{4,3,2,1,0:T(8,128)} %shard_map.63.ext.ext_ref, f32[8,32,1024]{2,1,0:T(8,128)} %sti.3, f32[10,32,1024]{2,1,0:T(8,128)} %collective-permute-done.gate_below.planes_below, ...), custom_call_target="tpu_custom_call" | custom-call | flops 20971520 | bytes 4194304 | tf_op jit(solution)/shard_map/pallas_call | solution.py:549
  108.0 2.9 %shard_map.68 = (f32[8,8,32,128]{3,2,1,0:T(8,128)}, f32[8,8,4,128]{3,2,1,0:T(4,128)}, f32[8,8,4,128]{3,2,1,0:T(4,128)}, f32[8,128]{1,0:T(8,128)}) custom-call(f32[8,8,32,128]{3,2,1,0:T(8,128)} %get-tuple-element.28.gate.moved, f32[8,8,32,128]{3,2,1,0:T(8,128)} %all-to-all-done.1.fixed, f32[8,128]{1,0:T(8,128)} %get-tuple-element.29.sums), custom_call_target="tpu_custom_call" | custom-call | bytes 4194304 | tf_op jit(solution)/shard_map/pallas_call | solution.py:557
  110.9 4.1 %collective-permute-start.8 = (f32[8,8,4,128]{3,2,1,0:T(4,128)}, f32[8,8,4,128]{3,2,1,0:T(4,128)S(1)}, u32[]{:S(2)}, u32[]{:S(2)}) collective-permute-start(f32[8,8,4,128]{3,2,1,0:T(4,128)} %get-tuple-element.31), channel_id=1, source_target_pairs={{0,1},{1,2},{2,3},{3,4},{4,5},{5,6},{6,7},{8,9},{9,10},{10,11},{11... | collective-permute-start | bytes 393224 | tf_op jit(solution)/shard_map/ppermute | solution.py:30
  115.0 1.3 collective-permute-start.9
  116.3 1.5 collective-permute-done.8.before
  117.8 4.3 %collective-permute-done.9.after = f32[8,8,4,128]{3,2,1,0:T(4,128)S(1)} collective-permute-done((f32[8,8,4,128]{3,2,1,0:T(4,128)}, f32[8,8,4,128]{3,2,1,0:T(4,128)S(1)}, u32[]{:S(2)}, u32[]{:S(2)}) %collective-permute-start.9) | collective-permute-done | bytes 131104 | tf_op jit(solution)/shard_map/ppermute | solution.py:31
  122.0 0.6 copy-done.6
  122.7 2.4 %shard_map.69 = (f32[8,3,40,128]{3,2,1,0:T(8,128)}, f32[8,3,40,128]{3,2,1,0:T(8,128)}) custom-call(f32[8,8,32,128]{3,2,1,0:T(8,128)} %get-tuple-element.30.field.own, f32[8,8,4,128]{3,2,1,0:T(4,128)} %copy-done.5, f32[8,8,4,128]{3,2,1,0:T(4,128)} %copy-done.6), custom_call_target="tpu_custom_call" | custom-call | bytes 4194304 | tf_op jit(solution)/shard_map/pallas_call | solution.py:561
  125.0 6.6 %collective-permute-start.10 = (f32[8,3,40,128]{3,2,1,0:T(8,128)}, f32[8,3,40,128]{3,2,1,0:T(8,128)S(1)}, u32[]{:S(2)}, u32[]{:S(2)}) collective-permute-start(f32[8,3,40,128]{3,2,1,0:T(8,128)} %get-tuple-element.33), channel_id=1, source_target_pairs={{0,8},{8,16},{16,24},{1,9},{9,17},{17,25},{2,10},{10,18},{18,26},{... | collective-permute-start | bytes 1474568 | tf_op jit(solution)/shard_map/ppermute | solution.py:30
  131.6 1.3 collective-permute-start.11
  132.9 3.6 %collective-permute-start.14 = (f32[8,128]{1,0:T(8,128)S(1)}, f32[8,128]{1,0:T(8,128)S(1)}, u32[]{:S(2)}, u32[]{:S(2)}) collective-permute-start(f32[8,128]{1,0:T(8,128)S(1)} %copy-done.11), channel_id=1, source_target_pairs={{0,3},{1,2},{2,1},{3,0},{4,7},{5,6},{6,5},{7,4},{8,11},{9,10},{10,... | collective-permute-start | bytes 12296 | tf_op jit(solution)/shard_map/ppermute | solution.py:471
  136.5 0.5 collective-permute-start.13
  137.1 0.1 collective-permute-start.12
  137.2 0.9 collective-permute-done.14
  138.1 2.0 %collective-permute-done.13 = f32[8,128]{1,0:T(8,128)S(1)} collective-permute-done((f32[8,128]{1,0:T(8,128)S(1)}, f32[8,128]{1,0:T(8,128)S(1)}, u32[]{:S(2)}, u32[]{:S(2)}) %collective-permute-start.13) | collective-permute-done | bytes 4128 | tf_op jit(solution)/shard_map/ppermute | solution.py:471
  140.1 0.5 collective-permute-done.12
  140.7 0.6 select_add_fusion.refs_0_
  141.3 2.1 %collective-permute-start.15 = (f32[8,128]{1,0:T(8,128)}, f32[8,128]{1,0:T(8,128)S(1)}, u32[]{:S(2)}, u32[]{:S(2)}) collective-permute-start(f32[8,128]{1,0:T(8,128)} %shard_map.70), channel_id=1, source_target_pairs={{0,4},{1,5},{2,6},{3,7},{4,0},{5,1},{6,2},{7,3},{8,12},{9,13},{10,... | collective-permute-start | bytes 12296 | tf_op jit(solution)/shard_map/ppermute | solution.py:471
  143.4 2.6 %collective-permute-done.15 = f32[8,128]{1,0:T(8,128)S(1)} collective-permute-done((f32[8,128]{1,0:T(8,128)}, f32[8,128]{1,0:T(8,128)S(1)}, u32[]{:S(2)}, u32[]{:S(2)}) %collective-permute-start.15) | collective-permute-done | bytes 4128 | tf_op jit(solution)/shard_map/ppermute | solution.py:471
  146.0 1.3 add.34.refs_0_
  147.3 0.8 copy-done.3
  148.1 0.8 copy-done.4
  148.8 3.1 %collective-permute-start.17 = (f32[8,128]{1,0:T(8,128)}, f32[8,128]{1,0:T(8,128)S(1)}, u32[]{:S(2)}, u32[]{:S(2)}) collective-permute-start(f32[8,128]{1,0:T(8,128)} %shard_map.71.gate), channel_id=1, source_target_pairs={{0,16},{8,24},{16,0},{24,8},{1,17},{9,25},{17,1},{25,9},{2,18},{10... | collective-permute-start | bytes 12296 | tf_op jit(solution)/shard_map/ppermute | solution.py:471
  152.1 13.8 %shard_map.72 = f32[3,8,32,1024]{3,2,1,0:T(8,128)} custom-call(f32[4]{0:T(128)} %add_convert_fusion.flags, f32[8,8,32,128]{3,2,1,0:T(8,128)} %get-tuple-element.30.field.own, f32[8,3,40,128]{3,2,1,0:T(8,128)} %copy-done.3, f32[8,3,40,128]{3,2,1,0:T(8,128)} %copy-done.4, f32[8,8,4,128]{3,2,1,0:T(4,128)} %copy-done.5, f32[8,8,4,128]{3,2,1,0:T(4,128)} %copy-done.6, ...), custom_call_target="tpu_custom_call" | custom-call | flops 20971520 | bytes 4194304 | tf_op jit(solution)/shard_map/pallas_call | solution.py:568
  165.9 0.6 add_reduce_fusion
  (40 shorter events, 0.2 us)
Async XLA Ops:
  8.4 11.2 %copy-start.12 = (f32[80,1024]{1,0:T(8,128)S(1)}, f32[80,1024]{1,0:T(8,128)}, u32[]{:S(2)}) copy-start(f32[80,1024]{1,0:T(8,128)} %get-tuple-element.25) | copy-start | bytes 983044
  8.4 15.0 %copy-start.7 = (f32[80,1024]{1,0:T(8,128)S(1)}, f32[80,1024]{1,0:T(8,128)}, u32[]{:S(2)}) copy-start(f32[80,1024]{1,0:T(8,128)} %get-tuple-element.20.gate) | copy-start | bytes 983044
  8.4 41.7 %all-to-all-start = ((f32[8,8,40,128]{3,2,1,0:T(8,128)}), f32[8,8,40,128]{3,2,1,0:T(8,128)}, u32[]{:S(2)}, u32[]{:S(2)}) async-start(f32[8,8,40,128]{3,2,1,0:T(8,128)} %shard_map.60), calls=%async_computation | async-start | bytes 2621440 | tf_op jit(solution)/shard_map/all_to_all | solution.py:461
  15.8 34.3 %collective-permute-start = (f32[10,32,1024]{2,1,0:T(8,128)}, f32[10,32,1024]{2,1,0:T(8,128)}, u32[]{:S(2)}, u32[]{:S(2)}) collective-permute-start(f32[10,32,1024]{2,1,0:T(8,128)} %get-tuple-element.21), channel_id=1, source_target_pairs={{0,8},{8,16},{16,24},{1,9},{9,17},{17,25},{2,10},{10,18},{18,26},{... | collective-permute-start | bytes 3932168 | tf_op jit(solution)/shard_map/ppermute | solution.py:30
  18.4 31.7 %collective-permute-start.1 = (f32[10,32,1024]{2,1,0:T(8,128)}, f32[10,32,1024]{2,1,0:T(8,128)}, u32[]{:S(2)}, u32[]{:S(2)}) collective-permute-start(f32[10,32,1024]{2,1,0:T(8,128)} %get-tuple-element.22), channel_id=1, source_target_pairs={{8,0},{16,8},{24,16},{9,1},{17,9},{25,17},{10,2},{18,10},{26,18},{... | collective-permute-start | bytes 3932168 | tf_op jit(solution)/shard_map/ppermute | solution.py:31
  19.7 24.0 %collective-permute-start.4 = (f32[80,1024]{1,0:T(8,128)S(1)}, f32[80,1024]{1,0:T(8,128)S(1)}, u32[]{:S(2)}, u32[]{:S(2)}) collective-permute-start(f32[80,1024]{1,0:T(8,128)S(1)} %copy-done.12), channel_id=1, source_target_pairs={{0,1},{1,2},{2,3},{3,4},{4,5},{5,6},{6,7},{8,9},{9,10},{10,11},{11... | collective-permute-start | bytes 983048 | tf_op jit(solution)/shard_map/ppermute | solution.py:30
  23.5 20.2 %collective-permute-start.5 = (f32[80,1024]{1,0:T(8,128)S(1)}, f32[80,1024]{1,0:T(8,128)S(1)}, u32[]{:S(2)}, u32[]{:S(2)}) collective-permute-start(f32[80,1024]{1,0:T(8,128)S(1)} %copy-done.7), channel_id=1, source_target_pairs={{1,0},{2,1},{3,2},{4,3},{5,4},{6,5},{7,6},{9,8},{10,9},{11,10},{12... | collective-permute-start | bytes 983048 | tf_op jit(solution)/shard_map/ppermute | solution.py:31
  43.7 0.7 copy-start
  44.4 0.7 copy-start.1
  52.6 16.4 %copy-start.13 = (f32[54,1024]{1,0:T(8,128)S(1)}, f32[54,1024]{1,0:T(8,128)}, u32[]{:S(2)}) copy-start(f32[54,1024]{1,0:T(8,128)} %get-tuple-element.26) | copy-start | bytes 663556
  52.6 20.8 %copy-start.8 = (f32[54,1024]{1,0:T(8,128)S(1)}, f32[54,1024]{1,0:T(8,128)}, u32[]{:S(2)}) copy-start(f32[54,1024]{1,0:T(8,128)} %get-tuple-element.27.gate) | copy-start | bytes 663556
  52.6 55.4 %all-to-all-start.1 = ((f32[8,8,32,128]{3,2,1,0:T(8,128)}), f32[8,8,32,128]{3,2,1,0:T(8,128)}, u32[]{:S(2)}, u32[]{:S(2)}) async-start(f32[8,8,32,128]{3,2,1,0:T(8,128)} %shard_map.66), calls=%async_computation.1 | async-start | bytes 2097152 | tf_op jit(solution)/shard_map/all_to_all | solution.py:461
  66.0 18.5 %collective-permute-start.2 = (f32[8,4,40,128]{3,2,1,0:T(8,128)}, f32[8,4,40,128]{3,2,1,0:T(8,128)S(1)}, u32[]{:S(2)}, u32[]{:S(2)}) collective-permute-start(f32[8,4,40,128]{3,2,1,0:T(8,128)} %get-tuple-element.23), channel_id=1, source_target_pairs={{0,8},{8,16},{16,24},{1,9},{9,17},{17,25},{2,10},{10,18},{18,26},{... | collective-permute-start | bytes 1966088 | tf_op jit(solution)/shard_map/ppermute | solution.py:30
  67.7 16.8 %collective-permute-start.3 = (f32[8,4,40,128]{3,2,1,0:T(8,128)}, f32[8,4,40,128]{3,2,1,0:T(8,128)}, u32[]{:S(2)}, u32[]{:S(2)}) collective-permute-start(f32[8,4,40,128]{3,2,1,0:T(8,128)} %get-tuple-element.24.refs_1_), channel_id=1, source_target_pairs={{8,0},{16,8},{24,16},{9,1},{17,9},{25,17},{10,2},{18,10},{26,18},{... | collective-permute-start | bytes 1966088 | tf_op jit(solution)/shard_map/ppermute | solution.py:31
  69.0 6.4 %collective-permute-start.6 = (f32[54,1024]{1,0:T(8,128)S(1)}, f32[54,1024]{1,0:T(8,128)S(1)}, u32[]{:S(2)}, u32[]{:S(2)}) collective-permute-start(f32[54,1024]{1,0:T(8,128)S(1)} %copy-done.13), channel_id=1, source_target_pairs={{0,8},{8,16},{16,24},{1,9},{9,17},{17,25},{2,10},{10,18},{18,26},{... | collective-permute-start | bytes 663560 | tf_op jit(solution)/shard_map/ppermute | solution.py:30
  73.4 4.7 %collective-permute-start.7 = (f32[54,1024]{1,0:T(8,128)S(1)}, f32[54,1024]{1,0:T(8,128)}, u32[]{:S(2)}, u32[]{:S(2)}) collective-permute-start(f32[54,1024]{1,0:T(8,128)S(1)} %copy-done.8), channel_id=1, source_target_pairs={{8,0},{16,8},{24,16},{9,1},{17,9},{25,17},{10,2},{18,10},{26,18},{... | collective-permute-start | bytes 663560 | tf_op jit(solution)/shard_map/ppermute | solution.py:31
  75.4 2.8 %copy-start.9 = (f32[54,1024]{1,0:T(8,128)}, f32[54,1024]{1,0:T(8,128)S(1)}, u32[]{:S(2)}) copy-start(f32[54,1024]{1,0:T(8,128)S(1)} %collective-permute-done.6.corners_below) | copy-start | bytes 663556
  84.6 0.9 copy-start.2
  110.9 22.0 %copy-start.11 = (f32[8,128]{1,0:T(8,128)S(1)}, f32[8,128]{1,0:T(8,128)}, u32[]{:S(2)}) copy-start(f32[8,128]{1,0:T(8,128)} %get-tuple-element.37) | copy-start | bytes 12292
  110.9 6.9 %collective-permute-start.8 = (f32[8,8,4,128]{3,2,1,0:T(4,128)}, f32[8,8,4,128]{3,2,1,0:T(4,128)S(1)}, u32[]{:S(2)}, u32[]{:S(2)}) collective-permute-start(f32[8,8,4,128]{3,2,1,0:T(4,128)} %get-tuple-element.31), channel_id=1, source_target_pairs={{0,1},{1,2},{2,3},{3,4},{4,5},{5,6},{6,7},{8,9},{9,10},{10,11},{11... | collective-permute-start | bytes 393224 | tf_op jit(solution)/shard_map/ppermute | solution.py:30
  115.0 7.1 %collective-permute-start.9 = (f32[8,8,4,128]{3,2,1,0:T(4,128)}, f32[8,8,4,128]{3,2,1,0:T(4,128)S(1)}, u32[]{:S(2)}, u32[]{:S(2)}) collective-permute-start(f32[8,8,4,128]{3,2,1,0:T(4,128)} %get-tuple-element.32), channel_id=1, source_target_pairs={{1,0},{2,1},{3,2},{4,3},{5,4},{6,5},{7,6},{9,8},{10,9},{11,10},{12... | collective-permute-start | bytes 393224 | tf_op jit(solution)/shard_map/ppermute | solution.py:31
  117.8 4.3 %copy-start.5 = (f32[8,8,4,128]{3,2,1,0:T(4,128)}, f32[8,8,4,128]{3,2,1,0:T(4,128)S(1)}, u32[]{:S(2)}) copy-start(f32[8,8,4,128]{3,2,1,0:T(4,128)S(1)} %collective-permute-done.8.before) | copy-start | bytes 393220
  122.0 0.6 copy-start.6
  125.0 22.2 %collective-permute-start.10 = (f32[8,3,40,128]{3,2,1,0:T(8,128)}, f32[8,3,40,128]{3,2,1,0:T(8,128)S(1)}, u32[]{:S(2)}, u32[]{:S(2)}) collective-permute-start(f32[8,3,40,128]{3,2,1,0:T(8,128)} %get-tuple-element.33), channel_id=1, source_target_pairs={{0,8},{8,16},{16,24},{1,9},{9,17},{17,25},{2,10},{10,18},{18,26},{... | collective-permute-start | bytes 1474568 | tf_op jit(solution)/shard_map/ppermute | solution.py:30
  131.6 15.7 %collective-permute-start.11 = (f32[8,3,40,128]{3,2,1,0:T(8,128)}, f32[8,3,40,128]{3,2,1,0:T(8,128)S(1)}, u32[]{:S(2)}, u32[]{:S(2)}) collective-permute-start(f32[8,3,40,128]{3,2,1,0:T(8,128)} %get-tuple-element.34.refs_1_), channel_id=1, source_target_pairs={{8,0},{16,8},{24,16},{9,1},{17,9},{25,17},{10,2},{18,10},{26,18},{... | collective-permute-start | bytes 1474568 | tf_op jit(solution)/shard_map/ppermute | solution.py:31
  132.9 5.2 %collective-permute-start.14 = (f32[8,128]{1,0:T(8,128)S(1)}, f32[8,128]{1,0:T(8,128)S(1)}, u32[]{:S(2)}, u32[]{:S(2)}) collective-permute-start(f32[8,128]{1,0:T(8,128)S(1)} %copy-done.11), channel_id=1, source_target_pairs={{0,3},{1,2},{2,1},{3,0},{4,7},{5,6},{6,5},{7,4},{8,11},{9,10},{10,... | collective-permute-start | bytes 12296 | tf_op jit(solution)/shard_map/ppermute | solution.py:471
  136.5 3.6 %collective-permute-start.13 = (f32[8,128]{1,0:T(8,128)S(1)}, f32[8,128]{1,0:T(8,128)S(1)}, u32[]{:S(2)}, u32[]{:S(2)}) collective-permute-start(f32[8,128]{1,0:T(8,128)S(1)} %copy-done.11), channel_id=1, source_target_pairs={{0,2},{1,3},{2,0},{3,1},{4,6},{5,7},{6,4},{7,5},{8,10},{9,11},{10,... | collective-permute-start | bytes 12296 | tf_op jit(solution)/shard_map/ppermute | solution.py:471
  137.1 3.6 %collective-permute-start.12 = (f32[8,128]{1,0:T(8,128)S(1)}, f32[8,128]{1,0:T(8,128)S(1)}, u32[]{:S(2)}, u32[]{:S(2)}) collective-permute-start(f32[8,128]{1,0:T(8,128)S(1)} %copy-done.11), channel_id=1, source_target_pairs={{0,1},{1,0},{2,3},{3,2},{4,5},{5,4},{6,7},{7,6},{8,9},{9,8},{10,11... | collective-permute-start | bytes 12296 | tf_op jit(solution)/shard_map/ppermute | solution.py:471
  141.3 4.7 %collective-permute-start.15 = (f32[8,128]{1,0:T(8,128)}, f32[8,128]{1,0:T(8,128)S(1)}, u32[]{:S(2)}, u32[]{:S(2)}) collective-permute-start(f32[8,128]{1,0:T(8,128)} %shard_map.70), channel_id=1, source_target_pairs={{0,4},{1,5},{2,6},{3,7},{4,0},{5,1},{6,2},{7,3},{8,12},{9,13},{10,... | collective-permute-start | bytes 12296 | tf_op jit(solution)/shard_map/ppermute | solution.py:471
  147.3 0.8 copy-start.3
  148.1 0.8 copy-start.4
  148.8 17.1 %collective-permute-start.18 = (f32[8,128]{1,0:T(8,128)}, f32[8,128]{1,0:T(8,128)S(1)}, u32[]{:S(2)}, u32[]{:S(2)}) collective-permute-start(f32[8,128]{1,0:T(8,128)} %shard_map.71.gate), channel_id=1, source_target_pairs={{0,24},{8,16},{16,8},{24,0},{1,25},{9,17},{17,9},{25,1},{2,26},{10... | collective-permute-start | bytes 12296 | tf_op jit(solution)/shard_map/ppermute | solution.py:471
  148.8 17.1 %collective-permute-start.17 = (f32[8,128]{1,0:T(8,128)}, f32[8,128]{1,0:T(8,128)S(1)}, u32[]{:S(2)}, u32[]{:S(2)}) collective-permute-start(f32[8,128]{1,0:T(8,128)} %shard_map.71.gate), channel_id=1, source_target_pairs={{0,16},{8,24},{16,0},{24,8},{1,17},{9,25},{17,1},{25,9},{2,18},{10... | collective-permute-start | bytes 12296 | tf_op jit(solution)/shard_map/ppermute | solution.py:471
  152.0 14.0 %collective-permute-start.16 = (f32[8,128]{1,0:T(8,128)}, f32[8,128]{1,0:T(8,128)S(1)}, u32[]{:S(2)}, u32[]{:S(2)}) collective-permute-start(f32[8,128]{1,0:T(8,128)} %shard_map.71.gate), channel_id=1, source_target_pairs={{0,8},{8,0},{16,24},{24,16},{1,9},{9,1},{17,25},{25,17},{2,10},{10... | collective-permute-start | bytes 12296 | tf_op jit(solution)/shard_map/ppermute | solution.py:471
  152.1 13.9 %copy-start.10 = (f32[8,128]{1,0:T(8,128)S(1)}, f32[8,128]{1,0:T(8,128)}, u32[]{:S(2)}) copy-start(f32[8,128]{1,0:T(8,128)} %shard_map.71.gate) | copy-start | bytes 12292

commit v5 on v4

--- a/solution.py
+++ b/solution.py
@@ -348,8 +348,10 @@
         out[i, z, pl.ds(row, count), :] = src[pl.ds(at, count), pl.ds(i * LANES, LANES)]
 
 
-def extend_kernel(vel, planes_below, planes_above, before, after, corners_below, corners_above, ext_ref):
-    _, sections, rows, _ = vel.shape
+def extend_kernel(vel, sti, planes_below, planes_above, before, after, corners_below, corners_above,
+                  ext_out, reg_ref, sum_ref, ext_ref, sti_ext, sem):
+    _, sections, rows, width = vel.shape
+    blocks = width // LANES
 
     def mid(z, _):
         for c in range(3):
@@ -375,18 +377,14 @@
             for src, z_out in ((corners_below, z), (corners_above, z + WIDE + sections)):
                 lay_rows(ext_ref.at[c], z_out, low, src, at, WIDE)
                 lay_rows(ext_ref.at[c], z_out, high, src, at + half, WIDE)
-
-
-def regular_kernel(gate, ext_ref, sti, planes_below, planes_above, before, after, reg_ref, sum_ref, sti_ext):
-    del gate
-    sections, rows, width = sti.shape
-    blocks = width // LANES
-
-    def mid(z, _):
+    out = pltpu.make_async_copy(ext_ref, ext_out, sem.at[0])
+    out.start()
+
+    def mid_s(z, _):
         lay(sti_ext, sti.at[z], z + 1)
         return 0
 
-    lax.fori_loop(0, sections, mid, 0)
+    lax.fori_loop(0, sections, mid_s, 0)
     lay(sti_ext, planes_below.at[3 * WIDE], 0)
     lay(sti_ext, planes_above.at[3 * WIDE], sections + 1)
     for z in range(sections):
@@ -429,6 +427,7 @@
 
     acc = lax.fori_loop(0, sections, plane, jnp.zeros((TILE, LANES), jnp.float32))
     sum_ref[...] = acc
+    out.wait()
 
 
 def after(value, *gates):
@@ -526,9 +525,14 @@
     template = to_rows(to_blocks(template_scan, SENT, low_rows))
     below, above = exchange(low, high, "sec")
     corners = call(corner_kernel, [(6 * WIDE * WIDE, width)] * 2, [VMEM] * 2)(before, after_)
-    (extended,) = call(extend_kernel, [(3, blocks, deep, tall, LANES)], [VMEM] * 7)(
-        velocity, below, above, before, after_, *exchange(*corners, "sec")
-    )
+    extended, reg, reg_sums = call(
+        extend_kernel,
+        [(3, blocks, deep, tall, LANES), velocity.shape, (TILE, LANES)],
+        [VMEM] * 8,
+        [(3, blocks, deep, tall, LANES), (blocks, sections + 2, tall, LANES), 1],
+        [ANY, VMEM, VMEM],
+        20 << 20,
+    )(velocity, stiffness, below, above, before, after_, *exchange(*corners, "sec"))
 
     fixed_blocks = to_blocks(reference_scan, 0, corners[0])
     low, high = call(slice_kernel, [(blocks, STEPS, tall, LANES)] * 2, [VMEM, ANY, ANY])(
@@ -545,14 +549,6 @@
         [VMEM, ANY],
         20 << 20,
     )(flags, *start, extended)
-
-    reg, reg_sums = call(
-        regular_kernel,
-        [velocity.shape, (TILE, LANES)],
-        [ANY] + [VMEM] * 6,
-        [(blocks, sections + 2, tall, LANES)],
-        flops=20 << 20,
-    )(moved, extended, stiffness, below, above, before, after_)
 
     misfit, low_rows, high_rows, partial = call(misfit_kernel, [own, ends, ends, (TILE, LANES)], [VMEM] * 3)(
         moved, fixed, reg_sums

time: 169 us -> 163 us (0.964)
  Pallas kernels: 63.3 us -> 56.7 us
    pallas_call x2 -> x1, Pallas kernels: 15.6 us -> 8.95 us  [local(): call(extend_kernel, [(3, blocks, deep, tall, LANES), velocity.shape, (TIL...]
  transfers between devices with their start and end apart: 21 -> 21, of which waited for: 8 -> 8; matrix products, arithmetic and copies ran while one was open for 1% -> 2% of each run, Pallas kernels for 28% -> 25%
where the time goes in v5:
time: 163 us; the launch traced here: 162 us
  starting transfers between devices  61.2 us (38%)
  Pallas kernels  56.7 us (35%)
  waiting for transfers between devices  33.6 us (21%)
  local copies, waits for them, and re-layouts  4.52 us (3%)
  other arithmetic  3.05 us (2%)
  between operations  2.68 us (2%)
    ppermute x6, starting transfers between devices, exchange(): lax.ppermute(high_part, axis, [(i, i + 1) for i in range(count - 1)])  23.1 us
    all_to_all x2, starting transfers between devices, to_rows(): lax.all_to_all(parts, 'row', split_axis=0, concat_axis=0, tiled=True)  20.8 us
    ppermute x6, waiting for transfers between devices, exchange(): lax.ppermute(high_part, axis, [(i, i + 1) for i in range(count - 1)])  20.4 us
    pallas_call x1, Pallas kernels, local(): call(adjoint_kernel, [velocity.shape], [SMEM] + [VMEM] * 5 + [ANY] * 7, [...  13.8 us
    pallas_call x1, Pallas kernels, local(): call(forward_kernel, [own, (STEPS - 1, blocks, sections + 2, tall, LANES)...  13.3 us
    ppermute x7, starting transfers between devices, summed(): lax.ppermute(part, axis, [(i, i ^ low) for i in range(count)])  9.53 us
    pallas_call x1, Pallas kernels, local(): call(extend_kernel, [(3, blocks, deep, tall, LANES), velocity.shape, (TIL...  8.95 us
    ppermute x6, starting transfers between devices, exchange(): above = lax.ppermute(low_part, axis, [(i + 1, i) for i in range(count - 1)])  7.74 us
  transfers between devices with their start and end apart: 21, of which 8 were waited for; matrix products, arithmetic and copies ran while one was open for 2% of the time, Pallas kernels for 25%

profile of v5, /device:TPU:0, one launch (start us, length us, event | category | flops | bytes accessed | tf_op | source)
XLA Modules:
  0.0 161.8 jit_solution(9469360065304878791)
XLA Ops:
  0.6 4.6 %shard_map.59 = (f32[80,1024]{1,0:T(8,128)}, f32[80,1024]{1,0:T(8,128)}, f32[10,32,1024]{2,1,0:T(8,128)}, f32[10,32,1024]{2,1,0:T(8,128)}) custom-call(f32[3,8,32,1024]{3,2,1,0:T(8,128)} %vel.3, f32[8,32,1024]{2,1,0:T(8,128)} %sti.3), custom_call_target="tpu_custom_call" | custom-call | bytes 4194304 | tf_op jit(solution)/shard_map/pallas_call | solution.py:517
  5.2 3.3 %shard_map.60 = f32[8,8,40,128]{3,2,1,0:T(8,128)} custom-call(f32[8,128,256]{2,1,0:T(8,128)} %scan.2, f32[80,1024]{1,0:T(8,128)} %get-tuple-element.21.gate), custom_call_target="tpu_custom_call" | custom-call | bytes 4194304 | tf_op jit(solution)/shard_map/pallas_call | solution.py:452
  8.5 7.4 %all-to-all-start = ((f32[8,8,40,128]{3,2,1,0:T(8,128)}), f32[8,8,40,128]{3,2,1,0:T(8,128)}, u32[]{:S(2)}, u32[]{:S(2)}) async-start(f32[8,8,40,128]{3,2,1,0:T(8,128)} %shard_map.60), calls=%async_computation | async-start | bytes 2621440 | tf_op jit(solution)/shard_map/all_to_all | solution.py:460
  15.9 2.6 %collective-permute-start = (f32[10,32,1024]{2,1,0:T(8,128)}, f32[10,32,1024]{2,1,0:T(8,128)}, u32[]{:S(2)}, u32[]{:S(2)}) collective-permute-start(f32[10,32,1024]{2,1,0:T(8,128)} %get-tuple-element.22), channel_id=1, source_target_pairs={{0,8},{8,16},{16,24},{1,9},{9,17},{17,25},{2,10},{10,18},{18,26},{... | collective-permute-start | bytes 3932168 | tf_op jit(solution)/shard_map/ppermute | solution.py:30
  18.6 1.3 collective-permute-start.1
  19.9 3.8 %collective-permute-start.4 = (f32[80,1024]{1,0:T(8,128)S(1)}, f32[80,1024]{1,0:T(8,128)S(1)}, u32[]{:S(2)}, u32[]{:S(2)}) collective-permute-start(f32[80,1024]{1,0:T(8,128)S(1)} %copy-done.12), channel_id=1, source_target_pairs={{0,1},{1,2},{2,3},{3,4},{4,5},{5,6},{6,7},{8,9},{9,10},{10,11},{11... | collective-permute-start | bytes 983048 | tf_op jit(solution)/shard_map/ppermute | solution.py:30
  23.6 1.3 collective-permute-start.5
  24.9 18.8 %collective-permute-done.4.before = f32[80,1024]{1,0:T(8,128)S(1)} collective-permute-done((f32[80,1024]{1,0:T(8,128)S(1)}, f32[80,1024]{1,0:T(8,128)S(1)}, u32[]{:S(2)}, u32[]{:S(2)}) %collective-permute-start.4) | collective-permute-done | bytes 327712 | tf_op jit(solution)/shard_map/ppermute | solution.py:30
  43.8 0.7 copy-done.3
  44.5 0.7 copy-done.4
  45.2 1.9 %shard_map.62 = (f32[54,1024]{1,0:T(8,128)}, f32[54,1024]{1,0:T(8,128)}) custom-call(f32[80,1024]{1,0:T(8,128)} %copy-done.3, f32[80,1024]{1,0:T(8,128)} %copy-done.4), custom_call_target="tpu_custom_call" | custom-call | bytes 4194304 | tf_op jit(solution)/shard_map/pallas_call | solution.py:527
  47.2 3.0 %shard_map.65.refs_0_ = f32[8,8,32,128]{3,2,1,0:T(8,128)} custom-call(f32[8,128,256]{2,1,0:T(8,128)} %scan.3, f32[54,1024]{1,0:T(8,128)} %get-tuple-element.28.gate), custom_call_target="tpu_custom_call" | custom-call | bytes 4194304 | tf_op jit(solution)/shard_map/pallas_call | solution.py:452
  50.2 2.5 %shard_map.61 = (f32[8,4,40,128]{3,2,1,0:T(8,128)}, f32[8,4,40,128]{3,2,1,0:T(8,128)}) custom-call(f32[8,8,40,128]{3,2,1,0:T(8,128)} %all-to-all-done.field.own.start, f32[10,32,1024]{2,1,0:T(8,128)} %collective-permute-done.gate_below.planes_below, f32[10,32,1024]{2,1,0:T(8,128)} %collective-permute-done.1.gate_above.planes_above), custom_call_target="tpu_custom_call" | custom-call | bytes 4194304 | tf_op jit(solution)/shard_map/pallas_call | solution.py:538
  52.7 13.4 %all-to-all-start.1 = ((f32[8,8,32,128]{3,2,1,0:T(8,128)}), f32[8,8,32,128]{3,2,1,0:T(8,128)}, u32[]{:S(2)}, u32[]{:S(2)}) async-start(f32[8,8,32,128]{3,2,1,0:T(8,128)} %shard_map.66), calls=%async_computation.1 | async-start | bytes 2097152 | tf_op jit(solution)/shard_map/all_to_all | solution.py:460
  66.2 1.7 %collective-permute-start.2 = (f32[8,4,40,128]{3,2,1,0:T(8,128)}, f32[8,4,40,128]{3,2,1,0:T(8,128)S(1)}, u32[]{:S(2)}, u32[]{:S(2)}) collective-permute-start(f32[8,4,40,128]{3,2,1,0:T(8,128)} %get-tuple-element.24), channel_id=1, source_target_pairs={{0,8},{8,16},{16,24},{1,9},{9,17},{17,25},{2,10},{10,18},{18,26},{... | collective-permute-start | bytes 1966088 | tf_op jit(solution)/shard_map/ppermute | solution.py:30
  67.8 1.3 collective-permute-start.3
  69.1 4.4 %collective-permute-start.6 = (f32[54,1024]{1,0:T(8,128)S(1)}, f32[54,1024]{1,0:T(8,128)S(1)}, u32[]{:S(2)}, u32[]{:S(2)}) collective-permute-start(f32[54,1024]{1,0:T(8,128)S(1)} %copy-done.13), channel_id=1, source_target_pairs={{0,8},{8,16},{16,24},{1,9},{9,17},{17,25},{2,10},{10,18},{18,26},{... | collective-permute-start | bytes 663560 | tf_op jit(solution)/shard_map/ppermute | solution.py:30
  73.6 1.3 collective-permute-start.7
  74.9 0.6 add_convert_fusion.flags
  75.5 2.8 %collective-permute-done.7.corners_above = f32[54,1024]{1,0:T(8,128)} collective-permute-done((f32[54,1024]{1,0:T(8,128)S(1)}, f32[54,1024]{1,0:T(8,128)}, u32[]{:S(2)}, u32[]{:S(2)}) %collective-permute-start.7) | collective-permute-done | bytes 221216 | tf_op jit(solution)/shard_map/ppermute | solution.py:31
  78.3 8.9 %shard_map.63 = (f32[3,8,14,40,128]{4,3,2,1,0:T(8,128)}, f32[3,8,32,1024]{3,2,1,0:T(8,128)}, f32[8,128]{1,0:T(8,128)}) custom-call(f32[3,8,32,1024]{3,2,1,0:T(8,128)} %vel.3, f32[8,32,1024]{2,1,0:T(8,128)} %sti.3, f32[10,32,1024]{2,1,0:T(8,128)} %collective-permute-done.gate_below.planes_below, ...), custom_call_target="tpu_custom_call" | custom-call | flops 20971520 | bytes 4194304 | tf_op jit(solution)/shard_map/pallas_call | solution.py:528
  87.3 0.8 copy-done
  88.1 13.3 %shard_map.64 = (f32[8,8,32,128]{3,2,1,0:T(8,128)}, f32[3,8,10,40,128]{4,3,2,1,0:T(8,128)}) custom-call(f32[4]{0:T(128)} %add_convert_fusion.flags, f32[8,8,40,128]{3,2,1,0:T(8,128)} %all-to-all-done.field.own.start, f32[8,4,40,128]{3,2,1,0:T(8,128)} %copy-done, f32[8,4,40,128]{3,2,1,0:T(8,128)} %collective-permute-done.3.above.start_above, ...), custom_call_target="tpu_custom_call" | custom-call | flops 20971520 | bytes 4194304 | tf_op jit(solution)/shard_map/pallas_call | solution.py:544
  101.5 2.9 %shard_map.67 = (f32[8,8,32,128]{3,2,1,0:T(8,128)}, f32[8,8,4,128]{3,2,1,0:T(4,128)}, f32[8,8,4,128]{3,2,1,0:T(4,128)}, f32[8,128]{1,0:T(8,128)}) custom-call(f32[8,8,32,128]{3,2,1,0:T(8,128)} %get-tuple-element.30.moved, f32[8,8,32,128]{3,2,1,0:T(8,128)} %all-to-all-done.1.fixed, f32[8,128]{1,0:T(8,128)} %get-tuple-element.31.sums), custom_call_target="tpu_custom_call" | custom-call | bytes 4194304 | tf_op jit(solution)/shard_map/pallas_call | solution.py:553
  104.4 4.1 %collective-permute-start.8 = (f32[8,8,4,128]{3,2,1,0:T(4,128)}, f32[8,8,4,128]{3,2,1,0:T(4,128)S(1)}, u32[]{:S(2)}, u32[]{:S(2)}) collective-permute-start(f32[8,8,4,128]{3,2,1,0:T(4,128)} %get-tuple-element.33), channel_id=1, source_target_pairs={{0,1},{1,2},{2,3},{3,4},{4,5},{5,6},{6,7},{8,9},{9,10},{10,11},{11... | collective-permute-start | bytes 393224 | tf_op jit(solution)/shard_map/ppermute | solution.py:30
  108.5 1.3 collective-permute-start.9
  109.8 1.5 collective-permute-done.8.before
  111.3 4.3 %collective-permute-done.9.after = f32[8,8,4,128]{3,2,1,0:T(4,128)S(1)} collective-permute-done((f32[8,8,4,128]{3,2,1,0:T(4,128)}, f32[8,8,4,128]{3,2,1,0:T(4,128)S(1)}, u32[]{:S(2)}, u32[]{:S(2)}) %collective-permute-start.9) | collective-permute-done | bytes 131104 | tf_op jit(solution)/shard_map/ppermute | solution.py:31
  115.6 0.6 copy-done.6
  116.2 2.3 %shard_map.68 = (f32[8,3,40,128]{3,2,1,0:T(8,128)}, f32[8,3,40,128]{3,2,1,0:T(8,128)}) custom-call(f32[8,8,32,128]{3,2,1,0:T(8,128)} %get-tuple-element.32.field.own, f32[8,8,4,128]{3,2,1,0:T(4,128)} %copy-done.5, f32[8,8,4,128]{3,2,1,0:T(4,128)} %copy-done.6), custom_call_target="tpu_custom_call" | custom-call | bytes 4194304 | tf_op jit(solution)/shard_map/pallas_call | solution.py:557
  118.5 6.6 %collective-permute-start.10 = (f32[8,3,40,128]{3,2,1,0:T(8,128)}, f32[8,3,40,128]{3,2,1,0:T(8,128)S(1)}, u32[]{:S(2)}, u32[]{:S(2)}) collective-permute-start(f32[8,3,40,128]{3,2,1,0:T(8,128)} %get-tuple-element.35), channel_id=1, source_target_pairs={{0,8},{8,16},{16,24},{1,9},{9,17},{17,25},{2,10},{10,18},{18,26},{... | collective-permute-start | bytes 1474568 | tf_op jit(solution)/shard_map/ppermute | solution.py:30
  125.1 1.3 collective-permute-start.11
  126.4 3.6 %collective-permute-start.14 = (f32[8,128]{1,0:T(8,128)S(1)}, f32[8,128]{1,0:T(8,128)S(1)}, u32[]{:S(2)}, u32[]{:S(2)}) collective-permute-start(f32[8,128]{1,0:T(8,128)S(1)} %copy-done.11), channel_id=1, source_target_pairs={{0,3},{1,2},{2,1},{3,0},{4,7},{5,6},{6,5},{7,4},{8,11},{9,10},{10,... | collective-permute-start | bytes 12296 | tf_op jit(solution)/shard_map/ppermute | solution.py:470
  130.0 0.6 collective-permute-start.13
  130.6 0.1 collective-permute-start.12
  130.7 0.9 collective-permute-done.14
  131.6 2.0 %collective-permute-done.13 = f32[8,128]{1,0:T(8,128)S(1)} collective-permute-done((f32[8,128]{1,0:T(8,128)S(1)}, f32[8,128]{1,0:T(8,128)S(1)}, u32[]{:S(2)}, u32[]{:S(2)}) %collective-permute-start.13) | collective-permute-done | bytes 4128 | tf_op jit(solution)/shard_map/ppermute | solution.py:470
  133.6 0.6 collective-permute-done.12
  134.2 0.6 select_add_fusion.refs_0_
  134.8 2.1 %collective-permute-start.15 = (f32[8,128]{1,0:T(8,128)}, f32[8,128]{1,0:T(8,128)S(1)}, u32[]{:S(2)}, u32[]{:S(2)}) collective-permute-start(f32[8,128]{1,0:T(8,128)} %shard_map.69), channel_id=1, source_target_pairs={{0,4},{1,5},{2,6},{3,7},{4,0},{5,1},{6,2},{7,3},{8,12},{9,13},{10,... | collective-permute-start | bytes 12296 | tf_op jit(solution)/shard_map/ppermute | solution.py:470
  136.9 2.6 %collective-permute-done.15 = f32[8,128]{1,0:T(8,128)S(1)} collective-permute-done((f32[8,128]{1,0:T(8,128)}, f32[8,128]{1,0:T(8,128)S(1)}, u32[]{:S(2)}, u32[]{:S(2)}) %collective-permute-start.15) | collective-permute-done | bytes 4128 | tf_op jit(solution)/shard_map/ppermute | solution.py:470
  139.5 1.3 add.34.refs_0_
  140.8 0.8 copy-done.1
  141.6 0.8 copy-done.2
  142.4 3.1 %collective-permute-start.17 = (f32[8,128]{1,0:T(8,128)}, f32[8,128]{1,0:T(8,128)S(1)}, u32[]{:S(2)}, u32[]{:S(2)}) collective-permute-start(f32[8,128]{1,0:T(8,128)} %shard_map.70.gate), channel_id=1, source_target_pairs={{0,16},{8,24},{16,0},{24,8},{1,17},{9,25},{17,1},{25,9},{2,18},{10... | collective-permute-start | bytes 12296 | tf_op jit(solution)/shard_map/ppermute | solution.py:470
  145.5 0.1 collective-permute-start.16
  145.6 13.8 %shard_map.71 = f32[3,8,32,1024]{3,2,1,0:T(8,128)} custom-call(f32[4]{0:T(128)} %add_convert_fusion.flags, f32[8,8,32,128]{3,2,1,0:T(8,128)} %get-tuple-element.32.field.own, f32[8,3,40,128]{3,2,1,0:T(8,128)} %copy-done.1, f32[8,3,40,128]{3,2,1,0:T(8,128)} %copy-done.2, f32[8,8,4,128]{3,2,1,0:T(4,128)} %copy-done.5, f32[8,8,4,128]{3,2,1,0:T(4,128)} %copy-done.6, ...), custom_call_target="tpu_custom_call" | custom-call | flops 20971520 | bytes 4194304 | tf_op jit(solution)/shard_map/pallas_call | solution.py:564
  159.4 0.6 add_reduce_fusion
  (39 shorter events, 0.1 us)
Async XLA Ops:
  8.5 11.3 %copy-start.12 = (f32[80,1024]{1,0:T(8,128)S(1)}, f32[80,1024]{1,0:T(8,128)}, u32[]{:S(2)}) copy-start(f32[80,1024]{1,0:T(8,128)} %get-tuple-element.26) | copy-start | bytes 983044
  8.5 15.1 %copy-start.7 = (f32[80,1024]{1,0:T(8,128)S(1)}, f32[80,1024]{1,0:T(8,128)}, u32[]{:S(2)}) copy-start(f32[80,1024]{1,0:T(8,128)} %get-tuple-element.21.gate) | copy-start | bytes 983044
  8.5 41.7 %all-to-all-start = ((f32[8,8,40,128]{3,2,1,0:T(8,128)}), f32[8,8,40,128]{3,2,1,0:T(8,128)}, u32[]{:S(2)}, u32[]{:S(2)}) async-start(f32[8,8,40,128]{3,2,1,0:T(8,128)} %shard_map.60), calls=%async_computation | async-start | bytes 2621440 | tf_op jit(solution)/shard_map/all_to_all | solution.py:460
  15.9 34.3 %collective-permute-start = (f32[10,32,1024]{2,1,0:T(8,128)}, f32[10,32,1024]{2,1,0:T(8,128)}, u32[]{:S(2)}, u32[]{:S(2)}) collective-permute-start(f32[10,32,1024]{2,1,0:T(8,128)} %get-tuple-element.22), channel_id=1, source_target_pairs={{0,8},{8,16},{16,24},{1,9},{9,17},{17,25},{2,10},{10,18},{18,26},{... | collective-permute-start | bytes 3932168 | tf_op jit(solution)/shard_map/ppermute | solution.py:30
  18.6 31.7 %collective-permute-start.1 = (f32[10,32,1024]{2,1,0:T(8,128)}, f32[10,32,1024]{2,1,0:T(8,128)}, u32[]{:S(2)}, u32[]{:S(2)}) collective-permute-start(f32[10,32,1024]{2,1,0:T(8,128)} %get-tuple-element.23), channel_id=1, source_target_pairs={{8,0},{16,8},{24,16},{9,1},{17,9},{25,17},{10,2},{18,10},{26,18},{... | collective-permute-start | bytes 3932168 | tf_op jit(solution)/shard_map/ppermute | solution.py:31
  19.9 23.9 %collective-permute-start.4 = (f32[80,1024]{1,0:T(8,128)S(1)}, f32[80,1024]{1,0:T(8,128)S(1)}, u32[]{:S(2)}, u32[]{:S(2)}) collective-permute-start(f32[80,1024]{1,0:T(8,128)S(1)} %copy-done.12), channel_id=1, source_target_pairs={{0,1},{1,2},{2,3},{3,4},{4,5},{5,6},{6,7},{8,9},{9,10},{10,11},{11... | collective-permute-start | bytes 983048 | tf_op jit(solution)/shard_map/ppermute | solution.py:30
  23.6 20.1 %collective-permute-start.5 = (f32[80,1024]{1,0:T(8,128)S(1)}, f32[80,1024]{1,0:T(8,128)S(1)}, u32[]{:S(2)}, u32[]{:S(2)}) collective-permute-start(f32[80,1024]{1,0:T(8,128)S(1)} %copy-done.7), channel_id=1, source_target_pairs={{1,0},{2,1},{3,2},{4,3},{5,4},{6,5},{7,6},{9,8},{10,9},{11,10},{12... | collective-permute-start | bytes 983048 | tf_op jit(solution)/shard_map/ppermute | solution.py:31
  43.8 0.7 copy-start.3
  44.5 0.7 copy-start.4
  52.7 16.4 %copy-start.13 = (f32[54,1024]{1,0:T(8,128)S(1)}, f32[54,1024]{1,0:T(8,128)}, u32[]{:S(2)}) copy-start(f32[54,1024]{1,0:T(8,128)} %get-tuple-element.27) | copy-start | bytes 663556
  52.7 20.8 %copy-start.8 = (f32[54,1024]{1,0:T(8,128)S(1)}, f32[54,1024]{1,0:T(8,128)}, u32[]{:S(2)}) copy-start(f32[54,1024]{1,0:T(8,128)} %get-tuple-element.28.gate) | copy-start | bytes 663556
  52.7 48.8 %all-to-all-start.1 = ((f32[8,8,32,128]{3,2,1,0:T(8,128)}), f32[8,8,32,128]{3,2,1,0:T(8,128)}, u32[]{:S(2)}, u32[]{:S(2)}) async-start(f32[8,8,32,128]{3,2,1,0:T(8,128)} %shard_map.66), calls=%async_computation.1 | async-start | bytes 2097152 | tf_op jit(solution)/shard_map/all_to_all | solution.py:460
  66.2 21.1 %collective-permute-start.2 = (f32[8,4,40,128]{3,2,1,0:T(8,128)}, f32[8,4,40,128]{3,2,1,0:T(8,128)S(1)}, u32[]{:S(2)}, u32[]{:S(2)}) collective-permute-start(f32[8,4,40,128]{3,2,1,0:T(8,128)} %get-tuple-element.24), channel_id=1, source_target_pairs={{0,8},{8,16},{16,24},{1,9},{9,17},{17,25},{2,10},{10,18},{18,26},{... | collective-permute-start | bytes 1966088 | tf_op jit(solution)/shard_map/ppermute | solution.py:30
  67.8 19.4 %collective-permute-start.3 = (f32[8,4,40,128]{3,2,1,0:T(8,128)}, f32[8,4,40,128]{3,2,1,0:T(8,128)}, u32[]{:S(2)}, u32[]{:S(2)}) collective-permute-start(f32[8,4,40,128]{3,2,1,0:T(8,128)} %get-tuple-element.25.refs_1_), channel_id=1, source_target_pairs={{8,0},{16,8},{24,16},{9,1},{17,9},{25,17},{10,2},{18,10},{26,18},{... | collective-permute-start | bytes 1966088 | tf_op jit(solution)/shard_map/ppermute | solution.py:31
  69.1 6.3 %collective-permute-start.6 = (f32[54,1024]{1,0:T(8,128)S(1)}, f32[54,1024]{1,0:T(8,128)S(1)}, u32[]{:S(2)}, u32[]{:S(2)}) collective-permute-start(f32[54,1024]{1,0:T(8,128)S(1)} %copy-done.13), channel_id=1, source_target_pairs={{0,8},{8,16},{16,24},{1,9},{9,17},{17,25},{2,10},{10,18},{18,26},{... | collective-permute-start | bytes 663560 | tf_op jit(solution)/shard_map/ppermute | solution.py:30
  73.6 4.7 %collective-permute-start.7 = (f32[54,1024]{1,0:T(8,128)S(1)}, f32[54,1024]{1,0:T(8,128)}, u32[]{:S(2)}, u32[]{:S(2)}) collective-permute-start(f32[54,1024]{1,0:T(8,128)S(1)} %copy-done.8), channel_id=1, source_target_pairs={{8,0},{16,8},{24,16},{9,1},{17,9},{25,17},{10,2},{18,10},{26,18},{... | collective-permute-start | bytes 663560 | tf_op jit(solution)/shard_map/ppermute | solution.py:31
  75.5 2.8 %copy-start.9 = (f32[54,1024]{1,0:T(8,128)}, f32[54,1024]{1,0:T(8,128)S(1)}, u32[]{:S(2)}) copy-start(f32[54,1024]{1,0:T(8,128)S(1)} %collective-permute-done.6.corners_below) | copy-start | bytes 663556
  87.3 0.9 copy-start
  104.4 22.0 %copy-start.11 = (f32[8,128]{1,0:T(8,128)S(1)}, f32[8,128]{1,0:T(8,128)}, u32[]{:S(2)}) copy-start(f32[8,128]{1,0:T(8,128)} %get-tuple-element.39) | copy-start | bytes 12292
  104.4 6.9 %collective-permute-start.8 = (f32[8,8,4,128]{3,2,1,0:T(4,128)}, f32[8,8,4,128]{3,2,1,0:T(4,128)S(1)}, u32[]{:S(2)}, u32[]{:S(2)}) collective-permute-start(f32[8,8,4,128]{3,2,1,0:T(4,128)} %get-tuple-element.33), channel_id=1, source_target_pairs={{0,1},{1,2},{2,3},{3,4},{4,5},{5,6},{6,7},{8,9},{9,10},{10,11},{11... | collective-permute-start | bytes 393224 | tf_op jit(solution)/shard_map/ppermute | solution.py:30
  108.5 7.1 %collective-permute-start.9 = (f32[8,8,4,128]{3,2,1,0:T(4,128)}, f32[8,8,4,128]{3,2,1,0:T(4,128)S(1)}, u32[]{:S(2)}, u32[]{:S(2)}) collective-permute-start(f32[8,8,4,128]{3,2,1,0:T(4,128)} %get-tuple-element.34), channel_id=1, source_target_pairs={{1,0},{2,1},{3,2},{4,3},{5,4},{6,5},{7,6},{9,8},{10,9},{11,10},{12... | collective-permute-start | bytes 393224 | tf_op jit(solution)/shard_map/ppermute | solution.py:31
  111.3 4.3 %copy-start.5 = (f32[8,8,4,128]{3,2,1,0:T(4,128)}, f32[8,8,4,128]{3,2,1,0:T(4,128)S(1)}, u32[]{:S(2)}) copy-start(f32[8,8,4,128]{3,2,1,0:T(4,128)S(1)} %collective-permute-done.8.before) | copy-start | bytes 393220
  115.6 0.6 copy-start.6
  118.5 22.2 %collective-permute-start.10 = (f32[8,3,40,128]{3,2,1,0:T(8,128)}, f32[8,3,40,128]{3,2,1,0:T(8,128)S(1)}, u32[]{:S(2)}, u32[]{:S(2)}) collective-permute-start(f32[8,3,40,128]{3,2,1,0:T(8,128)} %get-tuple-element.35), channel_id=1, source_target_pairs={{0,8},{8,16},{16,24},{1,9},{9,17},{17,25},{2,10},{10,18},{18,26},{... | collective-permute-start | bytes 1474568 | tf_op jit(solution)/shard_map/ppermute | solution.py:30
  125.1 15.7 %collective-permute-start.11 = (f32[8,3,40,128]{3,2,1,0:T(8,128)}, f32[8,3,40,128]{3,2,1,0:T(8,128)S(1)}, u32[]{:S(2)}, u32[]{:S(2)}) collective-permute-start(f32[8,3,40,128]{3,2,1,0:T(8,128)} %get-tuple-element.36.refs_1_), channel_id=1, source_target_pairs={{8,0},{16,8},{24,16},{9,1},{17,9},{25,17},{10,2},{18,10},{26,18},{... | collective-permute-start | bytes 1474568 | tf_op jit(solution)/shard_map/ppermute | solution.py:31
  126.4 5.2 %collective-permute-start.14 = (f32[8,128]{1,0:T(8,128)S(1)}, f32[8,128]{1,0:T(8,128)S(1)}, u32[]{:S(2)}, u32[]{:S(2)}) collective-permute-start(f32[8,128]{1,0:T(8,128)S(1)} %copy-done.11), channel_id=1, source_target_pairs={{0,3},{1,2},{2,1},{3,0},{4,7},{5,6},{6,5},{7,4},{8,11},{9,10},{10,... | collective-permute-start | bytes 12296 | tf_op jit(solution)/shard_map/ppermute | solution.py:470
  130.0 3.6 %collective-permute-start.13 = (f32[8,128]{1,0:T(8,128)S(1)}, f32[8,128]{1,0:T(8,128)S(1)}, u32[]{:S(2)}, u32[]{:S(2)}) collective-permute-start(f32[8,128]{1,0:T(8,128)S(1)} %copy-done.11), channel_id=1, source_target_pairs={{0,2},{1,3},{2,0},{3,1},{4,6},{5,7},{6,4},{7,5},{8,10},{9,11},{10,... | collective-permute-start | bytes 12296 | tf_op jit(solution)/shard_map/ppermute | solution.py:470
  130.6 3.6 %collective-permute-start.12 = (f32[8,128]{1,0:T(8,128)S(1)}, f32[8,128]{1,0:T(8,128)S(1)}, u32[]{:S(2)}, u32[]{:S(2)}) collective-permute-start(f32[8,128]{1,0:T(8,128)S(1)} %copy-done.11), channel_id=1, source_target_pairs={{0,1},{1,0},{2,3},{3,2},{4,5},{5,4},{6,7},{7,6},{8,9},{9,8},{10,11... | collective-permute-start | bytes 12296 | tf_op jit(solution)/shard_map/ppermute | solution.py:470
  134.8 4.7 %collective-permute-start.15 = (f32[8,128]{1,0:T(8,128)}, f32[8,128]{1,0:T(8,128)S(1)}, u32[]{:S(2)}, u32[]{:S(2)}) collective-permute-start(f32[8,128]{1,0:T(8,128)} %shard_map.69), channel_id=1, source_target_pairs={{0,4},{1,5},{2,6},{3,7},{4,0},{5,1},{6,2},{7,3},{8,12},{9,13},{10,... | collective-permute-start | bytes 12296 | tf_op jit(solution)/shard_map/ppermute | solution.py:470
  140.8 0.8 copy-start.1
  141.6 0.8 copy-start.2
  142.4 17.0 %collective-permute-start.18 = (f32[8,128]{1,0:T(8,128)}, f32[8,128]{1,0:T(8,128)S(1)}, u32[]{:S(2)}, u32[]{:S(2)}) collective-permute-start(f32[8,128]{1,0:T(8,128)} %shard_map.70.gate), channel_id=1, source_target_pairs={{0,24},{8,16},{16,8},{24,0},{1,25},{9,17},{17,9},{25,1},{2,26},{10... | collective-permute-start | bytes 12296 | tf_op jit(solution)/shard_map/ppermute | solution.py:470
  142.4 17.0 %collective-permute-start.17 = (f32[8,128]{1,0:T(8,128)}, f32[8,128]{1,0:T(8,128)S(1)}, u32[]{:S(2)}, u32[]{:S(2)}) collective-permute-start(f32[8,128]{1,0:T(8,128)} %shard_map.70.gate), channel_id=1, source_target_pairs={{0,16},{8,24},{16,0},{24,8},{1,17},{9,25},{17,1},{25,9},{2,18},{10... | collective-permute-start | bytes 12296 | tf_op jit(solution)/shard_map/ppermute | solution.py:470
  145.5 13.9 %collective-permute-start.16 = (f32[8,128]{1,0:T(8,128)}, f32[8,128]{1,0:T(8,128)S(1)}, u32[]{:S(2)}, u32[]{:S(2)}) collective-permute-start(f32[8,128]{1,0:T(8,128)} %shard_map.70.gate), channel_id=1, source_target_pairs={{0,8},{8,0},{16,24},{24,16},{1,9},{9,1},{17,25},{25,17},{2,10},{10... | collective-permute-start | bytes 12296 | tf_op jit(solution)/shard_map/ppermute | solution.py:470
  145.6 13.8 %copy-start.10 = (f32[8,128]{1,0:T(8,128)S(1)}, f32[8,128]{1,0:T(8,128)}, u32[]{:S(2)}) copy-start(f32[8,128]{1,0:T(8,128)} %shard_map.70.gate) | copy-start | bytes 12292

commit v6 on v5

--- a/solution.py
+++ b/solution.py
@@ -522,7 +522,8 @@
         [VMEM] * 2 + [ANY] * 2,
     )(velocity, stiffness)
     before, after_ = exchange(low_rows, high_rows, "row")
-    template = to_rows(to_blocks(template_scan, SENT, low_rows))
+    template_blocks = to_blocks(template_scan, SENT, low_rows)
+    template = to_rows(template_blocks)
     below, above = exchange(low, high, "sec")
     corners = call(corner_kernel, [(6 * WIDE * WIDE, width)] * 2, [VMEM] * 2)(before, after_)
     extended, reg, reg_sums = call(
@@ -534,7 +535,7 @@
         20 << 20,
     )(velocity, stiffness, below, above, before, after_, *exchange(*corners, "sec"))
 
-    fixed_blocks = to_blocks(reference_scan, 0, corners[0])
+    fixed_blocks = to_blocks(reference_scan, 0, template_blocks)
     low, high = call(slice_kernel, [(blocks, STEPS, tall, LANES)] * 2, [VMEM, ANY, ANY])(
         template, below, above
     )

time: 163 us -> 177 us (1.086)
  waiting for transfers between devices: 33.6 us -> 61.5 us
  starting transfers between devices: 61.2 us -> 48.2 us
    all_to_all x2, waiting for transfers between devices: 0.01 us -> 23.2 us  [to_rows(): lax.all_to_all(parts, 'row', split_axis=0, concat_axis=0, tiled=True)]
    all_to_all x2, starting transfers between devices: 20.8 us -> 11.7 us  [to_rows(): lax.all_to_all(parts, 'row', split_axis=0, concat_axis=0, tiled=True)]
    ppermute x6, waiting for transfers between devices: 7.11 us -> 12.1 us  [exchange(): above = lax.ppermute(low_part, axis, [(i + 1, i) for i in range(count - 1)])]
    ppermute x6, starting transfers between devices: 23.1 us -> 20.2 us  [exchange(): lax.ppermute(high_part, axis, [(i, i + 1) for i in range(count - 1)])]
    unnamed x28 -> x22, local copies, waits for them, and re-layouts: 4.52 us -> 3.79 us
  transfers between devices with their start and end apart: 21 -> 21, of which waited for: 8 -> 10; matrix products, arithmetic and copies ran while one was open for 2% -> 1% of each run, Pallas kernels for 25% -> 23%
where the time goes in v6:
time: 177 us; the launch traced here: 176 us
  waiting for transfers between devices  61.5 us (35%)
  Pallas kernels  56.7 us (32%)
  starting transfers between devices  48.2 us (27%)
  local copies, waits for them, and re-layouts  3.79 us (2%)
  other arithmetic  3.12 us (2%)
  between operations  2.66 us (2%)
    all_to_all x2, waiting for transfers between devices, to_rows(): lax.all_to_all(parts, 'row', split_axis=0, concat_axis=0, tiled=True)  23.2 us
    ppermute x6, starting transfers between devices, exchange(): lax.ppermute(high_part, axis, [(i, i + 1) for i in range(count - 1)])  20.2 us
    ppermute x6, waiting for transfers between devices, exchange(): lax.ppermute(high_part, axis, [(i, i + 1) for i in range(count - 1)])  18.7 us
    pallas_call x1, Pallas kernels, local(): call(adjoint_kernel, [velocity.shape], [SMEM] + [VMEM] * 5 + [ANY] * 7, [...  13.8 us
    pallas_call x1, Pallas kernels, local(): call(forward_kernel, [own, (STEPS - 1, blocks, sections + 2, tall, LANES)...  13.3 us
    ppermute x6, waiting for transfers between devices, exchange(): above = lax.ppermute(low_part, axis, [(i + 1, i) for i in range(count - 1)])  12.1 us
    all_to_all x2, starting transfers between devices, to_rows(): lax.all_to_all(parts, 'row', split_axis=0, concat_axis=0, tiled=True)  11.7 us
    pallas_call x1, Pallas kernels, local(): call(extend_kernel, [(3, blocks, deep, tall, LANES), velocity.shape, (TIL...  8.95 us
  transfers between devices with their start and end apart: 21, of which 10 were waited for; matrix products, arithmetic and copies ran while one was open for 1% of the time, Pallas kernels for 23%

profile of v6, /device:TPU:0, one launch (start us, length us, event | category | flops | bytes accessed | tf_op | source)
XLA Modules:
  0.0 176.0 jit_solution(10983186457807229559)
XLA Ops:
  0.6 4.6 %shard_map.59 = (f32[80,1024]{1,0:T(8,128)}, f32[80,1024]{1,0:T(8,128)}, f32[10,32,1024]{2,1,0:T(8,128)}, f32[10,32,1024]{2,1,0:T(8,128)}) custom-call(f32[3,8,32,1024]{3,2,1,0:T(8,128)} %vel.3, f32[8,32,1024]{2,1,0:T(8,128)} %sti.3), custom_call_target="tpu_custom_call" | custom-call | bytes 4194304 | tf_op jit(solution)/shard_map/pallas_call | solution.py:517
  5.2 3.3 %shard_map.60.gate = f32[8,8,40,128]{3,2,1,0:T(8,128)} custom-call(f32[8,128,256]{2,1,0:T(8,128)} %scan.2, f32[80,1024]{1,0:T(8,128)} %get-tuple-element.21.gate), custom_call_target="tpu_custom_call" | custom-call | bytes 4194304 | tf_op jit(solution)/shard_map/pallas_call | solution.py:452
  8.5 7.3 %all-to-all-start = ((f32[8,8,40,128]{3,2,1,0:T(8,128)}), f32[8,8,40,128]{3,2,1,0:T(8,128)}, u32[]{:S(2)}, u32[]{:S(2)}) async-start(f32[8,8,40,128]{3,2,1,0:T(8,128)} %shard_map.60.gate), calls=%async_computation | async-start | bytes 2621440 | tf_op jit(solution)/shard_map/all_to_all | solution.py:460
  15.8 2.6 %collective-permute-start = (f32[10,32,1024]{2,1,0:T(8,128)}, f32[10,32,1024]{2,1,0:T(8,128)}, u32[]{:S(2)}, u32[]{:S(2)}) collective-permute-start(f32[10,32,1024]{2,1,0:T(8,128)} %get-tuple-element.22), channel_id=1, source_target_pairs={{0,8},{8,16},{16,24},{1,9},{9,17},{17,25},{2,10},{10,18},{18,26},{... | collective-permute-start | bytes 3932168 | tf_op jit(solution)/shard_map/ppermute | solution.py:30
  18.4 1.3 collective-permute-start.1
  19.7 3.1 %shard_map.65.refs_0_ = f32[8,8,32,128]{3,2,1,0:T(8,128)} custom-call(f32[8,128,256]{2,1,0:T(8,128)} %scan.3, f32[8,8,40,128]{3,2,1,0:T(8,128)} %shard_map.60.gate), custom_call_target="tpu_custom_call" | custom-call | bytes 4194304 | tf_op jit(solution)/shard_map/pallas_call | solution.py:452
  22.7 1.3 collective-permute-done.1.gate_above.planes_above
  24.1 23.2 %all-to-all-done.field.own.start = f32[8,8,40,128]{3,2,1,0:T(8,128)} async-done(((f32[8,8,40,128]{3,2,1,0:T(8,128)}), f32[8,8,40,128]{3,2,1,0:T(8,128)}, u32[]{:S(2)}, u32[]{:S(2)}) %all-to-all-start) | async-done | bytes 1310752 | tf_op jit(solution)/shard_map/all_to_all | solution.py:460
  47.3 2.5 %shard_map.61 = (f32[8,4,40,128]{3,2,1,0:T(8,128)}, f32[8,4,40,128]{3,2,1,0:T(8,128)}) custom-call(f32[8,8,40,128]{3,2,1,0:T(8,128)} %all-to-all-done.field.own.start, f32[10,32,1024]{2,1,0:T(8,128)} %collective-permute-done.gate_below.planes_below, f32[10,32,1024]{2,1,0:T(8,128)} %collective-permute-done.1.gate_above.planes_above), custom_call_target="tpu_custom_call" | custom-call | bytes 4194304 | tf_op jit(solution)/shard_map/pallas_call | solution.py:539
  49.7 4.4 %all-to-all-start.1 = ((f32[8,8,32,128]{3,2,1,0:T(8,128)}), f32[8,8,32,128]{3,2,1,0:T(8,128)}, u32[]{:S(2)}, u32[]{:S(2)}) async-start(f32[8,8,32,128]{3,2,1,0:T(8,128)} %shard_map.66), calls=%async_computation.1 | async-start | bytes 2097152 | tf_op jit(solution)/shard_map/all_to_all | solution.py:460
  54.1 1.3 collective-permute-start.2
  55.5 1.3 collective-permute-start.3
  56.8 3.8 %collective-permute-start.4 = (f32[80,1024]{1,0:T(8,128)S(1)}, f32[80,1024]{1,0:T(8,128)S(1)}, u32[]{:S(2)}, u32[]{:S(2)}) collective-permute-start(f32[80,1024]{1,0:T(8,128)S(1)} %copy-done.10), channel_id=1, source_target_pairs={{0,1},{1,2},{2,3},{3,4},{4,5},{5,6},{6,7},{8,9},{9,10},{10,11},{11... | collective-permute-start | bytes 983048 | tf_op jit(solution)/shard_map/ppermute | solution.py:30
  60.6 1.3 collective-permute-start.5
  61.9 17.2 %collective-permute-done.4.before = f32[80,1024]{1,0:T(8,128)S(1)} collective-permute-done((f32[80,1024]{1,0:T(8,128)S(1)}, f32[80,1024]{1,0:T(8,128)S(1)}, u32[]{:S(2)}, u32[]{:S(2)}) %collective-permute-start.4) | collective-permute-done | bytes 327712 | tf_op jit(solution)/shard_map/ppermute | solution.py:30
  79.1 0.7 copy-done.3
  79.9 1.9 %shard_map.62 = (f32[54,1024]{1,0:T(8,128)}, f32[54,1024]{1,0:T(8,128)}) custom-call(f32[80,1024]{1,0:T(8,128)} %copy-done.3, f32[80,1024]{1,0:T(8,128)} %collective-permute-done.5.after), custom_call_target="tpu_custom_call" | custom-call | bytes 4194304 | tf_op jit(solution)/shard_map/pallas_call | solution.py:528
  81.8 2.7 %collective-permute-start.6 = (f32[54,1024]{1,0:T(8,128)}, f32[54,1024]{1,0:T(8,128)S(1)}, u32[]{:S(2)}, u32[]{:S(2)}) collective-permute-start(f32[54,1024]{1,0:T(8,128)} %get-tuple-element.27), channel_id=1, source_target_pairs={{0,8},{8,16},{16,24},{1,9},{9,17},{17,25},{2,10},{10,18},{18,26},{... | collective-permute-start | bytes 663560 | tf_op jit(solution)/shard_map/ppermute | solution.py:30
  84.5 1.3 collective-permute-start.7
  85.8 0.6 add_convert_fusion.flags
  86.5 3.2 %collective-permute-done.7.corners_above = f32[54,1024]{1,0:T(8,128)} collective-permute-done((f32[54,1024]{1,0:T(8,128)}, f32[54,1024]{1,0:T(8,128)}, u32[]{:S(2)}, u32[]{:S(2)}) %collective-permute-start.7) | collective-permute-done | bytes 221216 | tf_op jit(solution)/shard_map/ppermute | solution.py:31
  89.7 8.9 %shard_map.63 = (f32[3,8,14,40,128]{4,3,2,1,0:T(8,128)}, f32[3,8,32,1024]{3,2,1,0:T(8,128)}, f32[8,128]{1,0:T(8,128)}) custom-call(f32[3,8,32,1024]{3,2,1,0:T(8,128)} %vel.3, f32[8,32,1024]{2,1,0:T(8,128)} %sti.3, f32[10,32,1024]{2,1,0:T(8,128)} %collective-permute-done.gate_below.planes_below, ...), custom_call_target="tpu_custom_call" | custom-call | flops 20971520 | bytes 4194304 | tf_op jit(solution)/shard_map/pallas_call | solution.py:529
  98.7 0.8 copy-done
  99.5 13.3 %shard_map.64 = (f32[8,8,32,128]{3,2,1,0:T(8,128)}, f32[3,8,10,40,128]{4,3,2,1,0:T(8,128)}) custom-call(f32[4]{0:T(128)} %add_convert_fusion.flags, f32[8,8,40,128]{3,2,1,0:T(8,128)} %all-to-all-done.field.own.start, f32[8,4,40,128]{3,2,1,0:T(8,128)} %copy-done, f32[8,4,40,128]{3,2,1,0:T(8,128)} %collective-permute-done.3.above.start_above, ...), custom_call_target="tpu_custom_call" | custom-call | flops 20971520 | bytes 4194304 | tf_op jit(solution)/shard_map/pallas_call | solution.py:545
  112.8 2.9 %shard_map.67 = (f32[8,8,32,128]{3,2,1,0:T(8,128)}, f32[8,8,4,128]{3,2,1,0:T(4,128)}, f32[8,8,4,128]{3,2,1,0:T(4,128)}, f32[8,128]{1,0:T(8,128)}) custom-call(f32[8,8,32,128]{3,2,1,0:T(8,128)} %get-tuple-element.30.moved, f32[8,8,32,128]{3,2,1,0:T(8,128)} %all-to-all-done.1.fixed, f32[8,128]{1,0:T(8,128)} %get-tuple-element.31.sums), custom_call_target="tpu_custom_call" | custom-call | bytes 4194304 | tf_op jit(solution)/shard_map/pallas_call | solution.py:554
  115.8 4.5 %collective-permute-start.8 = (f32[8,8,4,128]{3,2,1,0:T(4,128)}, f32[8,8,4,128]{3,2,1,0:T(4,128)S(1)}, u32[]{:S(2)}, u32[]{:S(2)}) collective-permute-start(f32[8,8,4,128]{3,2,1,0:T(4,128)} %get-tuple-element.33), channel_id=1, source_target_pairs={{0,1},{1,2},{2,3},{3,4},{4,5},{5,6},{6,7},{8,9},{9,10},{10,11},{11... | collective-permute-start | bytes 393224 | tf_op jit(solution)/shard_map/ppermute | solution.py:30
  120.3 1.3 collective-permute-start.9
  121.6 1.5 collective-permute-done.8.before
  123.1 7.6 %collective-permute-done.9.after = f32[8,8,4,128]{3,2,1,0:T(4,128)S(1)} collective-permute-done((f32[8,8,4,128]{3,2,1,0:T(4,128)}, f32[8,8,4,128]{3,2,1,0:T(4,128)S(1)}, u32[]{:S(2)}, u32[]{:S(2)}) %collective-permute-start.9) | collective-permute-done | bytes 131104 | tf_op jit(solution)/shard_map/ppermute | solution.py:31
  130.7 0.6 copy-done.5
  131.3 2.3 %shard_map.68 = (f32[8,3,40,128]{3,2,1,0:T(8,128)}, f32[8,3,40,128]{3,2,1,0:T(8,128)}) custom-call(f32[8,8,32,128]{3,2,1,0:T(8,128)} %get-tuple-element.32.field.own, f32[8,8,4,128]{3,2,1,0:T(4,128)} %copy-done.4, f32[8,8,4,128]{3,2,1,0:T(4,128)} %copy-done.5), custom_call_target="tpu_custom_call" | custom-call | bytes 4194304 | tf_op jit(solution)/shard_map/pallas_call | solution.py:558
  133.7 5.2 %collective-permute-start.10 = (f32[8,3,40,128]{3,2,1,0:T(8,128)}, f32[8,3,40,128]{3,2,1,0:T(8,128)S(1)}, u32[]{:S(2)}, u32[]{:S(2)}) collective-permute-start(f32[8,3,40,128]{3,2,1,0:T(8,128)} %get-tuple-element.35), channel_id=1, source_target_pairs={{0,8},{8,16},{16,24},{1,9},{9,17},{17,25},{2,10},{10,18},{18,26},{... | collective-permute-start | bytes 1474568 | tf_op jit(solution)/shard_map/ppermute | solution.py:30
  138.9 1.3 collective-permute-start.11
  140.2 4.0 %collective-permute-start.14 = (f32[8,128]{1,0:T(8,128)S(1)}, f32[8,128]{1,0:T(8,128)S(1)}, u32[]{:S(2)}, u32[]{:S(2)}) collective-permute-start(f32[8,128]{1,0:T(8,128)S(1)} %copy-done.9), channel_id=1, source_target_pairs={{0,3},{1,2},{2,1},{3,0},{4,7},{5,6},{6,5},{7,4},{8,11},{9,10},{10,... | collective-permute-start | bytes 12296 | tf_op jit(solution)/shard_map/ppermute | solution.py:470
  144.2 0.2 collective-permute-start.13
  144.3 0.5 collective-permute-start.12
  144.8 0.9 collective-permute-done.14
  145.8 2.0 %collective-permute-done.13 = f32[8,128]{1,0:T(8,128)S(1)} collective-permute-done((f32[8,128]{1,0:T(8,128)S(1)}, f32[8,128]{1,0:T(8,128)S(1)}, u32[]{:S(2)}, u32[]{:S(2)}) %collective-permute-start.13) | collective-permute-done | bytes 4128 | tf_op jit(solution)/shard_map/ppermute | solution.py:470
  147.8 0.2 collective-permute-done.12
  148.0 0.6 select_add_fusion.refs_0_
  148.6 0.4 collective-permute-start.15
  148.9 4.3 %collective-permute-done.15 = f32[8,128]{1,0:T(8,128)S(1)} collective-permute-done((f32[8,128]{1,0:T(8,128)}, f32[8,128]{1,0:T(8,128)S(1)}, u32[]{:S(2)}, u32[]{:S(2)}) %collective-permute-start.15) | collective-permute-done | bytes 4128 | tf_op jit(solution)/shard_map/ppermute | solution.py:470
  153.3 1.3 add.34.refs_0_
  154.6 0.8 copy-done.1
  155.3 0.8 copy-done.2
  156.1 3.5 %collective-permute-start.17 = (f32[8,128]{1,0:T(8,128)}, f32[8,128]{1,0:T(8,128)S(1)}, u32[]{:S(2)}, u32[]{:S(2)}) collective-permute-start(f32[8,128]{1,0:T(8,128)} %shard_map.70.gate), channel_id=1, source_target_pairs={{0,16},{8,24},{16,0},{24,8},{1,17},{9,25},{17,1},{25,9},{2,18},{10... | collective-permute-start | bytes 12296 | tf_op jit(solution)/shard_map/ppermute | solution.py:470
  159.7 13.8 %shard_map.71 = f32[3,8,32,1024]{3,2,1,0:T(8,128)} custom-call(f32[4]{0:T(128)} %add_convert_fusion.flags, f32[8,8,32,128]{3,2,1,0:T(8,128)} %get-tuple-element.32.field.own, f32[8,3,40,128]{3,2,1,0:T(8,128)} %copy-done.1, f32[8,3,40,128]{3,2,1,0:T(8,128)} %copy-done.2, f32[8,8,4,128]{3,2,1,0:T(4,128)} %copy-done.4, f32[8,8,4,128]{3,2,1,0:T(4,128)} %copy-done.5, ...), custom_call_target="tpu_custom_call" | custom-call | flops 20971520 | bytes 4194304 | tf_op jit(solution)/shard_map/pallas_call | solution.py:565
  173.6 0.6 add_reduce_fusion
  (33 shorter events, 0.1 us)
Async XLA Ops:
  8.5 38.8 %all-to-all-start = ((f32[8,8,40,128]{3,2,1,0:T(8,128)}), f32[8,8,40,128]{3,2,1,0:T(8,128)}, u32[]{:S(2)}, u32[]{:S(2)}) async-start(f32[8,8,40,128]{3,2,1,0:T(8,128)} %shard_map.60.gate), calls=%async_computation | async-start | bytes 2621440 | tf_op jit(solution)/shard_map/all_to_all | solution.py:460
  15.8 7.0 %collective-permute-start = (f32[10,32,1024]{2,1,0:T(8,128)}, f32[10,32,1024]{2,1,0:T(8,128)}, u32[]{:S(2)}, u32[]{:S(2)}) collective-permute-start(f32[10,32,1024]{2,1,0:T(8,128)} %get-tuple-element.22), channel_id=1, source_target_pairs={{0,8},{8,16},{16,24},{1,9},{9,17},{17,25},{2,10},{10,18},{18,26},{... | collective-permute-start | bytes 3932168 | tf_op jit(solution)/shard_map/ppermute | solution.py:30
  18.4 5.7 %collective-permute-start.1 = (f32[10,32,1024]{2,1,0:T(8,128)}, f32[10,32,1024]{2,1,0:T(8,128)}, u32[]{:S(2)}, u32[]{:S(2)}) collective-permute-start(f32[10,32,1024]{2,1,0:T(8,128)} %get-tuple-element.23), channel_id=1, source_target_pairs={{8,0},{16,8},{24,16},{9,1},{17,9},{25,17},{10,2},{18,10},{26,18},{... | collective-permute-start | bytes 3932168 | tf_op jit(solution)/shard_map/ppermute | solution.py:31
  49.7 7.0 %copy-start.10 = (f32[80,1024]{1,0:T(8,128)S(1)}, f32[80,1024]{1,0:T(8,128)}, u32[]{:S(2)}) copy-start(f32[80,1024]{1,0:T(8,128)} %get-tuple-element.26) | copy-start | bytes 983044
  49.7 10.9 %copy-start.6 = (f32[80,1024]{1,0:T(8,128)S(1)}, f32[80,1024]{1,0:T(8,128)}, u32[]{:S(2)}) copy-start(f32[80,1024]{1,0:T(8,128)} %get-tuple-element.21.gate) | copy-start | bytes 983044
  49.7 63.1 %all-to-all-start.1 = ((f32[8,8,32,128]{3,2,1,0:T(8,128)}), f32[8,8,32,128]{3,2,1,0:T(8,128)}, u32[]{:S(2)}, u32[]{:S(2)}) async-start(f32[8,8,32,128]{3,2,1,0:T(8,128)} %shard_map.66), calls=%async_computation.1 | async-start | bytes 2097152 | tf_op jit(solution)/shard_map/all_to_all | solution.py:460
  54.1 44.5 %collective-permute-start.2 = (f32[8,4,40,128]{3,2,1,0:T(8,128)}, f32[8,4,40,128]{3,2,1,0:T(8,128)S(1)}, u32[]{:S(2)}, u32[]{:S(2)}) collective-permute-start(f32[8,4,40,128]{3,2,1,0:T(8,128)} %get-tuple-element.24), channel_id=1, source_target_pairs={{0,8},{8,16},{16,24},{1,9},{9,17},{17,25},{2,10},{10,18},{18,26},{... | collective-permute-start | bytes 1966088 | tf_op jit(solution)/shard_map/ppermute | solution.py:30
  55.5 43.2 %collective-permute-start.3 = (f32[8,4,40,128]{3,2,1,0:T(8,128)}, f32[8,4,40,128]{3,2,1,0:T(8,128)}, u32[]{:S(2)}, u32[]{:S(2)}) collective-permute-start(f32[8,4,40,128]{3,2,1,0:T(8,128)} %get-tuple-element.25.refs_1_), channel_id=1, source_target_pairs={{8,0},{16,8},{24,16},{9,1},{17,9},{25,17},{10,2},{18,10},{26,18},{... | collective-permute-start | bytes 1966088 | tf_op jit(solution)/shard_map/ppermute | solution.py:31
  56.8 22.3 %collective-permute-start.4 = (f32[80,1024]{1,0:T(8,128)S(1)}, f32[80,1024]{1,0:T(8,128)S(1)}, u32[]{:S(2)}, u32[]{:S(2)}) collective-permute-start(f32[80,1024]{1,0:T(8,128)S(1)} %copy-done.10), channel_id=1, source_target_pairs={{0,1},{1,2},{2,3},{3,4},{4,5},{5,6},{6,7},{8,9},{9,10},{10,11},{11... | collective-permute-start | bytes 983048 | tf_op jit(solution)/shard_map/ppermute | solution.py:30
  60.6 18.5 %collective-permute-start.5 = (f32[80,1024]{1,0:T(8,128)S(1)}, f32[80,1024]{1,0:T(8,128)}, u32[]{:S(2)}, u32[]{:S(2)}) collective-permute-start(f32[80,1024]{1,0:T(8,128)S(1)} %copy-done.6), channel_id=1, source_target_pairs={{1,0},{2,1},{3,2},{4,3},{5,4},{6,5},{7,6},{9,8},{10,9},{11,10},{12... | collective-permute-start | bytes 983048 | tf_op jit(solution)/shard_map/ppermute | solution.py:31
  79.1 0.7 copy-start.3
  81.8 4.7 %collective-permute-start.6 = (f32[54,1024]{1,0:T(8,128)}, f32[54,1024]{1,0:T(8,128)S(1)}, u32[]{:S(2)}, u32[]{:S(2)}) collective-permute-start(f32[54,1024]{1,0:T(8,128)} %get-tuple-element.27), channel_id=1, source_target_pairs={{0,8},{8,16},{16,24},{1,9},{9,17},{17,25},{2,10},{10,18},{18,26},{... | collective-permute-start | bytes 663560 | tf_op jit(solution)/shard_map/ppermute | solution.py:30
  84.5 5.2 %collective-permute-start.7 = (f32[54,1024]{1,0:T(8,128)}, f32[54,1024]{1,0:T(8,128)}, u32[]{:S(2)}, u32[]{:S(2)}) collective-permute-start(f32[54,1024]{1,0:T(8,128)} %get-tuple-element.28), channel_id=1, source_target_pairs={{8,0},{16,8},{24,16},{9,1},{17,9},{25,17},{10,2},{18,10},{26,18},{... | collective-permute-start | bytes 663560 | tf_op jit(solution)/shard_map/ppermute | solution.py:31
  86.5 3.2 %copy-start.7 = (f32[54,1024]{1,0:T(8,128)}, f32[54,1024]{1,0:T(8,128)S(1)}, u32[]{:S(2)}) copy-start(f32[54,1024]{1,0:T(8,128)S(1)} %collective-permute-done.6.corners_below) | copy-start | bytes 663556
  98.6 0.8 copy-start
  115.8 24.4 %copy-start.9 = (f32[8,128]{1,0:T(8,128)S(1)}, f32[8,128]{1,0:T(8,128)}, u32[]{:S(2)}) copy-start(f32[8,128]{1,0:T(8,128)} %get-tuple-element.39) | copy-start | bytes 12292
  115.8 7.3 %collective-permute-start.8 = (f32[8,8,4,128]{3,2,1,0:T(4,128)}, f32[8,8,4,128]{3,2,1,0:T(4,128)S(1)}, u32[]{:S(2)}, u32[]{:S(2)}) collective-permute-start(f32[8,8,4,128]{3,2,1,0:T(4,128)} %get-tuple-element.33), channel_id=1, source_target_pairs={{0,1},{1,2},{2,3},{3,4},{4,5},{5,6},{6,7},{8,9},{9,10},{10,11},{11... | collective-permute-start | bytes 393224 | tf_op jit(solution)/shard_map/ppermute | solution.py:30
  120.3 10.4 %collective-permute-start.9 = (f32[8,8,4,128]{3,2,1,0:T(4,128)}, f32[8,8,4,128]{3,2,1,0:T(4,128)S(1)}, u32[]{:S(2)}, u32[]{:S(2)}) collective-permute-start(f32[8,8,4,128]{3,2,1,0:T(4,128)} %get-tuple-element.34), channel_id=1, source_target_pairs={{1,0},{2,1},{3,2},{4,3},{5,4},{6,5},{7,6},{9,8},{10,9},{11,10},{12... | collective-permute-start | bytes 393224 | tf_op jit(solution)/shard_map/ppermute | solution.py:31
  123.1 7.6 %copy-start.4 = (f32[8,8,4,128]{3,2,1,0:T(4,128)}, f32[8,8,4,128]{3,2,1,0:T(4,128)S(1)}, u32[]{:S(2)}) copy-start(f32[8,8,4,128]{3,2,1,0:T(4,128)S(1)} %collective-permute-done.8.before) | copy-start | bytes 393220
  130.7 0.6 copy-start.5
  133.7 20.9 %collective-permute-start.10 = (f32[8,3,40,128]{3,2,1,0:T(8,128)}, f32[8,3,40,128]{3,2,1,0:T(8,128)S(1)}, u32[]{:S(2)}, u32[]{:S(2)}) collective-permute-start(f32[8,3,40,128]{3,2,1,0:T(8,128)} %get-tuple-element.35), channel_id=1, source_target_pairs={{0,8},{8,16},{16,24},{1,9},{9,17},{17,25},{2,10},{10,18},{18,26},{... | collective-permute-start | bytes 1474568 | tf_op jit(solution)/shard_map/ppermute | solution.py:30
  138.9 15.7 %collective-permute-start.11 = (f32[8,3,40,128]{3,2,1,0:T(8,128)}, f32[8,3,40,128]{3,2,1,0:T(8,128)S(1)}, u32[]{:S(2)}, u32[]{:S(2)}) collective-permute-start(f32[8,3,40,128]{3,2,1,0:T(8,128)} %get-tuple-element.36.refs_1_), channel_id=1, source_target_pairs={{8,0},{16,8},{24,16},{9,1},{17,9},{25,17},{10,2},{18,10},{26,18},{... | collective-permute-start | bytes 1474568 | tf_op jit(solution)/shard_map/ppermute | solution.py:31
  140.2 5.6 %collective-permute-start.14 = (f32[8,128]{1,0:T(8,128)S(1)}, f32[8,128]{1,0:T(8,128)S(1)}, u32[]{:S(2)}, u32[]{:S(2)}) collective-permute-start(f32[8,128]{1,0:T(8,128)S(1)} %copy-done.9), channel_id=1, source_target_pairs={{0,3},{1,2},{2,1},{3,0},{4,7},{5,6},{6,5},{7,4},{8,11},{9,10},{10,... | collective-permute-start | bytes 12296 | tf_op jit(solution)/shard_map/ppermute | solution.py:470
  144.2 3.6 %collective-permute-start.13 = (f32[8,128]{1,0:T(8,128)S(1)}, f32[8,128]{1,0:T(8,128)S(1)}, u32[]{:S(2)}, u32[]{:S(2)}) collective-permute-start(f32[8,128]{1,0:T(8,128)S(1)} %copy-done.9), channel_id=1, source_target_pairs={{0,2},{1,3},{2,0},{3,1},{4,6},{5,7},{6,4},{7,5},{8,10},{9,11},{10,... | collective-permute-start | bytes 12296 | tf_op jit(solution)/shard_map/ppermute | solution.py:470
  144.3 3.6 %collective-permute-start.12 = (f32[8,128]{1,0:T(8,128)S(1)}, f32[8,128]{1,0:T(8,128)S(1)}, u32[]{:S(2)}, u32[]{:S(2)}) collective-permute-start(f32[8,128]{1,0:T(8,128)S(1)} %copy-done.9), channel_id=1, source_target_pairs={{0,1},{1,0},{2,3},{3,2},{4,5},{5,4},{6,7},{7,6},{8,9},{9,8},{10,11... | collective-permute-start | bytes 12296 | tf_op jit(solution)/shard_map/ppermute | solution.py:470
  148.6 4.7 %collective-permute-start.15 = (f32[8,128]{1,0:T(8,128)}, f32[8,128]{1,0:T(8,128)S(1)}, u32[]{:S(2)}, u32[]{:S(2)}) collective-permute-start(f32[8,128]{1,0:T(8,128)} %shard_map.69), channel_id=1, source_target_pairs={{0,4},{1,5},{2,6},{3,7},{4,0},{5,1},{6,2},{7,3},{8,12},{9,13},{10,... | collective-permute-start | bytes 12296 | tf_op jit(solution)/shard_map/ppermute | solution.py:470
  154.5 0.8 copy-start.1
  155.3 0.8 copy-start.2
  156.1 17.4 %collective-permute-start.18 = (f32[8,128]{1,0:T(8,128)}, f32[8,128]{1,0:T(8,128)S(1)}, u32[]{:S(2)}, u32[]{:S(2)}) collective-permute-start(f32[8,128]{1,0:T(8,128)} %shard_map.70.gate), channel_id=1, source_target_pairs={{0,24},{8,16},{16,8},{24,0},{1,25},{9,17},{17,9},{25,1},{2,26},{10... | collective-permute-start | bytes 12296 | tf_op jit(solution)/shard_map/ppermute | solution.py:470
  156.1 17.4 %collective-permute-start.17 = (f32[8,128]{1,0:T(8,128)}, f32[8,128]{1,0:T(8,128)S(1)}, u32[]{:S(2)}, u32[]{:S(2)}) collective-permute-start(f32[8,128]{1,0:T(8,128)} %shard_map.70.gate), channel_id=1, source_target_pairs={{0,16},{8,24},{16,0},{24,8},{1,17},{9,25},{17,1},{25,9},{2,18},{10... | collective-permute-start | bytes 12296 | tf_op jit(solution)/shard_map/ppermute | solution.py:470
  159.6 13.9 %collective-permute-start.16 = (f32[8,128]{1,0:T(8,128)}, f32[8,128]{1,0:T(8,128)S(1)}, u32[]{:S(2)}, u32[]{:S(2)}) collective-permute-start(f32[8,128]{1,0:T(8,128)} %shard_map.70.gate), channel_id=1, source_target_pairs={{0,8},{8,0},{16,24},{24,16},{1,9},{9,1},{17,25},{25,17},{2,10},{10... | collective-permute-start | bytes 12296 | tf_op jit(solution)/shard_map/ppermute | solution.py:470
  159.7 13.9 %copy-start.8 = (f32[8,128]{1,0:T(8,128)S(1)}, f32[8,128]{1,0:T(8,128)}, u32[]{:S(2)}) copy-start(f32[8,128]{1,0:T(8,128)} %shard_map.70.gate) | copy-start | bytes 12292

commit v7 on v6

--- a/solution.py
+++ b/solution.py
@@ -86,8 +86,8 @@
     lax.fori_loop(0, sections, section, 0)
 
 
-def slice_kernel(field, gate_below, gate_above, low, high):
-    del gate_below, gate_above
+def slice_kernel(field, gate_below, gate_above, gate_corners, low, high):
+    del gate_below, gate_above, gate_corners
     blocks, sections = field.shape[:2]
     width = low.shape[1]
 
@@ -536,8 +536,8 @@
     )(velocity, stiffness, below, above, before, after_, *exchange(*corners, "sec"))
 
     fixed_blocks = to_blocks(reference_scan, 0, template_blocks)
-    low, high = call(slice_kernel, [(blocks, STEPS, tall, LANES)] * 2, [VMEM, ANY, ANY])(
-        template, below, above
+    low, high = call(slice_kernel, [(blocks, STEPS, tall, LANES)] * 2, [VMEM, ANY, ANY, ANY])(
+        template, below, above, corners[0]
     )
     start = (template,) + exchange(low, high, "sec")
     fixed = to_rows(after(fixed_blocks, low))

time: 177 us -> 160 us (0.904)
  waiting for transfers between devices: 61.5 us -> 32.1 us
  starting transfers between devices: 48.2 us -> 59.6 us
    all_to_all x2, waiting for transfers between devices: 23.2 us -> 1.74 us  [to_rows(): lax.all_to_all(parts, 'row', split_axis=0, concat_axis=0, tiled=True)]
    all_to_all x2, starting transfers between devices: 11.7 us -> 19.2 us  [to_rows(): lax.all_to_all(parts, 'row', split_axis=0, concat_axis=0, tiled=True)]
    ppermute x6, waiting for transfers between devices: 12.1 us -> 7.02 us  [exchange(): above = lax.ppermute(low_part, axis, [(i + 1, i) for i in range(count - 1)])]
    ppermute x6, starting transfers between devices: 20.2 us -> 23.1 us  [exchange(): lax.ppermute(high_part, axis, [(i, i + 1) for i in range(count - 1)])]
    unnamed x22 -> x26, local copies, waits for them, and re-layouts: 3.79 us -> 4.52 us
  transfers between devices with their start and end apart: 21 -> 21, of which waited for: 10 -> 9; matrix products, arithmetic and copies ran while one was open for 1% -> 2% of each run, Pallas kernels for 23% -> 26%
where the time goes in v7:
time: 160 us; the launch traced here: 159 us
  starting transfers between devices  59.6 us (37%)
  Pallas kernels  56.7 us (35%)
  waiting for transfers between devices  32.1 us (20%)
  local copies, waits for them, and re-layouts  4.52 us (3%)
  other arithmetic  3.14 us (2%)
  between operations  2.66 us (2%)
    ppermute x6, starting transfers between devices, exchange(): lax.ppermute(high_part, axis, [(i, i + 1) for i in range(count - 1)])  23.1 us
    all_to_all x2, starting transfers between devices, to_rows(): lax.all_to_all(parts, 'row', split_axis=0, concat_axis=0, tiled=True)  19.2 us
    ppermute x6, waiting for transfers between devices, exchange(): lax.ppermute(high_part, axis, [(i, i + 1) for i in range(count - 1)])  17.2 us
    pallas_call x1, Pallas kernels, local(): call(adjoint_kernel, [velocity.shape], [SMEM] + [VMEM] * 5 + [ANY] * 7, [...  13.8 us
    pallas_call x1, Pallas kernels, local(): call(forward_kernel, [own, (STEPS - 1, blocks, sections + 2, tall, LANES)...  13.3 us
    ppermute x7, starting transfers between devices, summed(): lax.ppermute(part, axis, [(i, i ^ low) for i in range(count)])  9.54 us
    pallas_call x1, Pallas kernels, local(): call(extend_kernel, [(3, blocks, deep, tall, LANES), velocity.shape, (TIL...  8.94 us
    ppermute x6, starting transfers between devices, exchange(): above = lax.ppermute(low_part, axis, [(i + 1, i) for i in range(count - 1)])  7.74 us
  transfers between devices with their start and end apart: 21, of which 9 were waited for; matrix products, arithmetic and copies ran while one was open for 2% of the time, Pallas kernels for 26%

profile of v7, /device:TPU:0, one launch (start us, length us, event | category | flops | bytes accessed | tf_op | source)
XLA Modules:
  0.0 158.7 jit_solution(11760609674014302405)
XLA Ops:
  0.6 4.6 %shard_map.59 = (f32[80,1024]{1,0:T(8,128)}, f32[80,1024]{1,0:T(8,128)}, f32[10,32,1024]{2,1,0:T(8,128)}, f32[10,32,1024]{2,1,0:T(8,128)}) custom-call(f32[3,8,32,1024]{3,2,1,0:T(8,128)} %vel.3, f32[8,32,1024]{2,1,0:T(8,128)} %sti.3), custom_call_target="tpu_custom_call" | custom-call | bytes 4194304 | tf_op jit(solution)/shard_map/pallas_call | solution.py:517
  5.2 3.3 %shard_map.60.gate = f32[8,8,40,128]{3,2,1,0:T(8,128)} custom-call(f32[8,128,256]{2,1,0:T(8,128)} %scan.2, f32[80,1024]{1,0:T(8,128)} %get-tuple-element.21.gate), custom_call_target="tpu_custom_call" | custom-call | bytes 4194304 | tf_op jit(solution)/shard_map/pallas_call | solution.py:452
  8.5 7.4 %all-to-all-start = ((f32[8,8,40,128]{3,2,1,0:T(8,128)}), f32[8,8,40,128]{3,2,1,0:T(8,128)}, u32[]{:S(2)}, u32[]{:S(2)}) async-start(f32[8,8,40,128]{3,2,1,0:T(8,128)} %shard_map.60.gate), calls=%async_computation | async-start | bytes 2621440 | tf_op jit(solution)/shard_map/all_to_all | solution.py:460
  15.9 2.6 %collective-permute-start = (f32[10,32,1024]{2,1,0:T(8,128)}, f32[10,32,1024]{2,1,0:T(8,128)}, u32[]{:S(2)}, u32[]{:S(2)}) collective-permute-start(f32[10,32,1024]{2,1,0:T(8,128)} %get-tuple-element.22), channel_id=1, source_target_pairs={{0,8},{8,16},{16,24},{1,9},{9,17},{17,25},{2,10},{10,18},{18,26},{... | collective-permute-start | bytes 3932168 | tf_op jit(solution)/shard_map/ppermute | solution.py:30
  18.5 1.3 collective-permute-start.1
  19.8 3.8 %collective-permute-start.2 = (f32[80,1024]{1,0:T(8,128)}, f32[80,1024]{1,0:T(8,128)S(1)}, u32[]{:S(2)}, u32[]{:S(2)}) collective-permute-start(f32[80,1024]{1,0:T(8,128)} %get-tuple-element.24), channel_id=1, source_target_pairs={{0,1},{1,2},{2,3},{3,4},{4,5},{5,6},{6,7},{8,9},{9,10},{10,11},{11... | collective-permute-start | bytes 983048 | tf_op jit(solution)/shard_map/ppermute | solution.py:30
  23.6 1.3 collective-permute-start.3
  24.9 3.1 %shard_map.65.refs_0_ = f32[8,8,32,128]{3,2,1,0:T(8,128)} custom-call(f32[8,128,256]{2,1,0:T(8,128)} %scan.3, f32[8,8,40,128]{3,2,1,0:T(8,128)} %shard_map.60.gate), custom_call_target="tpu_custom_call" | custom-call | bytes 4194304 | tf_op jit(solution)/shard_map/pallas_call | solution.py:452
  28.0 15.7 %collective-permute-done.2.before = f32[80,1024]{1,0:T(8,128)S(1)} collective-permute-done((f32[80,1024]{1,0:T(8,128)}, f32[80,1024]{1,0:T(8,128)S(1)}, u32[]{:S(2)}, u32[]{:S(2)}) %collective-permute-start.2) | collective-permute-done | bytes 327712 | tf_op jit(solution)/shard_map/ppermute | solution.py:30
  43.7 0.7 copy-done.3
  44.4 0.7 copy-done.4
  45.1 1.9 %shard_map.61 = (f32[54,1024]{1,0:T(8,128)}, f32[54,1024]{1,0:T(8,128)}) custom-call(f32[80,1024]{1,0:T(8,128)} %copy-done.3, f32[80,1024]{1,0:T(8,128)} %copy-done.4), custom_call_target="tpu_custom_call" | custom-call | bytes 4194304 | tf_op jit(solution)/shard_map/pallas_call | solution.py:528
  47.1 1.7 %all-to-all-done.field.own.start = f32[8,8,40,128]{3,2,1,0:T(8,128)} async-done(((f32[8,8,40,128]{3,2,1,0:T(8,128)}), f32[8,8,40,128]{3,2,1,0:T(8,128)}, u32[]{:S(2)}, u32[]{:S(2)}) %all-to-all-start) | async-done | bytes 1310752 | tf_op jit(solution)/shard_map/all_to_all | solution.py:460
  48.8 2.5 %shard_map.62 = (f32[8,4,40,128]{3,2,1,0:T(8,128)}, f32[8,4,40,128]{3,2,1,0:T(8,128)}) custom-call(f32[8,8,40,128]{3,2,1,0:T(8,128)} %all-to-all-done.field.own.start, f32[10,32,1024]{2,1,0:T(8,128)} %collective-permute-done.gate_below.planes_below, f32[10,32,1024]{2,1,0:T(8,128)} %collective-permute-done.1.gate_above.planes_above, ...), custom_call_target="tpu_custom_call" | custom-call | bytes 4194304 | tf_op jit(solution)/shard_map/pallas_call | solution.py:539
  51.3 11.8 %all-to-all-start.1 = ((f32[8,8,32,128]{3,2,1,0:T(8,128)}), f32[8,8,32,128]{3,2,1,0:T(8,128)}, u32[]{:S(2)}, u32[]{:S(2)}) async-start(f32[8,8,32,128]{3,2,1,0:T(8,128)} %shard_map.66), calls=%async_computation.1 | async-start | bytes 2097152 | tf_op jit(solution)/shard_map/all_to_all | solution.py:460
  63.1 1.7 %collective-permute-start.4 = (f32[8,4,40,128]{3,2,1,0:T(8,128)}, f32[8,4,40,128]{3,2,1,0:T(8,128)S(1)}, u32[]{:S(2)}, u32[]{:S(2)}) collective-permute-start(f32[8,4,40,128]{3,2,1,0:T(8,128)} %get-tuple-element.26), channel_id=1, source_target_pairs={{0,8},{8,16},{16,24},{1,9},{9,17},{17,25},{2,10},{10,18},{18,26},{... | collective-permute-start | bytes 1966088 | tf_op jit(solution)/shard_map/ppermute | solution.py:30
  64.8 1.3 collective-permute-start.5
  66.1 4.4 %collective-permute-start.6 = (f32[54,1024]{1,0:T(8,128)S(1)}, f32[54,1024]{1,0:T(8,128)S(1)}, u32[]{:S(2)}, u32[]{:S(2)}) collective-permute-start(f32[54,1024]{1,0:T(8,128)S(1)} %copy-done.12), channel_id=1, source_target_pairs={{0,8},{8,16},{16,24},{1,9},{9,17},{17,25},{2,10},{10,18},{18,26},{... | collective-permute-start | bytes 663560 | tf_op jit(solution)/shard_map/ppermute | solution.py:30
  70.5 1.3 collective-permute-start.7
  71.8 0.7 add_convert_fusion.flags
  72.5 2.8 %collective-permute-done.7.corners_above = f32[54,1024]{1,0:T(8,128)} collective-permute-done((f32[54,1024]{1,0:T(8,128)S(1)}, f32[54,1024]{1,0:T(8,128)}, u32[]{:S(2)}, u32[]{:S(2)}) %collective-permute-start.7) | collective-permute-done | bytes 221216 | tf_op jit(solution)/shard_map/ppermute | solution.py:31
  75.3 8.9 %shard_map.63 = (f32[3,8,14,40,128]{4,3,2,1,0:T(8,128)}, f32[3,8,32,1024]{3,2,1,0:T(8,128)}, f32[8,128]{1,0:T(8,128)}) custom-call(f32[3,8,32,1024]{3,2,1,0:T(8,128)} %vel.3, f32[8,32,1024]{2,1,0:T(8,128)} %sti.3, f32[10,32,1024]{2,1,0:T(8,128)} %collective-permute-done.gate_below.planes_below, ...), custom_call_target="tpu_custom_call" | custom-call | flops 20971520 | bytes 4194304 | tf_op jit(solution)/shard_map/pallas_call | solution.py:529
  84.2 0.8 copy-done
  85.0 13.3 %shard_map.64 = (f32[8,8,32,128]{3,2,1,0:T(8,128)}, f32[3,8,10,40,128]{4,3,2,1,0:T(8,128)}) custom-call(f32[4]{0:T(128)} %add_convert_fusion.flags, f32[8,8,40,128]{3,2,1,0:T(8,128)} %all-to-all-done.field.own.start, f32[8,4,40,128]{3,2,1,0:T(8,128)} %copy-done, f32[8,4,40,128]{3,2,1,0:T(8,128)} %collective-permute-done.5.above.start_above, ...), custom_call_target="tpu_custom_call" | custom-call | flops 20971520 | bytes 4194304 | tf_op jit(solution)/shard_map/pallas_call | solution.py:545
  98.4 3.0 %shard_map.67 = (f32[8,8,32,128]{3,2,1,0:T(8,128)}, f32[8,8,4,128]{3,2,1,0:T(4,128)}, f32[8,8,4,128]{3,2,1,0:T(4,128)}, f32[8,128]{1,0:T(8,128)}) custom-call(f32[8,8,32,128]{3,2,1,0:T(8,128)} %get-tuple-element.30.moved, f32[8,8,32,128]{3,2,1,0:T(8,128)} %all-to-all-done.1.fixed, f32[8,128]{1,0:T(8,128)} %get-tuple-element.31.sums), custom_call_target="tpu_custom_call" | custom-call | bytes 4194304 | tf_op jit(solution)/shard_map/pallas_call | solution.py:554
  101.4 4.1 %collective-permute-start.8 = (f32[8,8,4,128]{3,2,1,0:T(4,128)}, f32[8,8,4,128]{3,2,1,0:T(4,128)S(1)}, u32[]{:S(2)}, u32[]{:S(2)}) collective-permute-start(f32[8,8,4,128]{3,2,1,0:T(4,128)} %get-tuple-element.33), channel_id=1, source_target_pairs={{0,1},{1,2},{2,3},{3,4},{4,5},{5,6},{6,7},{8,9},{9,10},{10,11},{11... | collective-permute-start | bytes 393224 | tf_op jit(solution)/shard_map/ppermute | solution.py:30
  105.4 1.3 collective-permute-start.9
  106.7 1.5 collective-permute-done.8.before
  108.2 4.3 %collective-permute-done.9.after = f32[8,8,4,128]{3,2,1,0:T(4,128)S(1)} collective-permute-done((f32[8,8,4,128]{3,2,1,0:T(4,128)}, f32[8,8,4,128]{3,2,1,0:T(4,128)S(1)}, u32[]{:S(2)}, u32[]{:S(2)}) %collective-permute-start.9) | collective-permute-done | bytes 131104 | tf_op jit(solution)/shard_map/ppermute | solution.py:31
  112.5 0.6 copy-done.6
  113.2 2.3 %shard_map.68 = (f32[8,3,40,128]{3,2,1,0:T(8,128)}, f32[8,3,40,128]{3,2,1,0:T(8,128)}) custom-call(f32[8,8,32,128]{3,2,1,0:T(8,128)} %get-tuple-element.32.field.own, f32[8,8,4,128]{3,2,1,0:T(4,128)} %copy-done.5, f32[8,8,4,128]{3,2,1,0:T(4,128)} %copy-done.6), custom_call_target="tpu_custom_call" | custom-call | bytes 4194304 | tf_op jit(solution)/shard_map/pallas_call | solution.py:558
  115.5 6.6 %collective-permute-start.10 = (f32[8,3,40,128]{3,2,1,0:T(8,128)}, f32[8,3,40,128]{3,2,1,0:T(8,128)S(1)}, u32[]{:S(2)}, u32[]{:S(2)}) collective-permute-start(f32[8,3,40,128]{3,2,1,0:T(8,128)} %get-tuple-element.35), channel_id=1, source_target_pairs={{0,8},{8,16},{16,24},{1,9},{9,17},{17,25},{2,10},{10,18},{18,26},{... | collective-permute-start | bytes 1474568 | tf_op jit(solution)/shard_map/ppermute | solution.py:30
  122.1 1.3 collective-permute-start.11
  123.4 3.6 %collective-permute-start.14 = (f32[8,128]{1,0:T(8,128)S(1)}, f32[8,128]{1,0:T(8,128)S(1)}, u32[]{:S(2)}, u32[]{:S(2)}) collective-permute-start(f32[8,128]{1,0:T(8,128)S(1)} %copy-done.11), channel_id=1, source_target_pairs={{0,3},{1,2},{2,1},{3,0},{4,7},{5,6},{6,5},{7,4},{8,11},{9,10},{10,... | collective-permute-start | bytes 12296 | tf_op jit(solution)/shard_map/ppermute | solution.py:470
  127.0 0.5 collective-permute-start.13
  127.5 0.1 collective-permute-start.12
  127.6 0.9 collective-permute-done.14
  128.6 2.0 %collective-permute-done.13 = f32[8,128]{1,0:T(8,128)S(1)} collective-permute-done((f32[8,128]{1,0:T(8,128)S(1)}, f32[8,128]{1,0:T(8,128)S(1)}, u32[]{:S(2)}, u32[]{:S(2)}) %collective-permute-start.13) | collective-permute-done | bytes 4128 | tf_op jit(solution)/shard_map/ppermute | solution.py:470
  130.6 0.5 collective-permute-done.12
  131.1 0.6 select_add_fusion.refs_0_
  131.7 2.1 %collective-permute-start.15 = (f32[8,128]{1,0:T(8,128)}, f32[8,128]{1,0:T(8,128)S(1)}, u32[]{:S(2)}, u32[]{:S(2)}) collective-permute-start(f32[8,128]{1,0:T(8,128)} %shard_map.69), channel_id=1, source_target_pairs={{0,4},{1,5},{2,6},{3,7},{4,0},{5,1},{6,2},{7,3},{8,12},{9,13},{10,... | collective-permute-start | bytes 12296 | tf_op jit(solution)/shard_map/ppermute | solution.py:470
  133.8 2.6 %collective-permute-done.15 = f32[8,128]{1,0:T(8,128)S(1)} collective-permute-done((f32[8,128]{1,0:T(8,128)}, f32[8,128]{1,0:T(8,128)S(1)}, u32[]{:S(2)}, u32[]{:S(2)}) %collective-permute-start.15) | collective-permute-done | bytes 4128 | tf_op jit(solution)/shard_map/ppermute | solution.py:470
  136.5 1.3 add.34.refs_0_
  137.7 0.8 copy-done.1
  138.5 0.8 copy-done.2
  139.3 3.1 %collective-permute-start.17 = (f32[8,128]{1,0:T(8,128)}, f32[8,128]{1,0:T(8,128)S(1)}, u32[]{:S(2)}, u32[]{:S(2)}) collective-permute-start(f32[8,128]{1,0:T(8,128)} %shard_map.70.gate), channel_id=1, source_target_pairs={{0,16},{8,24},{16,0},{24,8},{1,17},{9,25},{17,1},{25,9},{2,18},{10... | collective-permute-start | bytes 12296 | tf_op jit(solution)/shard_map/ppermute | solution.py:470
  142.5 13.8 %shard_map.71 = f32[3,8,32,1024]{3,2,1,0:T(8,128)} custom-call(f32[4]{0:T(128)} %add_convert_fusion.flags, f32[8,8,32,128]{3,2,1,0:T(8,128)} %get-tuple-element.32.field.own, f32[8,3,40,128]{3,2,1,0:T(8,128)} %copy-done.1, f32[8,3,40,128]{3,2,1,0:T(8,128)} %copy-done.2, f32[8,8,4,128]{3,2,1,0:T(4,128)} %copy-done.5, f32[8,8,4,128]{3,2,1,0:T(4,128)} %copy-done.6, ...), custom_call_target="tpu_custom_call" | custom-call | flops 20971520 | bytes 4194304 | tf_op jit(solution)/shard_map/pallas_call | solution.py:565
  156.4 0.6 add_reduce_fusion
  (37 shorter events, 0.2 us)
Async XLA Ops:
  8.5 15.1 %copy-start.7 = (f32[80,1024]{1,0:T(8,128)S(1)}, f32[80,1024]{1,0:T(8,128)}, u32[]{:S(2)}) copy-start(f32[80,1024]{1,0:T(8,128)} %get-tuple-element.21.gate) | copy-start | bytes 983044
  8.5 40.3 %all-to-all-start = ((f32[8,8,40,128]{3,2,1,0:T(8,128)}), f32[8,8,40,128]{3,2,1,0:T(8,128)}, u32[]{:S(2)}, u32[]{:S(2)}) async-start(f32[8,8,40,128]{3,2,1,0:T(8,128)} %shard_map.60.gate), calls=%async_computation | async-start | bytes 2621440 | tf_op jit(solution)/shard_map/all_to_all | solution.py:460
  15.9 31.2 %collective-permute-start = (f32[10,32,1024]{2,1,0:T(8,128)}, f32[10,32,1024]{2,1,0:T(8,128)}, u32[]{:S(2)}, u32[]{:S(2)}) collective-permute-start(f32[10,32,1024]{2,1,0:T(8,128)} %get-tuple-element.22), channel_id=1, source_target_pairs={{0,8},{8,16},{16,24},{1,9},{9,17},{17,25},{2,10},{10,18},{18,26},{... | collective-permute-start | bytes 3932168 | tf_op jit(solution)/shard_map/ppermute | solution.py:30
  18.5 28.6 %collective-permute-start.1 = (f32[10,32,1024]{2,1,0:T(8,128)}, f32[10,32,1024]{2,1,0:T(8,128)}, u32[]{:S(2)}, u32[]{:S(2)}) collective-permute-start(f32[10,32,1024]{2,1,0:T(8,128)} %get-tuple-element.23), channel_id=1, source_target_pairs={{8,0},{16,8},{24,16},{9,1},{17,9},{25,17},{10,2},{18,10},{26,18},{... | collective-permute-start | bytes 3932168 | tf_op jit(solution)/shard_map/ppermute | solution.py:31
  19.8 23.8 %collective-permute-start.2 = (f32[80,1024]{1,0:T(8,128)}, f32[80,1024]{1,0:T(8,128)S(1)}, u32[]{:S(2)}, u32[]{:S(2)}) collective-permute-start(f32[80,1024]{1,0:T(8,128)} %get-tuple-element.24), channel_id=1, source_target_pairs={{0,1},{1,2},{2,3},{3,4},{4,5},{5,6},{6,7},{8,9},{9,10},{10,11},{11... | collective-permute-start | bytes 983048 | tf_op jit(solution)/shard_map/ppermute | solution.py:30
  23.6 20.0 %collective-permute-start.3 = (f32[80,1024]{1,0:T(8,128)S(1)}, f32[80,1024]{1,0:T(8,128)S(1)}, u32[]{:S(2)}, u32[]{:S(2)}) collective-permute-start(f32[80,1024]{1,0:T(8,128)S(1)} %copy-done.7), channel_id=1, source_target_pairs={{1,0},{2,1},{3,2},{4,3},{5,4},{6,5},{7,6},{9,8},{10,9},{11,10},{12... | collective-permute-start | bytes 983048 | tf_op jit(solution)/shard_map/ppermute | solution.py:31
  43.7 0.7 copy-start.3
  44.4 0.7 copy-start.4
  51.3 14.8 %copy-start.12 = (f32[54,1024]{1,0:T(8,128)S(1)}, f32[54,1024]{1,0:T(8,128)}, u32[]{:S(2)}) copy-start(f32[54,1024]{1,0:T(8,128)} %get-tuple-element.28) | copy-start | bytes 663556
  51.3 19.2 %copy-start.8 = (f32[54,1024]{1,0:T(8,128)S(1)}, f32[54,1024]{1,0:T(8,128)}, u32[]{:S(2)}) copy-start(f32[54,1024]{1,0:T(8,128)} %get-tuple-element.25.gate_corners) | copy-start | bytes 663556
  51.3 47.1 %all-to-all-start.1 = ((f32[8,8,32,128]{3,2,1,0:T(8,128)}), f32[8,8,32,128]{3,2,1,0:T(8,128)}, u32[]{:S(2)}, u32[]{:S(2)}) async-start(f32[8,8,32,128]{3,2,1,0:T(8,128)} %shard_map.66), calls=%async_computation.1 | async-start | bytes 2097152 | tf_op jit(solution)/shard_map/all_to_all | solution.py:460
  63.1 21.1 %collective-permute-start.4 = (f32[8,4,40,128]{3,2,1,0:T(8,128)}, f32[8,4,40,128]{3,2,1,0:T(8,128)S(1)}, u32[]{:S(2)}, u32[]{:S(2)}) collective-permute-start(f32[8,4,40,128]{3,2,1,0:T(8,128)} %get-tuple-element.26), channel_id=1, source_target_pairs={{0,8},{8,16},{16,24},{1,9},{9,17},{17,25},{2,10},{10,18},{18,26},{... | collective-permute-start | bytes 1966088 | tf_op jit(solution)/shard_map/ppermute | solution.py:30
  64.8 19.4 %collective-permute-start.5 = (f32[8,4,40,128]{3,2,1,0:T(8,128)}, f32[8,4,40,128]{3,2,1,0:T(8,128)}, u32[]{:S(2)}, u32[]{:S(2)}) collective-permute-start(f32[8,4,40,128]{3,2,1,0:T(8,128)} %get-tuple-element.27.refs_1_), channel_id=1, source_target_pairs={{8,0},{16,8},{24,16},{9,1},{17,9},{25,17},{10,2},{18,10},{26,18},{... | collective-permute-start | bytes 1966088 | tf_op jit(solution)/shard_map/ppermute | solution.py:31
  66.1 6.4 %collective-permute-start.6 = (f32[54,1024]{1,0:T(8,128)S(1)}, f32[54,1024]{1,0:T(8,128)S(1)}, u32[]{:S(2)}, u32[]{:S(2)}) collective-permute-start(f32[54,1024]{1,0:T(8,128)S(1)} %copy-done.12), channel_id=1, source_target_pairs={{0,8},{8,16},{16,24},{1,9},{9,17},{17,25},{2,10},{10,18},{18,26},{... | collective-permute-start | bytes 663560 | tf_op jit(solution)/shard_map/ppermute | solution.py:30
  70.5 4.7 %collective-permute-start.7 = (f32[54,1024]{1,0:T(8,128)S(1)}, f32[54,1024]{1,0:T(8,128)}, u32[]{:S(2)}, u32[]{:S(2)}) collective-permute-start(f32[54,1024]{1,0:T(8,128)S(1)} %copy-done.8), channel_id=1, source_target_pairs={{8,0},{16,8},{24,16},{9,1},{17,9},{25,17},{10,2},{18,10},{26,18},{... | collective-permute-start | bytes 663560 | tf_op jit(solution)/shard_map/ppermute | solution.py:31
  72.5 2.8 %copy-start.9 = (f32[54,1024]{1,0:T(8,128)}, f32[54,1024]{1,0:T(8,128)S(1)}, u32[]{:S(2)}) copy-start(f32[54,1024]{1,0:T(8,128)S(1)} %collective-permute-done.6.corners_below) | copy-start | bytes 663556
  84.2 0.8 copy-start
  101.4 22.0 %copy-start.11 = (f32[8,128]{1,0:T(8,128)S(1)}, f32[8,128]{1,0:T(8,128)}, u32[]{:S(2)}) copy-start(f32[8,128]{1,0:T(8,128)} %get-tuple-element.39) | copy-start | bytes 12292
  101.4 6.9 %collective-permute-start.8 = (f32[8,8,4,128]{3,2,1,0:T(4,128)}, f32[8,8,4,128]{3,2,1,0:T(4,128)S(1)}, u32[]{:S(2)}, u32[]{:S(2)}) collective-permute-start(f32[8,8,4,128]{3,2,1,0:T(4,128)} %get-tuple-element.33), channel_id=1, source_target_pairs={{0,1},{1,2},{2,3},{3,4},{4,5},{5,6},{6,7},{8,9},{9,10},{10,11},{11... | collective-permute-start | bytes 393224 | tf_op jit(solution)/shard_map/ppermute | solution.py:30
  105.4 7.1 %collective-permute-start.9 = (f32[8,8,4,128]{3,2,1,0:T(4,128)}, f32[8,8,4,128]{3,2,1,0:T(4,128)S(1)}, u32[]{:S(2)}, u32[]{:S(2)}) collective-permute-start(f32[8,8,4,128]{3,2,1,0:T(4,128)} %get-tuple-element.34), channel_id=1, source_target_pairs={{1,0},{2,1},{3,2},{4,3},{5,4},{6,5},{7,6},{9,8},{10,9},{11,10},{12... | collective-permute-start | bytes 393224 | tf_op jit(solution)/shard_map/ppermute | solution.py:31
  108.2 4.3 %copy-start.5 = (f32[8,8,4,128]{3,2,1,0:T(4,128)}, f32[8,8,4,128]{3,2,1,0:T(4,128)S(1)}, u32[]{:S(2)}) copy-start(f32[8,8,4,128]{3,2,1,0:T(4,128)S(1)} %collective-permute-done.8.before) | copy-start | bytes 393220
  112.5 0.7 copy-start.6
  115.5 22.2 %collective-permute-start.10 = (f32[8,3,40,128]{3,2,1,0:T(8,128)}, f32[8,3,40,128]{3,2,1,0:T(8,128)S(1)}, u32[]{:S(2)}, u32[]{:S(2)}) collective-permute-start(f32[8,3,40,128]{3,2,1,0:T(8,128)} %get-tuple-element.35), channel_id=1, source_target_pairs={{0,8},{8,16},{16,24},{1,9},{9,17},{17,25},{2,10},{10,18},{18,26},{... | collective-permute-start | bytes 1474568 | tf_op jit(solution)/shard_map/ppermute | solution.py:30
  122.1 15.7 %collective-permute-start.11 = (f32[8,3,40,128]{3,2,1,0:T(8,128)}, f32[8,3,40,128]{3,2,1,0:T(8,128)S(1)}, u32[]{:S(2)}, u32[]{:S(2)}) collective-permute-start(f32[8,3,40,128]{3,2,1,0:T(8,128)} %get-tuple-element.36.refs_1_), channel_id=1, source_target_pairs={{8,0},{16,8},{24,16},{9,1},{17,9},{25,17},{10,2},{18,10},{26,18},{... | collective-permute-start | bytes 1474568 | tf_op jit(solution)/shard_map/ppermute | solution.py:31
  123.4 5.2 %collective-permute-start.14 = (f32[8,128]{1,0:T(8,128)S(1)}, f32[8,128]{1,0:T(8,128)S(1)}, u32[]{:S(2)}, u32[]{:S(2)}) collective-permute-start(f32[8,128]{1,0:T(8,128)S(1)} %copy-done.11), channel_id=1, source_target_pairs={{0,3},{1,2},{2,1},{3,0},{4,7},{5,6},{6,5},{7,4},{8,11},{9,10},{10,... | collective-permute-start | bytes 12296 | tf_op jit(solution)/shard_map/ppermute | solution.py:470
  127.0 3.6 %collective-permute-start.13 = (f32[8,128]{1,0:T(8,128)S(1)}, f32[8,128]{1,0:T(8,128)S(1)}, u32[]{:S(2)}, u32[]{:S(2)}) collective-permute-start(f32[8,128]{1,0:T(8,128)S(1)} %copy-done.11), channel_id=1, source_target_pairs={{0,2},{1,3},{2,0},{3,1},{4,6},{5,7},{6,4},{7,5},{8,10},{9,11},{10,... | collective-permute-start | bytes 12296 | tf_op jit(solution)/shard_map/ppermute | solution.py:470
  127.5 3.6 %collective-permute-start.12 = (f32[8,128]{1,0:T(8,128)S(1)}, f32[8,128]{1,0:T(8,128)S(1)}, u32[]{:S(2)}, u32[]{:S(2)}) collective-permute-start(f32[8,128]{1,0:T(8,128)S(1)} %copy-done.11), channel_id=1, source_target_pairs={{0,1},{1,0},{2,3},{3,2},{4,5},{5,4},{6,7},{7,6},{8,9},{9,8},{10,11... | collective-permute-start | bytes 12296 | tf_op jit(solution)/shard_map/ppermute | solution.py:470
  131.7 4.7 %collective-permute-start.15 = (f32[8,128]{1,0:T(8,128)}, f32[8,128]{1,0:T(8,128)S(1)}, u32[]{:S(2)}, u32[]{:S(2)}) collective-permute-start(f32[8,128]{1,0:T(8,128)} %shard_map.69), channel_id=1, source_target_pairs={{0,4},{1,5},{2,6},{3,7},{4,0},{5,1},{6,2},{7,3},{8,12},{9,13},{10,... | collective-permute-start | bytes 12296 | tf_op jit(solution)/shard_map/ppermute | solution.py:470
  137.7 0.8 copy-start.1
  138.5 0.8 copy-start.2
  139.3 17.0 %collective-permute-start.18 = (f32[8,128]{1,0:T(8,128)}, f32[8,128]{1,0:T(8,128)S(1)}, u32[]{:S(2)}, u32[]{:S(2)}) collective-permute-start(f32[8,128]{1,0:T(8,128)} %shard_map.70.gate), channel_id=1, source_target_pairs={{0,24},{8,16},{16,8},{24,0},{1,25},{9,17},{17,9},{25,1},{2,26},{10... | collective-permute-start | bytes 12296 | tf_op jit(solution)/shard_map/ppermute | solution.py:470
  139.3 17.0 %collective-permute-start.17 = (f32[8,128]{1,0:T(8,128)}, f32[8,128]{1,0:T(8,128)S(1)}, u32[]{:S(2)}, u32[]{:S(2)}) collective-permute-start(f32[8,128]{1,0:T(8,128)} %shard_map.70.gate), channel_id=1, source_target_pairs={{0,16},{8,24},{16,0},{24,8},{1,17},{9,25},{17,1},{25,9},{2,18},{10... | collective-permute-start | bytes 12296 | tf_op jit(solution)/shard_map/ppermute | solution.py:470
  142.4 13.9 %collective-permute-start.16 = (f32[8,128]{1,0:T(8,128)}, f32[8,128]{1,0:T(8,128)S(1)}, u32[]{:S(2)}, u32[]{:S(2)}) collective-permute-start(f32[8,128]{1,0:T(8,128)} %shard_map.70.gate), channel_id=1, source_target_pairs={{0,8},{8,0},{16,24},{24,16},{1,9},{9,1},{17,25},{25,17},{2,10},{10... | collective-permute-start | bytes 12296 | tf_op jit(solution)/shard_map/ppermute | solution.py:470
  142.5 13.8 %copy-start.10 = (f32[8,128]{1,0:T(8,128)S(1)}, f32[8,128]{1,0:T(8,128)}, u32[]{:S(2)}) copy-start(f32[8,128]{1,0:T(8,128)} %shard_map.70.gate) | copy-start | bytes 12292
